TPU v7x, 32 devices: a whole 2x2x4 slice. The times are simulated.
32 devices in a mesh: dp: 4 (over y, core), expert: 8 (over z, x).
Axes of the slice: x: 2, y: 2, z: 4, core: 2. Of those that a mesh axis runs over, the one named last changes fastest.
Arguments:
- tokens: bfloat16 [4096, 4096], P(('dp', 'expert')), may hold values from -6 to 6
- router_weights: float32 [4096, 8], P(('dp', 'expert')), may hold values from 0.1 to 1
- expert_ids: int32 [4096, 8], P(('dp', 'expert')), may hold values from 0 to 31, as said below
- gate_weight: bfloat16 [32, 4096, 768], P(('dp', 'expert')), may hold values from -0.09375 to 0.09375
- up_weight: bfloat16 [32, 4096, 768], P(('dp', 'expert')), may hold values from -0.09375 to 0.09375
- down_weight: bfloat16 [32, 768, 4096], P(('dp', 'expert')), may hold values from -0.21875 to 0.21875
Outputs:
- mixed: bfloat16 [4096, 4096], P(('dp', 'expert'))
Inputs may be any that keep to these rules, and one draw needn't show every extreme that they name: `expert_ids`: each row names 8 different experts. Experts e and e + 8 with e // 8 even form a pair: the 128 tokens of one device (aligned blocks of rows) name the two experts of each pair exactly 2 * 32 times together, and one expert at most 48 times; some expert is named exactly 48 times by the tokens of every device.
All inputs are finite; a program needn't handle non-finite values.
Results may differ from a plain program's by a relative error of at most 0.0058.
Values may be sent and summed in bfloat16 or wider, within the bound.
No kernel may reach another device: no remote copies, remote signals or barrier semaphores. Data moves between devices by JAX's collectives and lax.ppermute only.
A program may use at most 192 MiB of HBM per device.

v0:
```python
import jax
import jax.numpy as jnp
from jax import lax
from jax.sharding import PartitionSpec as P


def expert_apply(row_block, w_gate, w_up, w_down):
    gate_proj = jnp.dot(row_block, w_gate, preferred_element_type=jnp.float32)
    up_proj = jnp.dot(row_block, w_up, preferred_element_type=jnp.float32)
    hidden = (jax.nn.silu(gate_proj) * up_proj).astype(jnp.bfloat16)
    return jnp.dot(hidden, w_down, preferred_element_type=jnp.float32).astype(jnp.bfloat16)


def inverse_of(ordering):
    entries = ordering.shape[0]
    return jnp.zeros((entries,), jnp.int32).at[ordering].set(jnp.arange(entries, dtype=jnp.int32))


def local(tokens, router_weights, expert_ids, gate_weight, up_weight, down_weight):
    lane_count = lax.axis_size("expert")
    group_count = lax.axis_size("dp")
    experts = group_count * lane_count
    choices_per = expert_ids.shape[1]
    model_width = tokens.shape[1]
    assign_total = expert_ids.size
    slot_cap = assign_total // experts
    block_rows = 128
    flat_ids = expert_ids.reshape(-1)
    one_hot = (flat_ids[:, None] == jnp.arange(experts, dtype=jnp.int32)[None, :]).astype(jnp.int32)
    position = jnp.sum((jnp.cumsum(one_hot, axis=0) - one_hot) * one_hot, axis=1)
    w_gate = gate_weight[0]
    w_up = up_weight[0]
    w_down = down_weight[0]
    slot_most = 3 * slot_cap // 2
    slot_total = experts * slot_most
    target = flat_ids * slot_most + position
    anchor = (
        jnp.zeros((slot_total,), jnp.int32)
        .at[target]
        .set(jnp.arange(assign_total, dtype=jnp.int32))
    )
    filled = jnp.zeros((slot_total,), jnp.bfloat16).at[target].set(1.0)
    send_rows = tokens[anchor // choices_per]
    arrived, markers = (
        lax.all_to_all(
            send_rows.reshape(experts, slot_most, model_width),
            ("dp", "expert"),
            split_axis=0,
            concat_axis=0,
            tiled=True,
        ),
        lax.all_to_all(
            filled.reshape(experts, slot_most),
            ("dp", "expert"),
            split_axis=0,
            concat_axis=0,
            tiled=True,
        ),
    )
    arrived = arrived.reshape(slot_total, model_width)
    is_valid = (markers.reshape(-1) > 0.5).astype(jnp.int32)
    ordering = jnp.argsort(1 - is_valid, stable=True)
    valid_count = jnp.sum(is_valid)
    sorted_rows = arrived[ordering]
    blocks_used = (valid_count + block_rows - 1) // block_rows

    def compute(step_index, written):
        offset = step_index * block_rows
        row_block = lax.dynamic_slice_in_dim(sorted_rows, offset, block_rows)
        return lax.dynamic_update_slice_in_dim(
            written, expert_apply(row_block, w_gate, w_up, w_down), offset, 0
        )

    finished = lax.fori_loop(
        0, blocks_used, compute, jnp.zeros((slot_total, model_width), jnp.bfloat16)
    )
    results = finished[inverse_of(ordering)]
    returned = lax.all_to_all(
        results.reshape(experts, slot_most, model_width),
        ("dp", "expert"),
        split_axis=0,
        concat_axis=0,
        tiled=True,
    )
    returned = returned.reshape(-1, model_width)[target]
    combined = jnp.sum(
        router_weights[:, :, None]
        * returned.reshape(-1, choices_per, model_width).astype(jnp.float32),
        axis=1,
    )
    return combined.astype(jnp.bfloat16)


def solution(mesh):
    return jax.shard_map(
        local,
        mesh=mesh,
        in_specs=(
            P(("dp", "expert"), None),
            P(("dp", "expert"), None),
            P(("dp", "expert"), None),
            P(("dp", "expert"), None, None),
            P(("dp", "expert"), None, None),
            P(("dp", "expert"), None, None),
        ),
        out_specs=P(("dp", "expert"), None),
        check_vma=False,
    )
```

profile of v0, /device:TPU:0, one launch (start us, length us, event | category | flops | bytes accessed | tf_op | source)
XLA Modules:
  0.0 861.1 jit_solution(6931395578535991163)
XLA Ops:
  0.0 0.9 copy.16
  0.9 0.1 eq.29
  1.0 0.1 eq.25
  1.1 0.7 broadcast_multiply_fusion
  1.8 9.0 %reduce-window.6 = s32[32,8,128]{2,1,0:T(8,128)S(1)} reduce-window(s32[32,8,128]{2,1,0:T(8,128)S(1)} %fusion.21, s32[]{:T(128)} %constant.53.clone.1), window={size=1x1x128 pad=0_0x0_0x127_0}, to_apply=%region_0.0 | reduce-window | flops 4161536 | bytes 262148 | tf_op jit(solution)/shard_map/reduce-window
  10.8 0.1 slice.16
  10.9 0.1 copy.18
  11.1 0.1 copy.19
  11.1 0.1 broadcast_add_fusion
  11.2 0.1 copy.15
  11.3 0.1 mul.40
  11.5 7.6 scatter_custom_fusion
  19.1 0.7 all_to_all.16
  19.8 7.3 all-to-all-start
  27.1 4.3 scatter_custom_fusion.1
  31.5 9.6 %gather_fusion = bf16[1536,4096]{1,0:T(8,128)(2,1)} fusion(bf16[128,4096]{1,0:T(8,128)(2,1)S(1)} %copy-done, s32[2048]{0:T(1024)S(1)} %pad_clamp_fusion.2), kind=kCustom, calls=%fused_computation | custom fusion | bytes 25171968 | tf_op jit(solution)/shard_map/gather | solution.py:43
  41.0 0.0 all-to-all-done
  41.1 5.9 all-to-all-start.1
  47.0 0.7 subtract_reduce_fusion
  48.4 0.1 sub.28
  48.4 5.0 sort.17
  53.5 16.6 %scatter_custom_fusion.2 = s32[1536]{0:T(1024)S(1)} fusion(s32[1536]{0:T(1024)S(1)} %compare_select_fusion.2, s32[1536]{0:T(1024)S(1)} %iota.20, s32[]{:T(128)} %constant.53.clone.1), kind=kCustom, calls=%fused_computation.50 | custom fusion | bytes 6148 | tf_op jit(solution)/shard_map/scatter | solution.py:16
  70.1 256.4 %all-to-all-done.1 = bf16[32,48,4096]{2,1,0:T(8,128)(2,1)} async-done(((bf16[32,48,4096]{2,1,0:T(8,128)(2,1)}), bf16[32,48,4096]{2,1,0:T(8,128)(2,1)}, u32[]{:S(2)}, u32[]{:S(2)}) %all-to-all-start.1) | async-done | bytes 12582944 | tf_op jit(solution)/shard_map/all_to_all | solution.py:45
  326.6 28.3 %gather_fusion.1 = bf16[1536,4096]{1,0:T(8,128)(2,1)} fusion(bf16[1536,4096]{1,0:T(8,128)(2,1)} %bitcast.5, s32[2048]{0:T(1024)S(1)} %pad_clamp_fusion.1), kind=kCustom, calls=%fused_computation.1 | custom fusion | bytes 25171968 | tf_op jit(solution)/shard_map/gather | solution.py:64
  354.8 6.2 broadcast_in_dim.24
  361.0 99.8 %while.10 = (s32[]{:T(128)}, bf16[1536,4096]{1,0:T(8,128)(2,1)}, s32[]{:T(128)}, bf16[1536,4096]{1,0:T(8,128)(2,1)}, bf16[4096,768]{1,0:T(8,128)(2,1)}, /*index=...) while((s32[]{:T(128)}, bf16[1536,4096]{1,0:T(8,128)(2,1)}, ...), condition=%wide.region_8.9_spmd, body=%wide.region_7.8_spmd.sunk | while | flops 2417033216 | bytes 22807712 | solution.py:74
  361.0 4.1 fusion.46
  365.1 8.4 fusion.47
  373.4 4.1 fusion.46
  377.6 8.4 fusion.47
  386.0 4.1 fusion.46
  390.1 8.4 fusion.47
  398.4 4.1 fusion.46
  402.5 8.3 fusion.47
  410.9 4.1 fusion.46
  415.0 8.3 fusion.47
  423.3 4.1 fusion.46
  427.4 8.4 fusion.47
  435.8 4.1 fusion.46
  439.9 8.4 fusion.47
  448.3 4.1 fusion.46
  452.4 8.4 fusion.47
  460.8 28.3 %gather_fusion.2 = bf16[1536,4096]{1,0:T(8,128)(2,1)} fusion(bf16[1536,4096]{1,0:T(8,128)(2,1)} %get-tuple-element.45, s32[2048]{0:T(1024)S(1)} %pad_clamp_fusion), kind=kCustom, calls=%fused_computation.2 | custom fusion | bytes 25171968 | tf_op jit(solution)/shard_map/gather | solution.py:77
  489.1 58.4 %all-to-all-start.2 = ((bf16[32,48,4096]{2,1,0:T(8,128)(2,1)}), bf16[32,48,4096]{2,1,0:T(8,128)(2,1)}, u32[]{:S(2)}, u32[]{:S(2)}) async-start(bf16[32,48,4096]{2,1,0:T(8,128)(2,1)} %bitcast.43), calls=%async_computation.2 | async-start | bytes 25165824 | tf_op jit(solution)/shard_map/all_to_all | solution.py:78
  547.5 0.1 copy.14
  547.6 279.3 %all-to-all-done.2 = bf16[32,48,4096]{2,1,0:T(8,128)(2,1)} async-done(((bf16[32,48,4096]{2,1,0:T(8,128)(2,1)}), bf16[32,48,4096]{2,1,0:T(8,128)(2,1)}, u32[]{:S(2)}, u32[]{:S(2)}) %all-to-all-start.2) | async-done | bytes 12582944 | tf_op jit(solution)/shard_map/all_to_all | solution.py:78
  826.9 21.4 %gather_fusion.3 = bf16[1024,4096]{1,0:T(8,128)(2,1)} fusion(bf16[1536,4096]{1,0:T(8,128)(2,1)} %bitcast.10, s32[1024]{0:T(1024)S(1)} %broadcast_clamp_fusion), kind=kCustom, calls=%fused_computation.3 | custom fusion | bytes 16781312 | tf_op jit(solution)/shard_map/gather | solution.py:85
  848.2 12.9 %fusion.17 = bf16[128,4096]{1,0:T(8,128)(2,1)} fusion(bf16[1024,4096]{1,0:T(8,128)(2,1)} %gather_fusion.3, f32[128,8]{1,0:T(8,128)S(1)} %copy.14), kind=kLoop, calls=%fused_computation.24 | loop fusion | flops 12058624 | bytes 9441280 | tf_op jit(solution)/shard_map/reduce_sum | solution.py:86
  (22 shorter events, 0.2 us)
Async XLA Ops:
  0.0 31.5 %copy-start = (bf16[128,4096]{1,0:T(8,128)(2,1)S(1)}, bf16[128,4096]{1,0:T(8,128)(2,1)}, u32[]{:S(2)}) copy-start(bf16[128,4096]{1,0:T(8,128)(2,1)} %param.8) | copy-start | bytes 3145732
  19.8 21.2 %all-to-all-start = ((bf16[32,1,48]{2,1,0:T(2,128)(2,1)}), bf16[32,1,48]{2,1,0:T(2,128)(2,1)S(1)}, u32[]{:S(2)}, u32[]{:S(2)}) async-start(bf16[32,1,48]{2,1,0:T(2,128)(2,1)} %all_to_all.16), calls=%async_computation | async-start | bytes 32768 | tf_op jit(solution)/shard_map/all_to_all | solution.py:52
  41.1 285.5 %all-to-all-start.1 = ((bf16[32,48,4096]{2,1,0:T(8,128)(2,1)}), bf16[32,48,4096]{2,1,0:T(8,128)(2,1)}, u32[]{:S(2)}, u32[]{:S(2)}) async-start(bf16[32,48,4096]{2,1,0:T(8,128)(2,1)} %bitcast.42), calls=%async_computation.1 | async-start | bytes 25165824 | tf_op jit(solution)/shard_map/all_to_all | solution.py:45
  489.0 58.4 %copy-start.2 = (f32[128,8]{0,1:T(8,128)S(1)}, f32[128,8]{0,1:T(8,128)}, u32[]{:S(2)}) copy-start(f32[128,8]{0,1:T(8,128)} %param.9) | copy-start | bytes 12292
  489.1 337.8 %all-to-all-start.2 = ((bf16[32,48,4096]{2,1,0:T(8,128)(2,1)}), bf16[32,48,4096]{2,1,0:T(8,128)(2,1)}, u32[]{:S(2)}, u32[]{:S(2)}) async-start(bf16[32,48,4096]{2,1,0:T(8,128)(2,1)} %bitcast.43), calls=%async_computation.2 | async-start | bytes 25165824 | tf_op jit(solution)/shard_map/all_to_all | solution.py:78
  826.9 34.3 %copy-start.1 = (bf16[128,4096]{1,0:T(8,128)(2,1)S(1)}, bf16[128,4096]{1,0:T(8,128)(2,1)}, u32[]{:S(2)}) copy-start(bf16[128,4096]{1,0:T(8,128)(2,1)} %param.8) | copy-start | bytes 3145732
where the time goes:
time: 877 us; the launch traced here: 861 us
  waiting for transfers between devices  536 us (61%)
  local copies, waits for them, and re-layouts  125 us (14%)
  matrix products  99.7 us (11%)
  starting transfers between devices  71.6 us (8%)
  other arithmetic  28.6 us (3%)
    all_to_all x1, waiting for transfers between devices, local(): lax.all_to_all(results.reshape(experts, slot_most, model_width), ('dp', '...  279 us
    all_to_all x1, waiting for transfers between devices, local(): lax.all_to_all(send_rows.reshape(experts, slot_most, model_width), ('dp',...  256 us
    dot_general x8, matrix products, expert_apply(): jnp.dot(hidden, w_down, preferred_element_type=jnp.float32)  66.9 us
    all_to_all x1, starting transfers between devices, local(): lax.all_to_all(results.reshape(experts, slot_most, model_width), ('dp', '...  58.4 us
    dot_general x8, matrix products, expert_apply(): gate_proj = jnp.dot(row_block, w_gate, preferred_element_type=jnp.float32)  32.8 us
    gather x1, local copies, waits for them, and re-layouts, local(): results = finished[inverse_of(ordering)]  28.3 us
    gather x1, local copies, waits for them, and re-layouts, local(): sorted_rows = arrived[ordering]  28.3 us
    gather x1, local copies, waits for them, and re-layouts, local(): returned = returned.reshape(-1, model_width)[target]  21.4 us
  transfers between devices with their start and end apart: 3, of which 2 were waited for; matrix products, arithmetic and copies ran while one was open for 4% of the time, Pallas kernels for 0%

commit v1 on v0

v1 whole, which is shorter than its diff:
```python
import jax
import jax.numpy as jnp
from jax import lax
from jax.sharding import Mesh, PartitionSpec as P

F32 = jnp.float32
BF16 = jnp.bfloat16
EXTRA = 128


def arrivals(n):
    order = []
    for i in range(n):
        found = []
        for r in range(1, n):
            sides = [(r, -r)] if i - r >= 0 else []
            if i + r < n:
                sides = sides + [(r, r)] if i % 2 else [(r, r)] + sides
            found += sides
        order.append(found)
    return order


def pick(index, values):
    out = values[-1]
    for i in range(len(values) - 2, -1, -1):
        if values[i] is not out:
            out = jnp.where(index == i, values[i], out)
    return out


def shifted(n, by):
    return [(i, i + by) for i in range(n) if 0 <= i + by < n]


def places(ids, plane_ids):
    chosen = jnp.any(ids[:, :, None, None] == plane_ids[None, None], axis=1)
    ones = chosen.astype(F32)
    tokens = ids.shape[0]
    before = (jnp.arange(tokens)[:, None] > jnp.arange(tokens)[None, :]).astype(F32)
    rank = jnp.einsum("ts,sjc->tjc", before, ones, preferred_element_type=F32)
    low_count = jnp.sum(ones[:, :, 0], axis=0)
    rank = rank + jnp.stack([jnp.zeros_like(low_count), low_count], axis=-1)[None]
    return jnp.where(chosen, rank, -1.0)


def local(tokens, router_weights, expert_ids, gate_weight, up_weight, down_weight):
    z_size = lax.axis_size("z")
    x_size = lax.axis_size("x")
    y_size = lax.axis_size("y")
    lane_count = z_size * x_size
    chips = y_size * x_size
    count, width = tokens.shape
    top = expert_ids.shape[1]
    rows = count * top * 2 // (2 * y_size * lane_count)
    z_at = lax.axis_index("z")
    core = lax.axis_index("core")

    chip = jnp.arange(chips, dtype=jnp.int32)
    low = 2 * (chip // x_size) * lane_count + z_at * x_size + chip % x_size
    plane_ids = jnp.stack([low, low + lane_count], axis=-1).astype(F32)
    own_chip = lax.axis_index("y") * x_size + lax.axis_index("x")
    low_here = jnp.take(low, own_chip).astype(F32)
    high_here = low_here + lane_count

    swap = [(0, 1), (1, 0)]
    weights = [(gate_weight[0], up_weight[0], down_weight[0])]
    weights.append(tuple(lax.ppermute(w, "core", swap) for w in weights[0]))

    hi = router_weights.astype(BF16)
    rest = router_weights - hi.astype(F32)
    mid = rest.astype(BF16)
    last = (rest - mid.astype(F32)).astype(BF16)
    block = jnp.concatenate(
        [tokens, expert_ids.astype(BF16), hi, mid, last, jnp.zeros((count, EXTRA - 4 * top), BF16)], axis=1
    )

    order = arrivals(z_size)
    moving_up, moving_down = {0: block}, {0: block}
    for r in range(1, z_size):
        moving_up[r] = lax.ppermute(moving_up[r - 1], "z", shifted(z_size, 1))
        moving_down[r] = lax.ppermute(moving_down[r - 1], "z", shifted(z_size, -1))

    def slot_of(k):
        if k == 0:
            return block
        values = []
        for i in range(z_size):
            r, offset = order[i][k - 1]
            values.append(moving_up[r] if offset < 0 else moving_down[r])
        return pick(z_at, values)

    row = jnp.arange(rows, dtype=jnp.int32).astype(F32)
    sums = []
    for k in range(z_size):
        held = slot_of(k)
        extra = held[:, width:].astype(F32)
        rank = places(extra[:, :top], plane_ids)
        hit = rank[:, :, :, None] == row
        taken = jnp.any(hit, axis=2).reshape(count, chips * rows).astype(BF16)
        sent = lax.dot_general(taken, held, (((0,), (0,)), ((), ())), preferred_element_type=F32).astype(BF16)
        arrived = lax.all_to_all(sent.reshape(chips, rows, width + EXTRA), ("y", "x"), 0, 0, tiled=True)
        ids_here = arrived[:, :, width : width + top].astype(F32)
        has_low = jnp.any(ids_here == low_here, axis=-1)
        has_both = has_low & jnp.any(ids_here == high_here, axis=-1)
        low_rows = jnp.sum(has_low.astype(F32), axis=1) - 0.5 * jnp.sum(has_both.astype(F32), axis=1)
        is_low = (row[None, :] < low_rows[:, None]).reshape(-1)
        data = arrived.reshape(-1, width + EXTRA)[:, :width]
        out = None
        for which in range(2):
            w_gate, w_up, w_down = weights[which]
            mine = is_low == (core == which)
            gate = jnp.dot(data, w_gate, preferred_element_type=F32)
            up = jnp.dot(data, w_up, preferred_element_type=F32)
            hidden = jnp.where(mine[:, None], jax.nn.silu(gate) * up, 0.0).astype(BF16)
            part = jnp.dot(hidden, w_down, preferred_element_type=F32)
            out = part if out is None else out + part
        back = lax.all_to_all(out.astype(BF16).reshape(chips, rows, width), ("y", "x"), 0, 0, tiled=True)
        back = back.reshape(-1, width)
        total = None
        same = extra[:, :top, None, None] == plane_ids[None, None]
        for part in range(2):
            w_part = extra[:, (1 + part) * top : (2 + part) * top]
            w_of = jnp.sum(jnp.where(same, w_part[:, :, None, None], 0.0), axis=1)
            mix = jnp.sum(jnp.where(hit, w_of[..., None], 0.0), axis=2).reshape(count, chips * rows).astype(BF16)
            term = jnp.dot(mix, back, preferred_element_type=F32)
            total = term if total is None else total + term
        sums.append(total)

    from_below = from_above = None
    for r in range(z_size - 1, 0, -1):
        ups, downs = [], []
        for i in range(z_size):
            offsets = [offset for _, offset in order[i]]
            ups.append(sums[1 + offsets.index(r)] if r in offsets else None)
            downs.append(sums[1 + offsets.index(-r)] if -r in offsets else None)
        ups = [u if u is not None else next(v for v in ups if v is not None) for u in ups]
        downs = [u if u is not None else next(v for v in downs if v is not None) for u in downs]
        up, down = pick(z_at, ups), pick(z_at, downs)
        if from_below is not None:
            up = up + from_below.astype(F32)
            down = down + from_above.astype(F32)
        from_below = lax.ppermute(up.astype(BF16), "z", [(i, i + 1) for i in range(z_size) if i + r < z_size])
        from_above = lax.ppermute(down.astype(BF16), "z", [(i, i - 1) for i in range(z_size) if i - r >= 0])
    mixed = sums[0]
    if from_below is not None:
        mixed = mixed + from_below.astype(F32) + from_above.astype(F32)
    return mixed.astype(BF16)


def solution(mesh):
    groups, lanes = mesh.shape["dp"], mesh.shape["expert"]
    y_size = groups // 2
    x_size = y_size if lanes % y_size == 0 else 1
    fine = Mesh(mesh.devices.reshape(y_size, 2, lanes // x_size, x_size), ("y", "core", "z", "x"))
    split = ("y", "core", "z", "x")
    return jax.shard_map(
        local,
        mesh=fine,
        in_specs=(P(split, None), P(split, None), P(split, None), P(split, None, None), P(split, None, None), P(split, None, None)),
        out_specs=P(split, None),
        check_vma=False,
    )
```

time: 877 us -> 440 us (0.50)
  waiting for transfers between devices: 536 us -> 154 us
  local copies, waits for them, and re-layouts: 125 us -> 17.3 us
  matrix products: 99.7 us -> 169 us
  other arithmetic: 28.6 us -> 18.8 us
    all_to_all x3 -> x8, waiting for transfers between devices: 536 us -> 87 us  [the longest x4 75.3 us: local(): lax.all_to_all(sent.reshape(chips, rows, width + EXTRA), ('y', 'x'), 0, 0...]
    gather x4 -> x0, local copies, waits for them, and re-layouts: 87.5 us -> none  [the longest x1 28.3 us: local(): results = finished[inverse_of(ordering)]]
    dot_general x16 -> x32, matrix products: 99.7 us -> 169 us  [the longest x8 97.1 us: local(): part = jnp.dot(hidden, w_down, preferred_element_type=F32)]
    ppermute x0 -> x15, waiting for transfers between devices: none -> 66.6 us  [the longest x3 61.1 us: local(): moving_down[r] = lax.ppermute(moving_down[r - 1], 'z', shifted(z_size, -1))]
    ppermute x0 -> x15, starting transfers between devices: none -> 38.7 us  [the longest x3 15.8 us: local(): moving_up[r] = lax.ppermute(moving_up[r - 1], 'z', shifted(z_size, 1))]
    all_to_all x3 -> x8, starting transfers between devices: 71.6 us -> 33.8 us  [the longest x4 17.7 us: local(): lax.all_to_all(sent.reshape(chips, rows, width + EXTRA), ('y', 'x'), 0, 0...]
    scatter x3 -> x0, local copies, waits for them, and re-layouts: 28.5 us -> none  [the longest x1 16.6 us: inverse_of(): jnp.zeros((entries,), jnp.int32).at[ordering]]
    another operation x3 -> x0, other arithmetic: 9.15 us -> none
  transfers between devices with their start and end apart: 3 -> 23, of which waited for: 2 -> 13; matrix products, arithmetic and copies ran while one was open for 4% -> 39% of each run, Pallas kernels for 0% -> 0%
where the time goes in v1:
time: 440 us; the launch traced here: 432 us
  matrix products  169 us (38%)
  waiting for transfers between devices  154 us (35%)
  starting transfers between devices  72.4 us (16%)
  other arithmetic  18.8 us (4%)
  local copies, waits for them, and re-layouts  17.3 us (4%)
    dot_general x8, matrix products, local(): part = jnp.dot(hidden, w_down, preferred_element_type=F32)  97.1 us
    all_to_all x4, waiting for transfers between devices, local(): lax.all_to_all(sent.reshape(chips, rows, width + EXTRA), ('y', 'x'), 0, 0...  75.3 us
    ppermute x3, waiting for transfers between devices, local(): moving_down[r] = lax.ppermute(moving_down[r - 1], 'z', shifted(z_size, -1))  61.1 us
    dot_general x4, matrix products, local(): gate = jnp.dot(data, w_gate, preferred_element_type=F32)  22.9 us
    dot_general x4, matrix products, local(): up = jnp.dot(data, w_up, preferred_element_type=F32)  22.6 us
    all_to_all x4, starting transfers between devices, local(): lax.all_to_all(sent.reshape(chips, rows, width + EXTRA), ('y', 'x'), 0, 0...  17.7 us
    dot_general x8, matrix products, local(): term = jnp.dot(mix, back, preferred_element_type=F32)  16.2 us
    all_to_all x4, starting transfers between devices, local(): lax.all_to_all(out.astype(BF16).reshape(chips, rows, width), ('y', 'x'),...  16.1 us
  transfers between devices with their start and end apart: 23, of which 13 were waited for; matrix products, arithmetic and copies ran while one was open for 39% of the time, Pallas kernels for 0%

profile of v1, /device:TPU:0, one launch (start us, length us, event | category | flops | bytes accessed | tf_op | source)
XLA Modules:
  0.0 432.3 jit_solution(13586732764176158938)
XLA Ops:
  2.0 2.3 concatenate.11
  5.6 5.6 %collective-permute-start.4 = (bf16[128,4224]{1,0:T(8,128)(2,1)S(1)}, bf16[128,4224]{1,0:T(8,128)(2,1)S(1)}, u32[]{:S(2)}, u32[]{:S(2)}) collective-permute-start(bf16[128,4224]{1,0:T(8,128)(2,1)S(1)} %concatenate.11), channel_id=1, source_target_pairs={{0,2},{2,4},{4,6},{1,3},{3,5},{5,7},{8,10},{10,12},{12,14},{9,11},... | collective-permute-start | bytes 3244040 | tf_op jit(solution)/shard_map/ppermute | solution.py:81
  11.2 21.9 %collective-permute-done.3 = bf16[128,4224]{1,0:T(8,128)(2,1)S(1)} collective-permute-done((bf16[128,4224]{1,0:T(8,128)(2,1)S(1)}, bf16[128,4224]{1,0:T(8,128)(2,1)S(1)}, u32[]{:S(2)}, u32[]{:S(2)}) %collective-permute-start.3) | collective-permute-done | bytes 1081376 | tf_op jit(solution)/shard_map/ppermute | solution.py:82
  34.4 4.6 %collective-permute-start.6 = (bf16[128,4224]{1,0:T(8,128)(2,1)S(1)}, bf16[128,4224]{1,0:T(8,128)(2,1)S(1)}, u32[]{:S(2)}, u32[]{:S(2)}) collective-permute-start(bf16[128,4224]{1,0:T(8,128)(2,1)S(1)} %collective-permute-done.4), channel_id=1, source_target_pairs={{0,2},{2,4},{4,6},{1,3},{3,5},{5,7},{8,10},{10,12},{12,14},{9,11},... | collective-permute-start | bytes 3244040 | tf_op jit(solution)/shard_map/ppermute | solution.py:81
  39.0 21.0 %collective-permute-done.5 = bf16[128,4224]{1,0:T(8,128)(2,1)S(1)} collective-permute-done((bf16[128,4224]{1,0:T(8,128)(2,1)S(1)}, bf16[128,4224]{1,0:T(8,128)(2,1)S(1)}, u32[]{:S(2)}, u32[]{:S(2)}) %collective-permute-start.5) | collective-permute-done | bytes 1081376 | tf_op jit(solution)/shard_map/ppermute | solution.py:82
  61.3 5.5 %collective-permute-start.8 = (bf16[128,4224]{1,0:T(8,128)(2,1)S(1)}, bf16[128,4224]{1,0:T(8,128)(2,1)}, u32[]{:S(2)}, u32[]{:S(2)}) collective-permute-start(bf16[128,4224]{1,0:T(8,128)(2,1)S(1)} %collective-permute-done.6), channel_id=1, source_target_pairs={{0,2},{2,4},{4,6},{1,3},{3,5},{5,7},{8,10},{10,12},{12,14},{9,11},... | collective-permute-start | bytes 3244040 | tf_op jit(solution)/shard_map/ppermute | solution.py:81
  67.8 18.3 %collective-permute-done.7 = bf16[128,4224]{1,0:T(8,128)(2,1)} collective-permute-done((bf16[128,4224]{1,0:T(8,128)(2,1)S(1)}, bf16[128,4224]{1,0:T(8,128)(2,1)}, u32[]{:S(2)}, u32[]{:S(2)}) %collective-permute-start.7) | collective-permute-done | bytes 1081376 | tf_op jit(solution)/shard_map/ppermute | solution.py:82
  87.2 3.4 select_select_fusion.5
  96.9 3.3 convolution_convert_fusion.3
  100.2 4.5 %all-to-all-start = ((bf16[4,64,4224]{2,1,0:T(8,128)(2,1)}), bf16[4,64,4224]{2,1,0:T(8,128)(2,1)}, u32[]{:S(2)}, u32[]{:S(2)}) async-start(bf16[4,64,4224]{2,1,0:T(8,128)(2,1)} %bitcast.3), calls=%async_computation | async-start | bytes 4325376 | tf_op jit(solution)/shard_map/all_to_all | solution.py:102
  106.8 21.2 %all-to-all-done = bf16[4,64,4224]{2,1,0:T(8,128)(2,1)} async-done(((bf16[4,64,4224]{2,1,0:T(8,128)(2,1)}), bf16[4,64,4224]{2,1,0:T(8,128)(2,1)}, u32[]{:S(2)}, u32[]{:S(2)}) %all-to-all-start) | async-done | bytes 2162720 | tf_op jit(solution)/shard_map/all_to_all | solution.py:102
  127.9 4.5 %all-to-all-start.4 = ((bf16[4,64,4224]{2,1,0:T(8,128)(2,1)}), bf16[4,64,4224]{2,1,0:T(8,128)(2,1)}, u32[]{:S(2)}, u32[]{:S(2)}) async-start(bf16[4,64,4224]{2,1,0:T(8,128)(2,1)} %bitcast.22), calls=%async_computation.4 | async-start | bytes 4325376 | tf_op jit(solution)/shard_map/all_to_all | solution.py:102
  134.4 23.0 %all-to-all-done.4 = bf16[4,64,4224]{2,1,0:T(8,128)(2,1)} async-done(((bf16[4,64,4224]{2,1,0:T(8,128)(2,1)}), bf16[4,64,4224]{2,1,0:T(8,128)(2,1)}, u32[]{:S(2)}, u32[]{:S(2)}) %all-to-all-start.4) | async-done | bytes 2162720 | tf_op jit(solution)/shard_map/all_to_all | solution.py:102
  157.5 3.7 all-to-all-start.2
  174.5 11.7 %all-to-all-done.2 = bf16[4,64,4224]{2,1,0:T(8,128)(2,1)S(1)} async-done(((bf16[4,64,4224]{2,1,0:T(8,128)(2,1)}), bf16[4,64,4224]{2,1,0:T(8,128)(2,1)S(1)}, u32[]{:S(2)}, u32[]{:S(2)}) %all-to-all-start.2) | async-done | bytes 2162720 | tf_op jit(solution)/shard_map/all_to_all | solution.py:102
  186.2 5.0 %all-to-all-start.6 = ((bf16[4,64,4224]{2,1,0:T(8,128)(2,1)}), bf16[4,64,4224]{2,1,0:T(8,128)(2,1)}, u32[]{:S(2)}, u32[]{:S(2)}) async-start(bf16[4,64,4224]{2,1,0:T(8,128)(2,1)} %bitcast.29), calls=%async_computation.6 | async-start | bytes 4325376 | tf_op jit(solution)/shard_map/all_to_all | solution.py:102
  191.8 4.6 %fusion.39 = f32[256,768]{1,0:T(8,128)S(1)} fusion(bf16[256,4224]{1,0:T(8,128)(2,1)S(1)} %bitcast.119, bf16[1,4096,768]{2,1,0:T(8,128)(2,1)} %param.9), kind=kOutput, calls=%fused_computation.61 | convolution fusion | flops 1610612736 | bytes 9175040 | tf_op jit(solution)/shard_map/dot_general | solution.py:113
  196.4 19.4 %all-to-all-done.6 = bf16[4,64,4224]{2,1,0:T(8,128)(2,1)} async-done(((bf16[4,64,4224]{2,1,0:T(8,128)(2,1)}), bf16[4,64,4224]{2,1,0:T(8,128)(2,1)}, u32[]{:S(2)}, u32[]{:S(2)}) %all-to-all-start.6) | async-done | bytes 2162720 | tf_op jit(solution)/shard_map/all_to_all | solution.py:102
  217.0 6.1 %fusion.23 = f32[256,768]{1,0:T(8,128)} fusion(bf16[256,4224]{1,0:T(8,128)(2,1)} %bitcast.30, bf16[1,4096,768]{2,1,0:T(8,128)(2,1)} %param.9), kind=kOutput, calls=%fused_computation.45 | convolution fusion | flops 1610612736 | bytes 9175040 | tf_op jit(solution)/shard_map/dot_general | solution.py:113
  223.9 6.1 %fusion.31 = f32[256,768]{1,0:T(8,128)} fusion(bf16[256,4224]{1,0:T(8,128)(2,1)} %bitcast.23, bf16[1,4096,768]{2,1,0:T(8,128)(2,1)} %param.9), kind=kOutput, calls=%fused_computation.53 | convolution fusion | flops 1610612736 | bytes 9175040 | tf_op jit(solution)/shard_map/dot_general | solution.py:113
  230.0 6.1 %fusion.47 = f32[256,768]{1,0:T(8,128)} fusion(bf16[256,4224]{1,0:T(8,128)(2,1)} %bitcast.6, bf16[1,4096,768]{2,1,0:T(8,128)(2,1)} %param.9), kind=kOutput, calls=%fused_computation.69 | convolution fusion | flops 1610612736 | bytes 9175040 | tf_op jit(solution)/shard_map/dot_general | solution.py:113
  236.1 11.2 %fusion.96 = f32[256,4096]{1,0:T(8,128)} fusion(bf16[256,4224]{1,0:T(8,128)(2,1)S(1)} %bitcast.120, f32[256,768]{1,0:T(8,128)S(1)} %fusion.39, pred[256]{0:T(512)(128)(4,1)S(1)} %eq.321, bf16[1,768,4096]{2,1,0:T(8,128)(2,1)} %param.11, bf16[1,4096,768]{2,1,0:T(8,128)(2,1)} %param.10), kind=kOutput, calls=%fused_computation.99 | convolution fusion | flops 3222601728 | bytes 19661312 | tf_op jit(solution)/shard_map/dot_general | solution.py:116
  247.3 12.2 %fusion.90 = f32[256,4096]{1,0:T(8,128)} fusion(bf16[256,4224]{1,0:T(8,128)(2,1)} %bitcast.30, f32[256,768]{1,0:T(8,128)} %fusion.23, pred[256]{0:T(512)(128)(4,1)S(1)} %eq.341, bf16[1,768,4096]{2,1,0:T(8,128)(2,1)} %param.11, bf16[1,4096,768]{2,1,0:T(8,128)(2,1)} %param.10), kind=kOutput, calls=%fused_computation.97 | convolution fusion | flops 3222601728 | bytes 19661056 | tf_op jit(solution)/shard_map/dot_general | solution.py:116
  259.5 11.9 %fusion.93 = f32[256,4096]{1,0:T(8,128)} fusion(bf16[256,4224]{1,0:T(8,128)(2,1)} %bitcast.23, f32[256,768]{1,0:T(8,128)S(1)} %copy-done.24, pred[256]{0:T(512)(128)(4,1)S(1)} %eq.331, bf16[1,768,4096]{2,1,0:T(8,128)(2,1)} %param.11, bf16[1,4096,768]{2,1,0:T(8,128)(2,1)} %param.10), kind=kOutput, calls=%fused_computation.98 | convolution fusion | flops 3222601728 | bytes 19661056 | tf_op jit(solution)/shard_map/dot_general | solution.py:116
  271.4 11.8 %fusion.99 = f32[256,4096]{1,0:T(8,128)} fusion(bf16[256,4224]{1,0:T(8,128)(2,1)} %bitcast.6, f32[256,768]{1,0:T(8,128)S(1)} %copy-done.23, pred[256]{0:T(512)(128)(4,1)S(1)} %eq.306, bf16[1,768,4096]{2,1,0:T(8,128)(2,1)} %param.11, bf16[1,4096,768]{2,1,0:T(8,128)(2,1)} %param.10), kind=kOutput, calls=%fused_computation.100 | convolution fusion | flops 3222601728 | bytes 19661056 | tf_op jit(solution)/shard_map/dot_general | solution.py:116
  283.2 5.2 %fusion.17 = f32[256,768]{1,0:T(8,128)S(1)} fusion(bf16[4096,768]{1,0:T(8,128)(2,1)} %collective-permute-done.1, bf16[256,4224]{1,0:T(8,128)(2,1)} %bitcast.30), kind=kOutput, calls=%fused_computation.39 | convolution fusion | flops 1610612736 | bytes 9175040 | tf_op jit(solution)/shard_map/dot_general | solution.py:114
  288.5 12.5 %fusion.3 = bf16[256,4096]{1,0:T(8,128)(2,1)} fusion(f32[256,4096]{1,0:T(8,128)} %fusion.90, bf16[768,4096]{1,0:T(8,128)(2,1)} %collective-permute-done.2, f32[256,768]{1,0:T(8,128)S(1)} %fusion.17, bf16[4096,768]{1,0:T(8,128)(2,1)} %collective-permute-done, bf16[256,4224]{1,0:T(8,128)(2,1)} %bitcast.30, pred[256]{0:T(512)(128)(4,1)S(1)} %eq.343), kind=kOutput, calls=%fused_computation.11 | convolution fusion | flops 3224698880 | bytes 21758208 | tf_op jit(solution)/shard_map/dot_general | solution.py:116
  301.0 3.6 all-to-all-start.7
  304.6 6.1 %fusion.33 = f32[256,768]{1,0:T(8,128)} fusion(bf16[4096,768]{1,0:T(8,128)(2,1)} %collective-permute-done.1, bf16[256,4224]{1,0:T(8,128)(2,1)} %bitcast.121), kind=kOutput, calls=%fused_computation.55 | convolution fusion | flops 1610612736 | bytes 9175040 | tf_op jit(solution)/shard_map/dot_general | solution.py:114
  310.7 5.2 %fusion.25 = f32[256,768]{1,0:T(8,128)S(1)} fusion(bf16[4096,768]{1,0:T(8,128)(2,1)} %collective-permute-done.1, bf16[256,4224]{1,0:T(8,128)(2,1)} %bitcast.23), kind=kOutput, calls=%fused_computation.47 | convolution fusion | flops 1610612736 | bytes 9175040 | tf_op jit(solution)/shard_map/dot_general | solution.py:114
  315.9 12.3 %fusion.2 = bf16[256,4096]{1,0:T(8,128)(2,1)} fusion(f32[256,4096]{1,0:T(8,128)} %fusion.93, bf16[768,4096]{1,0:T(8,128)(2,1)} %collective-permute-done.2, f32[256,768]{1,0:T(8,128)S(1)} %fusion.25, bf16[4096,768]{1,0:T(8,128)(2,1)} %collective-permute-done, bf16[256,4224]{1,0:T(8,128)(2,1)} %bitcast.23, pred[256]{0:T(512)(128)(4,1)S(1)} %eq.333), kind=kOutput, calls=%fused_computation.10 | convolution fusion | flops 3224698880 | bytes 21758208 | tf_op jit(solution)/shard_map/dot_general | solution.py:116
  330.2 3.6 all-to-all-start.5
  333.9 2.2 convolution_bitcast_fusion
  336.1 2.2 fusion.236
  338.3 4.2 collective-permute-start.9
  344.4 12.5 %fusion.1 = bf16[256,4096]{1,0:T(8,128)(2,1)} fusion(f32[256,4096]{1,0:T(8,128)} %fusion.96, bf16[768,4096]{1,0:T(8,128)(2,1)} %collective-permute-done.2, f32[256,768]{1,0:T(8,128)} %fusion.33, bf16[4096,768]{1,0:T(8,128)(2,1)} %collective-permute-done, bf16[256,4224]{1,0:T(8,128)(2,1)} %bitcast.122, pred[256]{0:T(512)(128)(4,1)S(1)} %eq.323), kind=kOutput, calls=%fused_computation.9 | convolution fusion | flops 3224698880 | bytes 21758208 | tf_op jit(solution)/shard_map/dot_general | solution.py:116
  356.9 6.1 %fusion.41 = f32[256,768]{1,0:T(8,128)} fusion(bf16[4096,768]{1,0:T(8,128)(2,1)} %collective-permute-done.1, bf16[256,4224]{1,0:T(8,128)(2,1)} %bitcast.6), kind=kOutput, calls=%fused_computation.63 | convolution fusion | flops 1610612736 | bytes 9175040 | tf_op jit(solution)/shard_map/dot_general | solution.py:114
  364.4 4.1 all-to-all-start.3
  368.5 2.2 convolution_bitcast_fusion.2
  371.8 4.4 %fusion.11 = (bf16[128,4096]{1,0:T(8,128)(2,1)}, bf16[128,4096]{1,0:T(8,128)(2,1)S(1)}, f32[128,4096]{1,0:T(8,128)}) fusion(f32[128,4096]{1,0:T(8,128)S(1)} %copy-done.5, bf16[128,4096]{1,0:T(8,128)(2,1)} %copy-done.12, pred[]{:T(512)S(6)} %eq.312, pred[]{:T(512)S(6)} %eq.311, bf16[128,4096]{1,0:T(8,128)(2,1)} %collective-permute-done.12, pred[]{:T(512)S(6)} %eq.313, ...), kind=kOutput, calls=%fused_computation.31 | convolution fusion | flops 274726912 | bytes 12648451 | tf_op jit(solution)/shard_map/dot_general | solution.py:126
  376.2 2.3 collective-permute-start.10
  380.1 12.5 %fusion = bf16[256,4096]{1,0:T(8,128)(2,1)} fusion(f32[256,4096]{1,0:T(8,128)} %fusion.99, bf16[768,4096]{1,0:T(8,128)(2,1)} %collective-permute-done.2, f32[256,768]{1,0:T(8,128)} %fusion.41, bf16[4096,768]{1,0:T(8,128)(2,1)} %collective-permute-done, bf16[256,4224]{1,0:T(8,128)(2,1)} %bitcast.6, pred[256]{0:T(512)(128)(4,1)S(1)} %eq.310), kind=kOutput, calls=%fused_computation.8 | convolution fusion | flops 3224698880 | bytes 21758208 | tf_op jit(solution)/shard_map/dot_general | solution.py:116
  392.7 4.7 %all-to-all-start.1 = ((bf16[4,64,4096]{2,1,0:T(8,128)(2,1)}), bf16[4,64,4096]{2,1,0:T(8,128)(2,1)}, u32[]{:S(2)}, u32[]{:S(2)}) async-start(bf16[4,64,4096]{2,1,0:T(8,128)(2,1)} %bitcast.124), calls=%async_computation.1 | async-start | bytes 4194304 | tf_op jit(solution)/shard_map/all_to_all | solution.py:118
  399.5 2.3 fusion.9
  403.0 7.0 %collective-permute-start.11 = (bf16[128,4096]{1,0:T(8,128)(2,1)S(1)}, bf16[128,4096]{1,0:T(8,128)(2,1)}, u32[]{:S(2)}, u32[]{:S(2)}) collective-permute-start(bf16[128,4096]{1,0:T(8,128)(2,1)S(1)} %get-tuple-element.68), channel_id=1, source_target_pairs={{0,2},{2,4},{4,6},{1,3},{3,5},{5,7},{8,10},{10,12},{12,14},{9,11},... | collective-permute-start | bytes 3145736 | tf_op jit(solution)/shard_map/ppermute | solution.py:143
  410.1 11.0 %all-to-all-done.1 = bf16[4,64,4096]{2,1,0:T(8,128)(2,1)} async-done(((bf16[4,64,4096]{2,1,0:T(8,128)(2,1)}), bf16[4,64,4096]{2,1,0:T(8,128)(2,1)}, u32[]{:S(2)}, u32[]{:S(2)}) %all-to-all-start.1) | async-done | bytes 2097184 | tf_op jit(solution)/shard_map/all_to_all | solution.py:118
  425.3 2.8 collective-permute-done.14
  429.2 2.6 add_convert_fusion
  (152 shorter events, 50.1 us)
Async XLA Ops:
  4.3 81.8 %copy-start.6 = (bf16[128,4224]{1,0:T(8,128)(2,1)}, bf16[128,4224]{1,0:T(8,128)(2,1)S(1)}, u32[]{:S(2)}) copy-start(bf16[128,4224]{1,0:T(8,128)(2,1)S(1)} %concatenate.11) | copy-start | bytes 3244036
  4.3 28.8 %collective-permute-start.3 = (bf16[128,4224]{1,0:T(8,128)(2,1)S(1)}, bf16[128,4224]{1,0:T(8,128)(2,1)S(1)}, u32[]{:S(2)}, u32[]{:S(2)}) collective-permute-start(bf16[128,4224]{1,0:T(8,128)(2,1)S(1)} %concatenate.11), channel_id=1, source_target_pairs={{2,0},{4,2},{6,4},{3,1},{5,3},{7,5},{10,8},{12,10},{14,12},{11,9},... | collective-permute-start | bytes 3244040 | tf_op jit(solution)/shard_map/ppermute | solution.py:82
  5.6 28.8 %collective-permute-start.4 = (bf16[128,4224]{1,0:T(8,128)(2,1)S(1)}, bf16[128,4224]{1,0:T(8,128)(2,1)S(1)}, u32[]{:S(2)}, u32[]{:S(2)}) collective-permute-start(bf16[128,4224]{1,0:T(8,128)(2,1)S(1)} %concatenate.11), channel_id=1, source_target_pairs={{0,2},{2,4},{4,6},{1,3},{3,5},{5,7},{8,10},{10,12},{12,14},{9,11},... | collective-permute-start | bytes 3244040 | tf_op jit(solution)/shard_map/ppermute | solution.py:81
  33.1 33.8 %copy-start.8 = (bf16[128,4224]{1,0:T(8,128)(2,1)}, bf16[128,4224]{1,0:T(8,128)(2,1)S(1)}, u32[]{:S(2)}) copy-start(bf16[128,4224]{1,0:T(8,128)(2,1)S(1)} %collective-permute-done.3) | copy-start | bytes 3244036
  33.1 26.9 %collective-permute-start.5 = (bf16[128,4224]{1,0:T(8,128)(2,1)S(1)}, bf16[128,4224]{1,0:T(8,128)(2,1)S(1)}, u32[]{:S(2)}, u32[]{:S(2)}) collective-permute-start(bf16[128,4224]{1,0:T(8,128)(2,1)S(1)} %collective-permute-done.3), channel_id=1, source_target_pairs={{2,0},{4,2},{6,4},{3,1},{5,3},{7,5},{10,8},{12,10},{14,12},{11,9},... | collective-permute-start | bytes 3244040 | tf_op jit(solution)/shard_map/ppermute | solution.py:82
  34.4 32.5 %copy-start.9 = (bf16[128,4224]{1,0:T(8,128)(2,1)}, bf16[128,4224]{1,0:T(8,128)(2,1)S(1)}, u32[]{:S(2)}) copy-start(bf16[128,4224]{1,0:T(8,128)(2,1)S(1)} %collective-permute-done.4) | copy-start | bytes 3244036
  34.4 26.9 %collective-permute-start.6 = (bf16[128,4224]{1,0:T(8,128)(2,1)S(1)}, bf16[128,4224]{1,0:T(8,128)(2,1)S(1)}, u32[]{:S(2)}, u32[]{:S(2)}) collective-permute-start(bf16[128,4224]{1,0:T(8,128)(2,1)S(1)} %collective-permute-done.4), channel_id=1, source_target_pairs={{0,2},{2,4},{4,6},{1,3},{3,5},{5,7},{8,10},{10,12},{12,14},{9,11},... | collective-permute-start | bytes 3244040 | tf_op jit(solution)/shard_map/ppermute | solution.py:81
  60.0 26.1 %copy-start.10 = (bf16[128,4224]{1,0:T(8,128)(2,1)}, bf16[128,4224]{1,0:T(8,128)(2,1)S(1)}, u32[]{:S(2)}) copy-start(bf16[128,4224]{1,0:T(8,128)(2,1)S(1)} %collective-permute-done.5) | copy-start | bytes 3244036
  60.0 26.1 %collective-permute-start.7 = (bf16[128,4224]{1,0:T(8,128)(2,1)S(1)}, bf16[128,4224]{1,0:T(8,128)(2,1)}, u32[]{:S(2)}, u32[]{:S(2)}) collective-permute-start(bf16[128,4224]{1,0:T(8,128)(2,1)S(1)} %collective-permute-done.5), channel_id=1, source_target_pairs={{2,0},{4,2},{6,4},{3,1},{5,3},{7,5},{10,8},{12,10},{14,12},{11,9},... | collective-permute-start | bytes 3244040 | tf_op jit(solution)/shard_map/ppermute | solution.py:82
  61.3 24.8 %copy-start.11 = (bf16[128,4224]{1,0:T(8,128)(2,1)}, bf16[128,4224]{1,0:T(8,128)(2,1)S(1)}, u32[]{:S(2)}) copy-start(bf16[128,4224]{1,0:T(8,128)(2,1)S(1)} %collective-permute-done.6) | copy-start | bytes 3244036
  61.3 25.9 %collective-permute-start.8 = (bf16[128,4224]{1,0:T(8,128)(2,1)S(1)}, bf16[128,4224]{1,0:T(8,128)(2,1)}, u32[]{:S(2)}, u32[]{:S(2)}) collective-permute-start(bf16[128,4224]{1,0:T(8,128)(2,1)S(1)} %collective-permute-done.6), channel_id=1, source_target_pairs={{0,2},{2,4},{4,6},{1,3},{3,5},{5,7},{8,10},{10,12},{12,14},{9,11},... | collective-permute-start | bytes 3244040 | tf_op jit(solution)/shard_map/ppermute | solution.py:81
  67.1 27.6 %copy-start.17 = (f32[128,8]{0,1:T(8,128)}, f32[128,8]{0,1:T(8,128)S(1)}, u32[]{:S(2)}) copy-start(f32[128,8]{0,1:T(8,128)S(1)} %copy.35) | copy-start | bytes 12292
  67.8 26.9 %copy-start.21 = (f32[4,2]{1,0:T(4,128)}, f32[4,2]{1,0:T(4,128)S(1)}, u32[]{:S(2)}) copy-start(f32[4,2]{1,0:T(4,128)S(1)} %add_convert_fusion.1) | copy-start | bytes 100
  91.3 4.6 %copy-start.18 = (f32[128,8]{0,1:T(8,128)}, f32[128,8]{0,1:T(8,128)S(1)}, u32[]{:S(2)}) copy-start(f32[128,8]{0,1:T(8,128)S(1)} %copy.45) | copy-start | bytes 12292
  93.0 3.0 copy-start.19
  94.7 1.3 copy-start.20
  100.2 27.7 %all-to-all-start = ((bf16[4,64,4224]{2,1,0:T(8,128)(2,1)}), bf16[4,64,4224]{2,1,0:T(8,128)(2,1)}, u32[]{:S(2)}, u32[]{:S(2)}) async-start(bf16[4,64,4224]{2,1,0:T(8,128)(2,1)} %bitcast.3), calls=%async_computation | async-start | bytes 4325376 | tf_op jit(solution)/shard_map/all_to_all | solution.py:102
  127.9 29.5 %all-to-all-start.4 = ((bf16[4,64,4224]{2,1,0:T(8,128)(2,1)}), bf16[4,64,4224]{2,1,0:T(8,128)(2,1)}, u32[]{:S(2)}, u32[]{:S(2)}) async-start(bf16[4,64,4224]{2,1,0:T(8,128)(2,1)} %bitcast.22), calls=%async_computation.4 | async-start | bytes 4325376 | tf_op jit(solution)/shard_map/all_to_all | solution.py:102
  157.5 9.9 %copy-start.16 = (f32[128,8]{1,0:T(8,128)S(1)}, f32[128,8]{1,0:T(8,128)}, u32[]{:S(2)}) copy-start(f32[128,8]{1,0:T(8,128)} %get-tuple-element.76) | copy-start | bytes 12292
  157.5 28.7 %all-to-all-start.2 = ((bf16[4,64,4224]{2,1,0:T(8,128)(2,1)}), bf16[4,64,4224]{2,1,0:T(8,128)(2,1)S(1)}, u32[]{:S(2)}, u32[]{:S(2)}) async-start(bf16[4,64,4224]{2,1,0:T(8,128)(2,1)} %bitcast.15), calls=%async_computation.2 | async-start | bytes 4325376 | tf_op jit(solution)/shard_map/all_to_all | solution.py:102
  161.2 127.2 %collective-permute-start.2 = (bf16[768,4096]{1,0:T(8,128)(2,1)}, bf16[768,4096]{1,0:T(8,128)(2,1)}, u32[]{:S(2)}, u32[]{:S(2)}) collective-permute-start(bf16[768,4096]{1,0:T(8,128)(2,1)} %bitcast.136), channel_id=1, source_target_pairs={{0,8},{8,0},{1,9},{9,1},{2,10},{10,2},{3,11},{11,3},{4,12},{12,4},... | collective-permute-start | bytes 18874376 | tf_op jit(solution)/shard_map/ppermute | solution.py:68
  161.3 121.9 %collective-permute-start.1 = (bf16[4096,768]{1,0:T(8,128)(2,1)}, bf16[4096,768]{1,0:T(8,128)(2,1)}, u32[]{:S(2)}, u32[]{:S(2)}) collective-permute-start(bf16[4096,768]{1,0:T(8,128)(2,1)} %bitcast.135), channel_id=1, source_target_pairs={{0,8},{8,0},{1,9},{9,1},{2,10},{10,2},{3,11},{11,3},{4,12},{12,4},... | collective-permute-start | bytes 18874376 | tf_op jit(solution)/shard_map/ppermute | solution.py:68
  161.8 126.6 %collective-permute-start = (bf16[4096,768]{1,0:T(8,128)(2,1)}, bf16[4096,768]{1,0:T(8,128)(2,1)}, u32[]{:S(2)}, u32[]{:S(2)}) collective-permute-start(bf16[4096,768]{1,0:T(8,128)(2,1)} %bitcast.137), channel_id=1, source_target_pairs={{0,8},{8,0},{1,9},{9,1},{2,10},{10,2},{3,11},{11,3},{4,12},{12,4},... | collective-permute-start | bytes 18874376 | tf_op jit(solution)/shard_map/ppermute | solution.py:68
  186.2 49.9 %copy-start.7 = (bf16[4,64,4224]{2,1,0:T(8,128)(2,1)}, bf16[4,64,4224]{2,1,0:T(8,128)(2,1)S(1)}, u32[]{:S(2)}) copy-start(bf16[4,64,4224]{2,1,0:T(8,128)(2,1)S(1)} %all-to-all-done.2) | copy-start | bytes 6488068
  186.2 29.6 %all-to-all-start.6 = ((bf16[4,64,4224]{2,1,0:T(8,128)(2,1)}), bf16[4,64,4224]{2,1,0:T(8,128)(2,1)}, u32[]{:S(2)}, u32[]{:S(2)}) async-start(bf16[4,64,4224]{2,1,0:T(8,128)(2,1)} %bitcast.29), calls=%async_computation.6 | async-start | bytes 4325376 | tf_op jit(solution)/shard_map/all_to_all | solution.py:102
  217.0 6.1 %copy-start.22 = (f32[64]{0:T(128)S(1)}, f32[64]{0:T(128)}, u32[]{:S(2)}) copy-start(f32[64]{0:T(128)} %iota_convert_fusion) | copy-start | bytes 772
  247.3 12.2 %copy-start.24 = (f32[256,768]{1,0:T(8,128)S(1)}, f32[256,768]{1,0:T(8,128)}, u32[]{:S(2)}) copy-start(f32[256,768]{1,0:T(8,128)} %fusion.31) | copy-start | bytes 2359300
  259.5 11.9 %copy-start.23 = (f32[256,768]{1,0:T(8,128)S(1)}, f32[256,768]{1,0:T(8,128)}, u32[]{:S(2)}) copy-start(f32[256,768]{1,0:T(8,128)} %fusion.47) | copy-start | bytes 2359300
  301.0 27.9 %all-to-all-start.7 = ((bf16[4,64,4096]{2,1,0:T(8,128)(2,1)}), bf16[4,64,4096]{2,1,0:T(8,128)(2,1)S(1)}, u32[]{:S(2)}, u32[]{:S(2)}) async-start(bf16[4,64,4096]{2,1,0:T(8,128)(2,1)} %bitcast.126), calls=%async_computation.7 | async-start | bytes 4194304 | tf_op jit(solution)/shard_map/all_to_all | solution.py:118
  328.3 5.6 %copy-start.15 = (bf16[128,4,64]{0,2,1:T(8,128)(2,1)S(1)}, bf16[128,4,64]{0,2,1:T(8,128)(2,1)}, u32[]{:S(2)}) copy-start(bf16[128,4,64]{0,2,1:T(8,128)(2,1)} %get-tuple-element.54) | copy-start | bytes 196612
  328.9 1.3 copy-start.2
  330.2 32.8 %all-to-all-start.5 = ((bf16[4,64,4096]{2,1,0:T(8,128)(2,1)}), bf16[4,64,4096]{2,1,0:T(8,128)(2,1)S(1)}, u32[]{:S(2)}, u32[]{:S(2)}) async-start(bf16[4,64,4096]{2,1,0:T(8,128)(2,1)} %bitcast.125), calls=%async_computation.5 | async-start | bytes 4194304 | tf_op jit(solution)/shard_map/all_to_all | solution.py:118
  333.8 2.2 copy-start.3
  333.9 2.2 copy-start.14
  338.3 32.5 %collective-permute-start.9 = (bf16[128,4096]{1,0:T(8,128)(2,1)}, bf16[128,4096]{1,0:T(8,128)(2,1)S(1)}, u32[]{:S(2)}, u32[]{:S(2)}) collective-permute-start(bf16[128,4096]{1,0:T(8,128)(2,1)} %get-tuple-element.104), channel_id=1, source_target_pairs={{0,2},{1,3},{8,10},{9,11},{16,18},{17,19},{24,26},{25,27}} | collective-permute-start | bytes 3145736 | tf_op jit(solution)/shard_map/ppermute | solution.py:143
  342.5 28.3 %collective-permute-start.12 = (bf16[128,4096]{1,0:T(8,128)(2,1)}, bf16[128,4096]{1,0:T(8,128)(2,1)}, u32[]{:S(2)}, u32[]{:S(2)}) collective-permute-start(bf16[128,4096]{1,0:T(8,128)(2,1)} %get-tuple-element.104), channel_id=1, source_target_pairs={{6,4},{7,5},{14,12},{15,13},{22,20},{23,21},{30,28},{31,29}} | collective-permute-start | bytes 3145736 | tf_op jit(solution)/shard_map/ppermute | solution.py:144
  363.0 1.4 copy-start
  364.4 28.3 %all-to-all-start.3 = ((bf16[4,64,4096]{2,1,0:T(8,128)(2,1)}), bf16[4,64,4096]{2,1,0:T(8,128)(2,1)S(1)}, u32[]{:S(2)}, u32[]{:S(2)}) async-start(bf16[4,64,4096]{2,1,0:T(8,128)(2,1)} %bitcast.123), calls=%async_computation.3 | async-start | bytes 4194304 | tf_op jit(solution)/shard_map/all_to_all | solution.py:118
  368.5 3.3 copy-start.1
  368.5 3.3 copy-start.5
  368.5 3.3 copy-start.13
  370.8 1.0 copy-start.12
  376.2 22.7 %collective-permute-start.10 = (bf16[128,4096]{1,0:T(8,128)(2,1)}, bf16[128,4096]{1,0:T(8,128)(2,1)}, u32[]{:S(2)}, u32[]{:S(2)}) collective-permute-start(bf16[128,4096]{1,0:T(8,128)(2,1)} %get-tuple-element.70), channel_id=1, source_target_pairs={{0,2},{2,4},{1,3},{3,5},{8,10},{10,12},{9,11},{11,13},{16,18},{18,... | collective-permute-start | bytes 3145736 | tf_op jit(solution)/shard_map/ppermute | solution.py:143
  378.4 20.4 %collective-permute-start.13 = (bf16[128,4096]{1,0:T(8,128)(2,1)S(1)}, bf16[128,4096]{1,0:T(8,128)(2,1)}, u32[]{:S(2)}, u32[]{:S(2)}) collective-permute-start(bf16[128,4096]{1,0:T(8,128)(2,1)S(1)} %get-tuple-element.71), channel_id=1, source_target_pairs={{4,2},{6,4},{5,3},{7,5},{12,10},{14,12},{13,11},{15,13},{20,18},{2... | collective-permute-start | bytes 3145736 | tf_op jit(solution)/shard_map/ppermute | solution.py:144
  392.7 28.4 %all-to-all-start.1 = ((bf16[4,64,4096]{2,1,0:T(8,128)(2,1)}), bf16[4,64,4096]{2,1,0:T(8,128)(2,1)}, u32[]{:S(2)}, u32[]{:S(2)}) async-start(bf16[4,64,4096]{2,1,0:T(8,128)(2,1)} %bitcast.124), calls=%async_computation.1 | async-start | bytes 4194304 | tf_op jit(solution)/shard_map/all_to_all | solution.py:118
  397.9 1.6 copy-start.4
  401.7 26.3 %collective-permute-start.14 = (bf16[128,4096]{1,0:T(8,128)(2,1)S(1)}, bf16[128,4096]{1,0:T(8,128)(2,1)S(1)}, u32[]{:S(2)}, u32[]{:S(2)}) collective-permute-start(bf16[128,4096]{1,0:T(8,128)(2,1)S(1)} %get-tuple-element.69), channel_id=1, source_target_pairs={{2,0},{4,2},{6,4},{3,1},{5,3},{7,5},{10,8},{12,10},{14,12},{11,9},... | collective-permute-start | bytes 3145736 | tf_op jit(solution)/shard_map/ppermute | solution.py:144
  403.0 26.2 %collective-permute-start.11 = (bf16[128,4096]{1,0:T(8,128)(2,1)S(1)}, bf16[128,4096]{1,0:T(8,128)(2,1)}, u32[]{:S(2)}, u32[]{:S(2)}) collective-permute-start(bf16[128,4096]{1,0:T(8,128)(2,1)S(1)} %get-tuple-element.68), channel_id=1, source_target_pairs={{0,2},{2,4},{4,6},{1,3},{3,5},{5,7},{8,10},{10,12},{12,14},{9,11},... | collective-permute-start | bytes 3145736 | tf_op jit(solution)/shard_map/ppermute | solution.py:143

commit v2 on v1

v2 whole, which is shorter than its diff:
```python
from functools import partial

import jax
import jax.numpy as jnp
from jax import lax
from jax.experimental import pallas as pl
from jax.experimental.pallas import tpu as pltpu
from jax.sharding import Mesh, PartitionSpec as P

F32 = jnp.float32
BF16 = jnp.bfloat16
EXTRA = 128
MIB = 2**20


def divisor(size, most):
    return next(d for d in range(min(size, most), 0, -1) if size % d == 0)


def experts_kernel(info, x_ref, g0, u0, d0, g1, u1, d1, o_ref, bg0, bu0, bd0, bg1, bu1, bd1, gate_ref, hid, sems, *, rows, top, tile, span):
    total, width = o_ref.shape
    ff = g0.shape[1]
    pairs = ((g0, bg0), (u0, bu0), (g1, bg1), (u1, bu1), (d0, bd0), (d1, bd1))
    copies = [pltpu.make_async_copy(src, dst, sems.at[n]) for n, (src, dst) in enumerate(pairs)]
    for c in copies:
        c.start()

    ids = x_ref[:, width:].astype(F32)
    is_id = lax.broadcasted_iota(jnp.int32, ids.shape, 1) < top
    low, high, flip = info[0].astype(F32), info[1].astype(F32), info[2].astype(F32)
    has_low = jnp.max(jnp.where(is_id & (ids == low), 1.0, 0.0), axis=1, keepdims=True)
    has_high = jnp.max(jnp.where(is_id & (ids == high), 1.0, 0.0), axis=1, keepdims=True)
    share = jnp.broadcast_to(has_low * (1.0 - 0.5 * has_high), (total, 128)).astype(BF16)
    r = lax.broadcasted_iota(jnp.int32, (total, total), 0)
    c = lax.broadcasted_iota(jnp.int32, (total, total), 1)
    same = jnp.where(r // rows == c // rows, 1.0, 0.0).astype(BF16)
    low_rows = jnp.dot(same, share, preferred_element_type=F32)
    at = (lax.broadcasted_iota(jnp.int32, (total, 128), 0) % rows).astype(F32)
    is_low = jnp.where(at < low_rows, 1.0, 0.0)
    first = (is_low * (1.0 - flip) + (1.0 - is_low) * flip)[:, :1]

    for which, (bg, bu) in enumerate(((bg0, bu0), (bg1, bu1))):
        keep = first if which == 0 else 1.0 - first
        copies[2 * which].wait()

        @pl.loop(0, ff // tile)
        def _(t):
            s = pl.ds(pl.multiple_of(t * tile, tile), tile)
            gate_ref[:, s] = jnp.dot(x_ref[:, :width], bg[:, s], preferred_element_type=F32)

        copies[2 * which + 1].wait()

        @pl.loop(0, ff // tile)
        def _(t):
            s = pl.ds(pl.multiple_of(t * tile, tile), tile)
            up = jnp.dot(x_ref[:, :width], bu[:, s], preferred_element_type=F32)
            gate = gate_ref[:, s]
            h = jnp.where(keep > 0.5, gate / (1.0 + jnp.exp(-gate)) * up, 0.0)
            hid[:, pl.ds(pl.multiple_of(which * ff + t * tile, tile), tile)] = h.astype(BF16)

    copies[4].wait()
    copies[5].wait()

    @pl.loop(0, width // span)
    def _(n):
        s = pl.ds(pl.multiple_of(n * span, span), span)
        o_ref[:, s] = (
            jnp.dot(hid[:, :ff], bd0[:, s], preferred_element_type=F32)
            + jnp.dot(hid[:, ff:], bd1[:, s], preferred_element_type=F32)
        ).astype(BF16)


def experts_apply(info, x, first, second, rows, top):
    width, ff = first[0].shape
    total = x.shape[0]
    weights = [pltpu.VMEM(w.shape, BF16) for w in first + second]
    return pl.pallas_call(
        partial(experts_kernel, rows=rows, top=top, tile=divisor(ff // 128, 2) * 128, span=divisor(width // 128, 4) * 128),
        out_shape=jax.ShapeDtypeStruct((total, width), BF16),
        grid_spec=pltpu.PrefetchScalarGridSpec(
            num_scalar_prefetch=1,
            grid=(1,),
            in_specs=[pl.BlockSpec(x.shape, lambda i, s: (0, 0))] + [pl.BlockSpec(memory_space=pl.ANY)] * 6,
            out_specs=pl.BlockSpec((total, width), lambda i, s: (0, 0)),
            scratch_shapes=weights
            + [pltpu.VMEM((total, ff), F32), pltpu.VMEM((total, 2 * ff), BF16), pltpu.SemaphoreType.DMA((6,))],
        ),
        compiler_params=pltpu.CompilerParams(vmem_limit_bytes=54 * MIB),
        cost_estimate=pl.CostEstimate(
            flops=12 * total * width * ff, bytes_accessed=12 * width * ff + 4 * total * width, transcendentals=2 * total * ff
        ),
    )(info, x, *first, *second)


def places(ids, plane_ids):
    chosen = jnp.any(ids[:, :, None, None] == plane_ids[None, None], axis=1)
    ones = chosen.astype(F32)
    tokens = ids.shape[0]
    before = (jnp.arange(tokens)[:, None] > jnp.arange(tokens)[None, :]).astype(F32)
    rank = jnp.einsum("ts,sjc->tjc", before, ones, preferred_element_type=F32)
    low_count = jnp.sum(ones[:, :, 0], axis=0)
    rank = rank + jnp.stack([jnp.zeros_like(low_count), low_count], axis=-1)[None]
    return jnp.where(chosen, rank, -1.0)


def after(value, *others):
    return lax.optimization_barrier((value,) + others)[0]


def local(tokens, router_weights, expert_ids, gate_weight, up_weight, down_weight):
    z_size = lax.axis_size("z")
    x_size = lax.axis_size("x")
    y_size = lax.axis_size("y")
    lane_count = z_size * x_size
    chips = y_size * x_size
    count, width = tokens.shape
    top = expert_ids.shape[1]
    rows = count * top // (y_size * lane_count)
    z_at = lax.axis_index("z")

    chip = jnp.arange(chips, dtype=jnp.int32)
    low = 2 * (chip // x_size) * lane_count + z_at * x_size + chip % x_size
    plane_ids = jnp.stack([low, low + lane_count], axis=-1).astype(F32)
    low_here = 2 * lax.axis_index("y") * lane_count + z_at * x_size + lax.axis_index("x")
    info = jnp.stack([low_here, low_here + lane_count, lax.axis_index("core")]).astype(jnp.int32)

    def flip(value, mask):
        return lax.ppermute(value, "z", [(i, i ^ mask) for i in range(z_size)])

    hi = router_weights.astype(BF16)
    mid = (router_weights - hi.astype(F32)).astype(BF16)
    block = jnp.concatenate(
        [tokens, expert_ids.astype(BF16), hi, mid, jnp.zeros((count, EXTRA - 3 * top), BF16)], axis=1
    )

    swap = [(0, 1), (1, 0)]
    own = [gate_weight[0], up_weight[0], down_weight[0]]
    other = [lax.ppermute(w, "core", swap) for w in own]

    row = jnp.arange(rows, dtype=jnp.int32).astype(F32)

    def routed(part):
        extra = part[:, width:].astype(F32)
        rank = places(extra[:, :top], plane_ids)
        hit = rank[:, :, :, None] == row
        taken = jnp.any(hit, axis=2).reshape(count, chips * rows).astype(BF16)
        same = extra[:, :top, None, None] == plane_ids[None, None]
        mixes = []
        for n in (1, 2):
            w_of = jnp.sum(jnp.where(same, extra[:, n * top : (n + 1) * top, None, None], 0.0), axis=1)
            mixes.append(jnp.sum(jnp.where(hit, w_of[..., None], 0.0), axis=2).reshape(count, chips * rows).astype(BF16))
        return taken, mixes

    def exchange(value):
        moved = lax.all_to_all(value.reshape(chips, rows, value.shape[1]), ("y", "x"), 0, 0, tiled=True)
        return moved.reshape(value.shape)

    def gather(part, taken):
        return lax.dot_general(taken, part, (((0,), (0,)), ((), ())), preferred_element_type=F32).astype(BF16)

    def run(k, *others):
        outs[k] = experts_apply(info, after(arrived[k], *others), own, other, rows, top)

    moving = {k: flip(block, k) for k in range(1, z_size) if k & (k - 1) == 0}
    held, mixes, sent, arrived, outs = {0: block}, {}, {}, {}, {}
    for k in range(z_size):
        if k:
            bit = k & -k
            held[k] = after(moving[k] if k == bit else flip(held[k ^ bit], bit), sent[k - 1])
        taken, mixes[k] = routed(held[k])
        sent[k] = gather(held[k], taken)
        if k:
            sent[k] = after(sent[k], arrived[k - 1], *[outs[o] for o in outs if o == k - 3])
        if k >= 2:
            run(k - 2, sent[k])
        arrived[k] = exchange(sent[k])
    last = z_size - 1
    run(last, *[outs[o] for o in outs if o == last - 2])
    if last:
        run(last - 1, outs[last])

    sums, back, backs = {}, None, {}
    for k in range(last, -1, -1):
        source = outs[k] if back is None else after(outs[k], back)
        if back is not None:
            backs[k + 1] = after(back, source)
        back = exchange(source)
    backs[0] = back
    for k in range(last, -1, -1):
        sums[k] = sum(jnp.dot(mix, backs[k], preferred_element_type=F32) for mix in mixes[k])
    mask = 1
    while mask < z_size:
        for o in sorted(sums, reverse=True):
            if o & mask:
                sums[o ^ mask] = sums[o ^ mask] + flip(sums.pop(o).astype(BF16), mask).astype(F32)
        mask *= 2
    return sums[0].astype(BF16)


def solution(mesh):
    groups, lanes = mesh.shape["dp"], mesh.shape["expert"]
    y_size = groups // 2
    x_size = y_size if lanes % y_size == 0 else 1
    fine = Mesh(mesh.devices.reshape(y_size, 2, lanes // x_size, x_size), ("y", "core", "z", "x"))
    split = ("y", "core", "z", "x")
    flat, deep = P(split, None), P(split, None, None)
    return jax.shard_map(
        local, mesh=fine, in_specs=(flat, flat, flat, deep, deep, deep), out_specs=flat, check_vma=False
    )
```

time: 440 us -> 319 us (0.72); the launches traced: 432 us -> 318 us
  matrix products: 169 us -> 26.5 us
  Pallas kernels: 0 us -> 80.1 us
  starting transfers between devices: 72.4 us -> 42.9 us
  other arithmetic: 18.8 us -> 7.18 us
  waiting for transfers between devices: 154 us -> 148 us
  local copies, waits for them, and re-layouts: 17.3 us -> 12.4 us
    dot_general x28 -> x12, matrix products: 168 us -> 26.1 us  [the longest x8 15.3 us: local(): jnp.dot(mix, backs[k], preferred_element_type=F32)]
    pallas_call x0 -> x4, Pallas kernels: none -> 80.1 us  [experts_apply(): pl.pallas_call(partial(experts_kernel, rows=rows, top=top, tile=divisor(f...]
    ppermute x15 -> x9, starting transfers between devices: 38.7 us -> 9.87 us  [the longest x6 8.91 us: flip(): return lax.ppermute(value, 'z', [(i, i ^ mask) for i in range(z_size)])]
    all_to_all x8, waiting for transfers between devices: 87 us -> 82 us  [exchange(): lax.all_to_all(value.reshape(chips, rows, value.shape[1]), ('y', 'x'), 0,...]
    ppermute x15 -> x9, waiting for transfers between devices: 66.6 us -> 66.3 us  [the longest x6 66.3 us: flip(): return lax.ppermute(value, 'z', [(i, i ^ mask) for i in range(z_size)])]
  transfers between devices with their start and end apart: 23 -> 17, of which waited for: 13 -> 12; matrix products, arithmetic and copies ran while one was open for 39% -> 12% of each run, Pallas kernels for 0% -> 19%
where the time goes in v2:
time: 319 us; the launch traced here: 318 us
  waiting for transfers between devices  148 us (46%)
  Pallas kernels  80.1 us (25%)
  starting transfers between devices  42.9 us (13%)
  matrix products  26.5 us (8%)
  local copies, waits for them, and re-layouts  12.4 us (4%)
  other arithmetic  7.18 us (2%)
    all_to_all x8, waiting for transfers between devices, exchange(): lax.all_to_all(value.reshape(chips, rows, value.shape[1]), ('y', 'x'), 0,...  82 us
    pallas_call x4, Pallas kernels, experts_apply(): pl.pallas_call(partial(experts_kernel, rows=rows, top=top, tile=divisor(f...  80.1 us
    ppermute x6, waiting for transfers between devices, flip(): return lax.ppermute(value, 'z', [(i, i ^ mask) for i in range(z_size)])  66.3 us
    all_to_all x8, starting transfers between devices, exchange(): lax.all_to_all(value.reshape(chips, rows, value.shape[1]), ('y', 'x'), 0,...  33 us
    dot_general x8, matrix products, local(): jnp.dot(mix, backs[k], preferred_element_type=F32)  15.3 us
    dot_general x4, matrix products, gather(): lax.dot_general(taken, part, (((0,), (0,)), ((), ())), preferred_element_...  10.8 us
    ppermute x6, starting transfers between devices, flip(): return lax.ppermute(value, 'z', [(i, i ^ mask) for i in range(z_size)])  8.91 us
  transfers between devices with their start and end apart: 17, of which 12 were waited for; matrix products, arithmetic and copies ran while one was open for 12% of the time, Pallas kernels for 19%

profile of v2, /device:TPU:0, one launch (start us, length us, event | category | flops | bytes accessed | tf_op | source)
XLA Modules:
  0.0 317.7 jit_solution(4888141381642671096)
XLA Ops:
  1.7 0.8 subtract_convert_fusion
  2.8 2.3 concatenate.11
  5.1 2.6 collective-permute-start.1
  8.6 2.0 convolution_convert_fusion.3
  10.6 3.7 %all-to-all-start = ((bf16[4,64,4224]{2,1,0:T(8,128)(2,1)}), bf16[4,64,4224]{2,1,0:T(8,128)(2,1)S(1)}, u32[]{:S(2)}, u32[]{:S(2)}) async-start(bf16[4,64,4224]{2,1,0:T(8,128)(2,1)} %bitcast.94), calls=%async_computation | async-start | bytes 4325376 | tf_op jit(solution)/shard_map/all_to_all | solution.py:155
  14.3 2.6 collective-permute-start
  16.9 31.9 %collective-permute-done.1 = bf16[128,4224]{1,0:T(8,128)(2,1)} collective-permute-done((bf16[128,4224]{1,0:T(8,128)(2,1)S(1)}, bf16[128,4224]{1,0:T(8,128)(2,1)}, u32[]{:S(2)}, u32[]{:S(2)}) %collective-permute-start.1) | collective-permute-done | bytes 1081376 | tf_op jit(solution)/shard_map/ppermute | solution.py:128
  50.2 0.9 copy.38
  51.6 3.3 %convolution_convert_fusion.2 = bf16[256,4224]{1,0:T(8,128)(2,1)} fusion(pred[128,256]{0,1:T(8,128)(4,1)S(1)} %bitcast.106, bf16[128,4224]{1,0:T(8,128)(2,1)} %collective-permute-done.1), kind=kOutput, calls=%fused_computation.2 | convolution fusion | flops 277905408 | bytes 3276800 | tf_op jit(solution)/shard_map/dot_general | solution.py:159
  54.9 1.3 copy-done.2
  56.3 4.5 %all-to-all-start.1 = ((bf16[4,64,4224]{2,1,0:T(8,128)(2,1)}), bf16[4,64,4224]{2,1,0:T(8,128)(2,1)}, u32[]{:S(2)}, u32[]{:S(2)}) async-start(bf16[4,64,4224]{2,1,0:T(8,128)(2,1)} %bitcast.92), calls=%async_computation.1 | async-start | bytes 4325376 | tf_op jit(solution)/shard_map/all_to_all | solution.py:155
  61.4 3.1 collective-permute-done
  64.5 0.8 slice_convert_fusion.1
  66.7 3.3 %convolution_convert_fusion.1 = bf16[256,4224]{1,0:T(8,128)(2,1)} fusion(pred[128,256]{0,1:T(8,128)(4,1)S(1)} %bitcast.109, bf16[128,4224]{1,0:T(8,128)(2,1)} %collective-permute-done), kind=kOutput, calls=%fused_computation.1 | convolution fusion | flops 277905408 | bytes 3276800 | tf_op jit(solution)/shard_map/dot_general | solution.py:159
  70.0 16.8 %all-to-all-done.1 = bf16[4,64,4224]{2,1,0:T(8,128)(2,1)} async-done(((bf16[4,64,4224]{2,1,0:T(8,128)(2,1)}), bf16[4,64,4224]{2,1,0:T(8,128)(2,1)}, u32[]{:S(2)}, u32[]{:S(2)}) %all-to-all-start.1) | async-done | bytes 2162720 | tf_op jit(solution)/shard_map/all_to_all | solution.py:155
  86.8 3.1 collective-permute-done.5
  89.9 3.6 %all-to-all-start.2 = ((bf16[4,64,4224]{2,1,0:T(8,128)(2,1)}), bf16[4,64,4224]{2,1,0:T(8,128)(2,1)S(1)}, u32[]{:S(2)}, u32[]{:S(2)}) async-start(bf16[4,64,4224]{2,1,0:T(8,128)(2,1)} %bitcast.93), calls=%async_computation.2 | async-start | bytes 4325376 | tf_op jit(solution)/shard_map/all_to_all | solution.py:155
  94.3 0.9 copy.46
  95.7 2.1 convolution_convert_fusion
  97.8 20.0 %shard_map.64 = bf16[256,4096]{1,0:T(8,128)(2,1)} custom-call(s32[3]{0:T(128)} %pad_add_fusion.info, bf16[256,4224]{1,0:T(8,128)(2,1)} %bitcast.90, bf16[4096,768]{1,0:T(8,128)(2,1)} %bitcast.72, bf16[4096,768]{1,0:T(8,128)(2,1)} %bitcast.77, bf16[768,4096]{1,0:T(8,128)(2,1)} %bitcast.82, bf16[4096,768]{1,0:T(8,128)(2,1)} %collective-permute-done.2.g1, ...), custom_call_target="tpu_custom_call" | custom-call | flops 9663676416 | bytes 41943040 | tf_op jit(solution)/shard_map/pallas_call | solution.py:77
  118.0 1.3 copy-done.3
  119.3 4.7 %all-to-all-start.3 = ((bf16[4,64,4224]{2,1,0:T(8,128)(2,1)}), bf16[4,64,4224]{2,1,0:T(8,128)(2,1)}, u32[]{:S(2)}, u32[]{:S(2)}) async-start(bf16[4,64,4224]{2,1,0:T(8,128)(2,1)} %bitcast.95), calls=%async_computation.3 | async-start | bytes 4325376 | tf_op jit(solution)/shard_map/all_to_all | solution.py:155
  124.0 20.0 %shard_map.65 = bf16[256,4096]{1,0:T(8,128)(2,1)} custom-call(s32[3]{0:T(128)} %pad_add_fusion.info, bf16[256,4224]{1,0:T(8,128)(2,1)} %bitcast.13.x_ref, bf16[4096,768]{1,0:T(8,128)(2,1)} %bitcast.73, bf16[4096,768]{1,0:T(8,128)(2,1)} %bitcast.78, bf16[768,4096]{1,0:T(8,128)(2,1)} %bitcast.83, bf16[4096,768]{1,0:T(8,128)(2,1)} %collective-permute-done.2.g1, ...), custom_call_target="tpu_custom_call" | custom-call | flops 9663676416 | bytes 41943040 | tf_op jit(solution)/shard_map/pallas_call | solution.py:77
  144.0 4.9 %all-to-all-done.3 = bf16[4,64,4224]{2,1,0:T(8,128)(2,1)} async-done(((bf16[4,64,4224]{2,1,0:T(8,128)(2,1)}), bf16[4,64,4224]{2,1,0:T(8,128)(2,1)}, u32[]{:S(2)}, u32[]{:S(2)}) %all-to-all-start.3) | async-done | bytes 2162720 | tf_op jit(solution)/shard_map/all_to_all | solution.py:155
  148.9 20.0 %shard_map.66 = bf16[256,4096]{1,0:T(8,128)(2,1)} custom-call(s32[3]{0:T(128)} %pad_add_fusion.info, bf16[256,4224]{1,0:T(8,128)(2,1)} %bitcast.22.x_ref, bf16[4096,768]{1,0:T(8,128)(2,1)} %bitcast.74, bf16[4096,768]{1,0:T(8,128)(2,1)} %bitcast.79, bf16[768,4096]{1,0:T(8,128)(2,1)} %bitcast.84, bf16[4096,768]{1,0:T(8,128)(2,1)} %collective-permute-done.2.g1, ...), custom_call_target="tpu_custom_call" | custom-call | flops 9663676416 | bytes 41943040 | tf_op jit(solution)/shard_map/pallas_call | solution.py:77
  168.9 3.6 %all-to-all-start.4 = ((bf16[4,64,4096]{2,1,0:T(8,128)(2,1)}), bf16[4,64,4096]{2,1,0:T(8,128)(2,1)S(1)}, u32[]{:S(2)}, u32[]{:S(2)}) async-start(bf16[4,64,4096]{2,1,0:T(8,128)(2,1)} %bitcast.99), calls=%async_computation.4 | async-start | bytes 4194304 | tf_op jit(solution)/shard_map/all_to_all | solution.py:155
  172.5 20.0 %shard_map.67 = bf16[256,4096]{1,0:T(8,128)(2,1)} custom-call(s32[3]{0:T(128)} %pad_add_fusion.info, bf16[256,4224]{1,0:T(8,128)(2,1)} %bitcast.91, bf16[4096,768]{1,0:T(8,128)(2,1)} %bitcast.75, bf16[4096,768]{1,0:T(8,128)(2,1)} %bitcast.80, bf16[768,4096]{1,0:T(8,128)(2,1)} %bitcast.85, bf16[4096,768]{1,0:T(8,128)(2,1)} %collective-permute-done.2.g1, ...), custom_call_target="tpu_custom_call" | custom-call | flops 9663676416 | bytes 41943040 | tf_op jit(solution)/shard_map/pallas_call | solution.py:77
  192.5 4.3 %all-to-all-done.4 = bf16[4,64,4096]{2,1,0:T(8,128)(2,1)S(1)} async-done(((bf16[4,64,4096]{2,1,0:T(8,128)(2,1)}), bf16[4,64,4096]{2,1,0:T(8,128)(2,1)S(1)}, u32[]{:S(2)}, u32[]{:S(2)}) %all-to-all-start.4) | async-done | bytes 2097184 | tf_op jit(solution)/shard_map/all_to_all | solution.py:155
  196.9 1.3 copy-done
  198.2 3.6 %all-to-all-start.5 = ((bf16[4,64,4096]{2,1,0:T(8,128)(2,1)}), bf16[4,64,4096]{2,1,0:T(8,128)(2,1)S(1)}, u32[]{:S(2)}, u32[]{:S(2)}) async-start(bf16[4,64,4096]{2,1,0:T(8,128)(2,1)} %bitcast.98), calls=%async_computation.5 | async-start | bytes 4194304 | tf_op jit(solution)/shard_map/all_to_all | solution.py:155
  202.3 23.7 %all-to-all-done.5 = bf16[4,64,4096]{2,1,0:T(8,128)(2,1)S(1)} async-done(((bf16[4,64,4096]{2,1,0:T(8,128)(2,1)}), bf16[4,64,4096]{2,1,0:T(8,128)(2,1)S(1)}, u32[]{:S(2)}, u32[]{:S(2)}) %all-to-all-start.5) | async-done | bytes 2097184 | tf_op jit(solution)/shard_map/all_to_all | solution.py:155
  226.1 4.6 %all-to-all-start.6 = ((bf16[4,64,4096]{2,1,0:T(8,128)(2,1)}), bf16[4,64,4096]{2,1,0:T(8,128)(2,1)}, u32[]{:S(2)}, u32[]{:S(2)}) async-start(bf16[4,64,4096]{2,1,0:T(8,128)(2,1)} %bitcast.97), calls=%async_computation.6 | async-start | bytes 4194304 | tf_op jit(solution)/shard_map/all_to_all | solution.py:155
  231.2 2.2 fusion.54
  233.4 1.5 fusion.2
  235.4 19.6 %all-to-all-done.6 = bf16[4,64,4096]{2,1,0:T(8,128)(2,1)} async-done(((bf16[4,64,4096]{2,1,0:T(8,128)(2,1)}), bf16[4,64,4096]{2,1,0:T(8,128)(2,1)}, u32[]{:S(2)}, u32[]{:S(2)}) %all-to-all-start.6) | async-done | bytes 2097184 | tf_op jit(solution)/shard_map/all_to_all | solution.py:155
  255.0 4.7 %all-to-all-start.7 = ((bf16[4,64,4096]{2,1,0:T(8,128)(2,1)}), bf16[4,64,4096]{2,1,0:T(8,128)(2,1)}, u32[]{:S(2)}, u32[]{:S(2)}) async-start(bf16[4,64,4096]{2,1,0:T(8,128)(2,1)} %bitcast.96), calls=%async_computation.7 | async-start | bytes 4194304 | tf_op jit(solution)/shard_map/all_to_all | solution.py:155
  260.3 1.0 copy-done.4
  261.2 1.9 add_convert_fusion.1
  263.1 1.7 collective-permute-start.8
  264.8 2.1 fusion.52
  266.8 3.1 fusion.1
  269.9 1.4 collective-permute-start.6
  271.4 12.6 %all-to-all-done.7 = bf16[4,64,4096]{2,1,0:T(8,128)(2,1)} async-done(((bf16[4,64,4096]{2,1,0:T(8,128)(2,1)}), bf16[4,64,4096]{2,1,0:T(8,128)(2,1)}, u32[]{:S(2)}, u32[]{:S(2)}) %all-to-all-start.7) | async-done | bytes 2097184 | tf_op jit(solution)/shard_map/all_to_all | solution.py:155
  283.9 2.1 convolution_bitcast_fusion
  286.0 2.1 fusion
  288.1 22.6 %collective-permute-done.8 = bf16[128,4096]{1,0:T(8,128)(2,1)S(1)} collective-permute-done((bf16[128,4096]{1,0:T(8,128)(2,1)S(1)}, bf16[128,4096]{1,0:T(8,128)(2,1)S(1)}, u32[]{:S(2)}, u32[]{:S(2)}) %collective-permute-start.8) | collective-permute-done | bytes 1048608 | tf_op jit(solution)/shard_map/ppermute | solution.py:128
  310.7 5.6 %collective-permute-done.6 = bf16[128,4096]{1,0:T(8,128)(2,1)S(1)} collective-permute-done((bf16[128,4096]{1,0:T(8,128)(2,1)}, bf16[128,4096]{1,0:T(8,128)(2,1)S(1)}, u32[]{:S(2)}, u32[]{:S(2)}) %collective-permute-start.6) | collective-permute-done | bytes 1048608 | tf_op jit(solution)/shard_map/ppermute | solution.py:128
  316.3 1.4 add_convert_fusion
  (82 shorter events, 10.3 us)
Async XLA Ops:
  0.0 97.8 %collective-permute-start.2 = (bf16[4096,768]{1,0:T(8,128)(2,1)}, bf16[4096,768]{1,0:T(8,128)(2,1)}, u32[]{:S(2)}, u32[]{:S(2)}) collective-permute-start(bf16[4096,768]{1,0:T(8,128)(2,1)} %bitcast.71), channel_id=1, source_target_pairs={{0,8},{8,0},{1,9},{9,1},{2,10},{10,2},{3,11},{11,3},{4,12},{12,4},... | collective-permute-start | bytes 18874376 | tf_op jit(solution)/shard_map/ppermute | solution.py:138
  0.5 97.3 %collective-permute-start.3 = (bf16[4096,768]{1,0:T(8,128)(2,1)}, bf16[4096,768]{1,0:T(8,128)(2,1)}, u32[]{:S(2)}, u32[]{:S(2)}) collective-permute-start(bf16[4096,768]{1,0:T(8,128)(2,1)} %bitcast.76), channel_id=1, source_target_pairs={{0,8},{8,0},{1,9},{9,1},{2,10},{10,2},{3,11},{11,3},{4,12},{12,4},... | collective-permute-start | bytes 18874376 | tf_op jit(solution)/shard_map/ppermute | solution.py:138
  0.5 97.3 %collective-permute-start.4 = (bf16[768,4096]{1,0:T(8,128)(2,1)}, bf16[768,4096]{1,0:T(8,128)(2,1)}, u32[]{:S(2)}, u32[]{:S(2)}) collective-permute-start(bf16[768,4096]{1,0:T(8,128)(2,1)} %bitcast.81), channel_id=1, source_target_pairs={{0,8},{8,0},{1,9},{9,1},{2,10},{10,2},{3,11},{11,3},{4,12},{12,4},... | collective-permute-start | bytes 18874376 | tf_op jit(solution)/shard_map/ppermute | solution.py:138
  5.1 43.7 %collective-permute-start.1 = (bf16[128,4224]{1,0:T(8,128)(2,1)S(1)}, bf16[128,4224]{1,0:T(8,128)(2,1)}, u32[]{:S(2)}, u32[]{:S(2)}) collective-permute-start(bf16[128,4224]{1,0:T(8,128)(2,1)S(1)} %concatenate.11), channel_id=1, source_target_pairs={{0,2},{2,0},{4,6},{6,4},{1,3},{3,1},{5,7},{7,5},{8,10},{10,8},{12,... | collective-permute-start | bytes 3244040 | tf_op jit(solution)/shard_map/ppermute | solution.py:128
  8.4 87.1 %copy-start.9 = (f32[64]{0:T(128)}, f32[64]{0:T(128)S(1)}, u32[]{:S(2)}) copy-start(f32[64]{0:T(128)S(1)} %iota_convert_fusion) | copy-start | bytes 772
  10.6 44.3 %all-to-all-start = ((bf16[4,64,4224]{2,1,0:T(8,128)(2,1)}), bf16[4,64,4224]{2,1,0:T(8,128)(2,1)S(1)}, u32[]{:S(2)}, u32[]{:S(2)}) async-start(bf16[4,64,4224]{2,1,0:T(8,128)(2,1)} %bitcast.94), calls=%async_computation | async-start | bytes 4325376 | tf_op jit(solution)/shard_map/all_to_all | solution.py:155
  14.3 50.2 %collective-permute-start = (bf16[128,4224]{1,0:T(8,128)(2,1)S(1)}, bf16[128,4224]{1,0:T(8,128)(2,1)}, u32[]{:S(2)}, u32[]{:S(2)}) collective-permute-start(bf16[128,4224]{1,0:T(8,128)(2,1)S(1)} %concatenate.11), channel_id=1, source_target_pairs={{0,4},{2,6},{4,0},{6,2},{1,5},{3,7},{5,1},{7,3},{8,12},{10,14},{12... | collective-permute-start | bytes 3244040 | tf_op jit(solution)/shard_map/ppermute | solution.py:128
  54.9 1.3 copy-start.2
  56.3 30.5 %all-to-all-start.1 = ((bf16[4,64,4224]{2,1,0:T(8,128)(2,1)}), bf16[4,64,4224]{2,1,0:T(8,128)(2,1)}, u32[]{:S(2)}, u32[]{:S(2)}) async-start(bf16[4,64,4224]{2,1,0:T(8,128)(2,1)} %bitcast.92), calls=%async_computation.1 | async-start | bytes 4325376 | tf_op jit(solution)/shard_map/all_to_all | solution.py:155
  64.5 25.4 %collective-permute-start.5 = (bf16[128,4224]{1,0:T(8,128)(2,1)}, bf16[128,4224]{1,0:T(8,128)(2,1)S(1)}, u32[]{:S(2)}, u32[]{:S(2)}) collective-permute-start(bf16[128,4224]{1,0:T(8,128)(2,1)} %collective-permute-done), channel_id=1, source_target_pairs={{0,2},{2,0},{4,6},{6,4},{1,3},{3,1},{5,7},{7,5},{8,10},{10,8},{12,... | collective-permute-start | bytes 3244040 | tf_op jit(solution)/shard_map/ppermute | solution.py:128
  89.9 28.1 %all-to-all-start.2 = ((bf16[4,64,4224]{2,1,0:T(8,128)(2,1)}), bf16[4,64,4224]{2,1,0:T(8,128)(2,1)S(1)}, u32[]{:S(2)}, u32[]{:S(2)}) async-start(bf16[4,64,4224]{2,1,0:T(8,128)(2,1)} %bitcast.93), calls=%async_computation.2 | async-start | bytes 4325376 | tf_op jit(solution)/shard_map/all_to_all | solution.py:155
  117.9 1.3 copy-start.3
  119.3 29.6 %all-to-all-start.3 = ((bf16[4,64,4224]{2,1,0:T(8,128)(2,1)}), bf16[4,64,4224]{2,1,0:T(8,128)(2,1)}, u32[]{:S(2)}, u32[]{:S(2)}) async-start(bf16[4,64,4224]{2,1,0:T(8,128)(2,1)} %bitcast.95), calls=%async_computation.3 | async-start | bytes 4325376 | tf_op jit(solution)/shard_map/all_to_all | solution.py:155
  168.9 27.9 %all-to-all-start.4 = ((bf16[4,64,4096]{2,1,0:T(8,128)(2,1)}), bf16[4,64,4096]{2,1,0:T(8,128)(2,1)S(1)}, u32[]{:S(2)}, u32[]{:S(2)}) async-start(bf16[4,64,4096]{2,1,0:T(8,128)(2,1)} %bitcast.99), calls=%async_computation.4 | async-start | bytes 4194304 | tf_op jit(solution)/shard_map/all_to_all | solution.py:155
  196.8 1.3 copy-start
  196.8 5.2 %copy-start.6 = (f32[128,8]{1,0:T(8,128)S(1)}, f32[128,8]{1,0:T(8,128)}, u32[]{:S(2)}) copy-start(f32[128,8]{1,0:T(8,128)} %get-tuple-element.70) | copy-start | bytes 12292
  196.8 5.3 %copy-start.5 = (f32[128,8]{1,0:T(8,128)S(1)}, f32[128,8]{1,0:T(8,128)}, u32[]{:S(2)}) copy-start(f32[128,8]{1,0:T(8,128)} %get-tuple-element.71) | copy-start | bytes 12292
  196.8 5.3 %copy-start.8 = (f32[128,8]{1,0:T(8,128)S(1)}, f32[128,8]{1,0:T(8,128)}, u32[]{:S(2)}) copy-start(f32[128,8]{1,0:T(8,128)} %get-tuple-element.73) | copy-start | bytes 12292
  196.8 5.4 %copy-start.7 = (f32[128,8]{1,0:T(8,128)S(1)}, f32[128,8]{1,0:T(8,128)}, u32[]{:S(2)}) copy-start(f32[128,8]{1,0:T(8,128)} %get-tuple-element.74) | copy-start | bytes 12292
  198.2 27.9 %all-to-all-start.5 = ((bf16[4,64,4096]{2,1,0:T(8,128)(2,1)}), bf16[4,64,4096]{2,1,0:T(8,128)(2,1)S(1)}, u32[]{:S(2)}, u32[]{:S(2)}) async-start(bf16[4,64,4096]{2,1,0:T(8,128)(2,1)} %bitcast.98), calls=%async_computation.5 | async-start | bytes 4194304 | tf_op jit(solution)/shard_map/all_to_all | solution.py:155
  226.1 4.8 %copy-start.10 = (f32[64]{0:T(128)S(1)}, f32[64]{0:T(128)}, u32[]{:S(2)}) copy-start(f32[64]{0:T(128)} %copy-done.9) | copy-start | bytes 772
  226.1 29.0 %all-to-all-start.6 = ((bf16[4,64,4096]{2,1,0:T(8,128)(2,1)}), bf16[4,64,4096]{2,1,0:T(8,128)(2,1)}, u32[]{:S(2)}, u32[]{:S(2)}) async-start(bf16[4,64,4096]{2,1,0:T(8,128)(2,1)} %bitcast.97), calls=%async_computation.6 | async-start | bytes 4194304 | tf_op jit(solution)/shard_map/all_to_all | solution.py:155
  231.1 2.2 copy-start.1
  234.8 25.4 %collective-permute-start.7 = (bf16[128,4096]{1,0:T(8,128)(2,1)}, bf16[128,4096]{1,0:T(8,128)(2,1)S(1)}, u32[]{:S(2)}, u32[]{:S(2)}) collective-permute-start(bf16[128,4096]{1,0:T(8,128)(2,1)} %fusion.2), channel_id=1, source_target_pairs={{0,2},{2,0},{4,6},{6,4},{1,3},{3,1},{5,7},{7,5},{8,10},{10,8},{12,... | collective-permute-start | bytes 3145736 | tf_op jit(solution)/shard_map/ppermute | solution.py:128
  255.0 28.9 %all-to-all-start.7 = ((bf16[4,64,4096]{2,1,0:T(8,128)(2,1)}), bf16[4,64,4096]{2,1,0:T(8,128)(2,1)}, u32[]{:S(2)}, u32[]{:S(2)}) async-start(bf16[4,64,4096]{2,1,0:T(8,128)(2,1)} %bitcast.96), calls=%async_computation.7 | async-start | bytes 4194304 | tf_op jit(solution)/shard_map/all_to_all | solution.py:155
  260.2 1.0 copy-start.4
  263.1 47.6 %collective-permute-start.8 = (bf16[128,4096]{1,0:T(8,128)(2,1)S(1)}, bf16[128,4096]{1,0:T(8,128)(2,1)S(1)}, u32[]{:S(2)}, u32[]{:S(2)}) collective-permute-start(bf16[128,4096]{1,0:T(8,128)(2,1)S(1)} %add_convert_fusion.1), channel_id=1, source_target_pairs={{0,4},{2,6},{4,0},{6,2},{1,5},{3,7},{5,1},{7,3},{8,12},{10,14},{12... | collective-permute-start | bytes 3145736 | tf_op jit(solution)/shard_map/ppermute | solution.py:128
  269.9 46.4 %collective-permute-start.6 = (bf16[128,4096]{1,0:T(8,128)(2,1)}, bf16[128,4096]{1,0:T(8,128)(2,1)S(1)}, u32[]{:S(2)}, u32[]{:S(2)}) collective-permute-start(bf16[128,4096]{1,0:T(8,128)(2,1)} %fusion.1), channel_id=1, source_target_pairs={{0,2},{2,0},{4,6},{6,4},{1,3},{3,1},{5,7},{7,5},{8,10},{10,8},{12,... | collective-permute-start | bytes 3145736 | tf_op jit(solution)/shard_map/ppermute | solution.py:128

commit v3 on v2

--- a/solution.py
+++ b/solution.py
@@ -17,13 +17,25 @@
     return next(d for d in range(min(size, most), 0, -1) if size % d == 0)
 
 
-def experts_kernel(info, x_ref, g0, u0, d0, g1, u1, d1, o_ref, bg0, bu0, bd0, bg1, bu1, bd1, gate_ref, hid, sems, *, rows, top, tile, span):
+def experts_kernel(
+    info, x_hbm, g0, u0, d0, g1, u1, d1, o_hbm, x_ref, bg0, bu0, bd0, bg1, bu1, bd1, gate_ref, hid, o_ref, sems, out_sems,
+    *, rows, top, tile, span
+):
     total, width = o_ref.shape
     ff = g0.shape[1]
-    pairs = ((g0, bg0), (u0, bu0), (g1, bg1), (u1, bu1), (d0, bd0), (d1, bd1))
-    copies = [pltpu.make_async_copy(src, dst, sems.at[n]) for n, (src, dst) in enumerate(pairs)]
-    for c in copies:
+    spans = width // span
+    x_copy = pltpu.make_async_copy(x_hbm, x_ref, sems.at[0])
+    x_copy.start()
+    ins = [pltpu.make_async_copy(src, dst, sems.at[1 + n]) for n, (src, dst) in enumerate(((g0, bg0), (u0, bu0), (g1, bg1), (u1, bu1)))]
+    for c in ins:
         c.start()
+    downs = []
+    for n in range(spans):
+        s = pl.ds(n * span, span)
+        for m, (src, dst) in enumerate(((d0, bd0), (d1, bd1))):
+            downs.append(pltpu.make_async_copy(src.at[:, s], dst.at[:, s], sems.at[5 + 2 * n + m]))
+            downs[-1].start()
+    x_copy.wait()
 
     ids = x_ref[:, width:].astype(F32)
     is_id = lax.broadcasted_iota(jnp.int32, ids.shape, 1) < top
@@ -41,14 +53,14 @@
 
     for which, (bg, bu) in enumerate(((bg0, bu0), (bg1, bu1))):
         keep = first if which == 0 else 1.0 - first
-        copies[2 * which].wait()
+        ins[2 * which].wait()
 
         @pl.loop(0, ff // tile)
         def _(t):
             s = pl.ds(pl.multiple_of(t * tile, tile), tile)
             gate_ref[:, s] = jnp.dot(x_ref[:, :width], bg[:, s], preferred_element_type=F32)
 
-        copies[2 * which + 1].wait()
+        ins[2 * which + 1].wait()
 
         @pl.loop(0, ff // tile)
         def _(t):
@@ -58,32 +70,39 @@
             h = jnp.where(keep > 0.5, gate / (1.0 + jnp.exp(-gate)) * up, 0.0)
             hid[:, pl.ds(pl.multiple_of(which * ff + t * tile, tile), tile)] = h.astype(BF16)
 
-    copies[4].wait()
-    copies[5].wait()
-
-    @pl.loop(0, width // span)
-    def _(n):
-        s = pl.ds(pl.multiple_of(n * span, span), span)
+    outs = []
+    for n in range(spans):
+        downs[2 * n].wait()
+        downs[2 * n + 1].wait()
+        s = pl.ds(n * span, span)
         o_ref[:, s] = (
             jnp.dot(hid[:, :ff], bd0[:, s], preferred_element_type=F32)
             + jnp.dot(hid[:, ff:], bd1[:, s], preferred_element_type=F32)
         ).astype(BF16)
+        outs.append(pltpu.make_async_copy(o_ref.at[:, s], o_hbm.at[:, s], out_sems.at[n]))
+        outs[-1].start()
+    for c in outs:
+        c.wait()
 
 
 def experts_apply(info, x, first, second, rows, top):
     width, ff = first[0].shape
     total = x.shape[0]
-    weights = [pltpu.VMEM(w.shape, BF16) for w in first + second]
+    span = divisor(width // 128, 8) * 128
+    spans = width // span
+    anywhere = pl.BlockSpec(memory_space=pl.ANY)
     return pl.pallas_call(
-        partial(experts_kernel, rows=rows, top=top, tile=divisor(ff // 128, 2) * 128, span=divisor(width // 128, 4) * 128),
+        partial(experts_kernel, rows=rows, top=top, tile=divisor(ff // 128, 2) * 128, span=span),
         out_shape=jax.ShapeDtypeStruct((total, width), BF16),
         grid_spec=pltpu.PrefetchScalarGridSpec(
             num_scalar_prefetch=1,
             grid=(1,),
-            in_specs=[pl.BlockSpec(x.shape, lambda i, s: (0, 0))] + [pl.BlockSpec(memory_space=pl.ANY)] * 6,
-            out_specs=pl.BlockSpec((total, width), lambda i, s: (0, 0)),
-            scratch_shapes=weights
-            + [pltpu.VMEM((total, ff), F32), pltpu.VMEM((total, 2 * ff), BF16), pltpu.SemaphoreType.DMA((6,))],
+            in_specs=[anywhere] * 7,
+            out_specs=anywhere,
+            scratch_shapes=[pltpu.VMEM(x.shape, BF16)]
+            + [pltpu.VMEM(w.shape, BF16) for w in first + second]
+            + [pltpu.VMEM((total, ff), F32), pltpu.VMEM((total, 2 * ff), BF16), pltpu.VMEM((total, width), BF16)]
+            + [pltpu.SemaphoreType.DMA((5 + 2 * spans,)), pltpu.SemaphoreType.DMA((spans,))],
         ),
         compiler_params=pltpu.CompilerParams(vmem_limit_bytes=54 * MIB),
         cost_estimate=pl.CostEstimate(
@@ -126,6 +145,17 @@
 
     def flip(value, mask):
         return lax.ppermute(value, "z", [(i, i ^ mask) for i in range(z_size)])
+
+    def inner(value):
+        return lax.ppermute(value, "z", [(1, 2), (2, 1)])
+
+    def outward(value):
+        return lax.ppermute(value, "z", [(1, 0), (2, 3)])
+
+    def inward(value):
+        return lax.ppermute(value, "z", [(0, 1), (3, 2)])
+
+    is_end = (z_at == 0) | (z_at == z_size - 1)
 
     hi = router_weights.astype(BF16)
     mid = (router_weights - hi.astype(F32)).astype(BF16)
@@ -161,40 +191,61 @@
     def run(k, *others):
         outs[k] = experts_apply(info, after(arrived[k], *others), own, other, rows, top)
 
-    moving = {k: flip(block, k) for k in range(1, z_size) if k & (k - 1) == 0}
+    line = z_size == 4
+    moving = {k: flip(block, k) for k in ((1,) if line else range(1, z_size)) if k & (k - 1) == 0}
+    if line:
+        middle = inner(block)
     held, mixes, sent, arrived, outs = {0: block}, {}, {}, {}, {}
     for k in range(z_size):
-        if k:
+        if k and line:
+            if k == 1:
+                held[1] = after(moving[1], sent[0])
+                next_inner, next_outer = inner(held[1]), outward(after(middle, sent[0]))
+            elif k == 2:
+                passed = after(next_inner, sent[1])
+                last_outer = outward(passed)
+                held[2] = jnp.where(is_end, next_outer, passed)
+            else:
+                held[3] = jnp.where(is_end, after(last_outer, outs[0]), middle)
+        elif k:
             bit = k & -k
             held[k] = after(moving[k] if k == bit else flip(held[k ^ bit], bit), sent[k - 1])
         taken, mixes[k] = routed(held[k])
         sent[k] = gather(held[k], taken)
         if k:
-            sent[k] = after(sent[k], arrived[k - 1], *[outs[o] for o in outs if o == k - 3])
-        if k >= 2:
+            sent[k] = after(sent[k], arrived[k - 1])
+        if k > 1:
             run(k - 2, sent[k])
         arrived[k] = exchange(sent[k])
     last = z_size - 1
-    run(last, *[outs[o] for o in outs if o == last - 2])
-    if last:
-        run(last - 1, outs[last])
-
-    sums, back, backs = {}, None, {}
+    run(last, *[outs[o] for o in outs])
+    def mixed(k, arrived_back):
+        return sum(jnp.dot(mix, arrived_back, preferred_element_type=F32) for mix in mixes[k])
+
+    back, hold, extra = None, [], []
     for k in range(last, -1, -1):
-        source = outs[k] if back is None else after(outs[k], back)
-        if back is not None:
-            backs[k + 1] = after(back, source)
+        source = outs[k] if k == last else after(outs[k], back, *hold)
+        if k < last:
+            total, done = mixed(k + 1, after(back, source)), k + 1
+            if not line:
+                bit = done & -done
+                total = sum((r for o, r in extra if o == done), total).astype(BF16)
+                extra.append((done ^ bit, flip(total, bit).astype(F32)))
+                hold = [total]
+            elif done == 3:
+                third = total
+                hold = [total.astype(BF16)]
+                from_end = inward(hold[0])
+            elif done == 2:
+                hold = [total.astype(BF16), (total + from_end.astype(F32)).astype(BF16)]
+                near, far = inward(hold[0]), inner(hold[1])
+            else:
+                hold = [(total + far.astype(F32)).astype(BF16), (third + near.astype(F32)).astype(BF16)]
+                extra += [(0, flip(hold[0], 1).astype(F32)), (0, inner(hold[1]).astype(F32))]
+        if k and k - 1 not in outs:
+            run(k - 1, source, *hold)
         back = exchange(source)
-    backs[0] = back
-    for k in range(last, -1, -1):
-        sums[k] = sum(jnp.dot(mix, backs[k], preferred_element_type=F32) for mix in mixes[k])
-    mask = 1
-    while mask < z_size:
-        for o in sorted(sums, reverse=True):
-            if o & mask:
-                sums[o ^ mask] = sums[o ^ mask] + flip(sums.pop(o).astype(BF16), mask).astype(F32)
-        mask *= 2
-    return sums[0].astype(BF16)
+    return sum((r for o, r in extra if o == 0), mixed(0, back)).astype(BF16)
 
 
 def solution(mesh):

time: 319 us -> 288 us (0.903)
  waiting for transfers between devices: 148 us -> 109 us
  starting transfers between devices: 42.9 us -> 59.6 us
  Pallas kernels: 80.1 us -> 70.8 us
  other arithmetic: 7.18 us -> 13.7 us
  matrix products: 26.5 us -> 22.8 us
    ppermute x6 -> x2, waiting for transfers between devices: 66.3 us -> 15.6 us  [flip(): return lax.ppermute(value, 'z', [(i, i ^ mask) for i in range(z_size)])]
    ppermute x0 -> x8, waiting for transfers between devices: none -> 33.8 us  [the longest x2 20.7 us: inward(): return lax.ppermute(value, 'z', [(0, 1), (3, 2)])]
    all_to_all x8, waiting for transfers between devices: 82 us -> 59.1 us  [exchange(): lax.all_to_all(value.reshape(chips, rows, value.shape[1]), ('y', 'x'), 0,...]
    ppermute x0 -> x8, starting transfers between devices: none -> 21.5 us  [the longest x2 14.1 us: inward(): return lax.ppermute(value, 'z', [(0, 1), (3, 2)])]
    pallas_call x4, Pallas kernels: 80.1 us -> 70.8 us  [experts_apply(): pl.pallas_call(partial(experts_kernel, rows=rows, top=top, tile=divisor(f...]
    ppermute x6 -> x2, starting transfers between devices: 8.91 us -> 3.84 us  [flip(): return lax.ppermute(value, 'z', [(i, i ^ mask) for i in range(z_size)])]
    convert_element_type x1 -> x3, other arithmetic: 1.39 us -> 5.94 us  [the longest x1 3.05 us: local(): (third + near.astype(F32)).astype(BF16)]
  transfers between devices with their start and end apart: 17 -> 21, of which waited for: 12 -> 12; matrix products, arithmetic and copies ran while one was open for 12% -> 14% of each run, Pallas kernels for 19% -> 19%
where the time goes in v3:
time: 288 us; the launch traced here: 286 us
  waiting for transfers between devices  109 us (38%)
  Pallas kernels  70.8 us (25%)
  starting transfers between devices  59.6 us (21%)
  matrix products  22.8 us (8%)
  other arithmetic  13.7 us (5%)
  local copies, waits for them, and re-layouts  10.1 us (4%)
    pallas_call x4, Pallas kernels, experts_apply(): pl.pallas_call(partial(experts_kernel, rows=rows, top=top, tile=divisor(f...  70.8 us
    all_to_all x8, waiting for transfers between devices, exchange(): lax.all_to_all(value.reshape(chips, rows, value.shape[1]), ('y', 'x'), 0,...  59.1 us
    all_to_all x8, starting transfers between devices, exchange(): lax.all_to_all(value.reshape(chips, rows, value.shape[1]), ('y', 'x'), 0,...  33.3 us
    ppermute x2, waiting for transfers between devices, inward(): return lax.ppermute(value, 'z', [(0, 1), (3, 2)])  20.7 us
    ppermute x2, waiting for transfers between devices, flip(): return lax.ppermute(value, 'z', [(i, i ^ mask) for i in range(z_size)])  15.6 us
    ppermute x2, starting transfers between devices, inward(): return lax.ppermute(value, 'z', [(0, 1), (3, 2)])  14.1 us
    ppermute x2, waiting for transfers between devices, outward(): return lax.ppermute(value, 'z', [(1, 0), (2, 3)])  13.2 us
    dot_general x8, matrix products, mixed(): jnp.dot(mix, arrived_back, preferred_element_type=F32)  12.8 us
  transfers between devices with their start and end apart: 21, of which 12 were waited for; matrix products, arithmetic and copies ran while one was open for 14% of the time, Pallas kernels for 19%

profile of v3, /device:TPU:0, one launch (start us, length us, event | category | flops | bytes accessed | tf_op | source)
XLA Modules:
  0.0 286.0 jit_solution(14699348874322810497)
XLA Ops:
  2.8 2.3 concatenate.11
  5.1 2.6 collective-permute-start.2
  7.7 1.7 collective-permute-start
  10.3 2.0 convolution_convert_fusion.3
  12.3 3.7 %all-to-all-start = ((bf16[4,64,4224]{2,1,0:T(8,128)(2,1)}), bf16[4,64,4224]{2,1,0:T(8,128)(2,1)S(1)}, u32[]{:S(2)}, u32[]{:S(2)}) async-start(bf16[4,64,4224]{2,1,0:T(8,128)(2,1)} %bitcast.92), calls=%async_computation | async-start | bytes 4325376 | tf_op jit(solution)/shard_map/all_to_all | solution.py:185
  16.7 15.6 %collective-permute-done.2 = bf16[128,4224]{1,0:T(8,128)(2,1)} collective-permute-done((bf16[128,4224]{1,0:T(8,128)(2,1)S(1)}, bf16[128,4224]{1,0:T(8,128)(2,1)}, u32[]{:S(2)}, u32[]{:S(2)}) %collective-permute-start.2) | collective-permute-done | bytes 1081376 | tf_op jit(solution)/shard_map/ppermute | solution.py:147
  32.4 1.3 collective-permute-start.1
  37.2 3.3 %convolution_convert_fusion.2 = bf16[256,4224]{1,0:T(8,128)(2,1)} fusion(pred[128,256]{0,1:T(8,128)(4,1)S(1)} %bitcast.109, bf16[128,4224]{1,0:T(8,128)(2,1)} %collective-permute-done.2), kind=kOutput, calls=%fused_computation.2 | convolution fusion | flops 277905408 | bytes 3276800 | tf_op jit(solution)/shard_map/dot_general | solution.py:189
  40.5 1.6 all-to-all-done
  42.2 1.4 copy-done
  43.5 4.5 %all-to-all-start.1 = ((bf16[4,64,4224]{2,1,0:T(8,128)(2,1)}), bf16[4,64,4224]{2,1,0:T(8,128)(2,1)}, u32[]{:S(2)}, u32[]{:S(2)}) async-start(bf16[4,64,4224]{2,1,0:T(8,128)(2,1)} %bitcast.94), calls=%async_computation.1 | async-start | bytes 4325376 | tf_op jit(solution)/shard_map/all_to_all | solution.py:185
  48.0 1.3 collective-permute-start.7
  49.3 13.2 %collective-permute-done.1 = bf16[128,4224]{1,0:T(8,128)(2,1)} collective-permute-done((bf16[128,4224]{1,0:T(8,128)(2,1)}, bf16[128,4224]{1,0:T(8,128)(2,1)}, u32[]{:S(2)}, u32[]{:S(2)}) %collective-permute-start.1) | collective-permute-done | bytes 1081376 | tf_op jit(solution)/shard_map/ppermute | solution.py:153
  62.5 1.4 broadcast_select_fusion.1
  65.1 2.1 convolution_convert_fusion.1
  67.2 6.2 %all-to-all-done.1 = bf16[4,64,4224]{2,1,0:T(8,128)(2,1)} async-done(((bf16[4,64,4224]{2,1,0:T(8,128)(2,1)}), bf16[4,64,4224]{2,1,0:T(8,128)(2,1)}, u32[]{:S(2)}, u32[]{:S(2)}) %all-to-all-start.1) | async-done | bytes 2162720 | tf_op jit(solution)/shard_map/all_to_all | solution.py:185
  73.4 3.6 %all-to-all-start.2 = ((bf16[4,64,4224]{2,1,0:T(8,128)(2,1)}), bf16[4,64,4224]{2,1,0:T(8,128)(2,1)S(1)}, u32[]{:S(2)}, u32[]{:S(2)}) async-start(bf16[4,64,4224]{2,1,0:T(8,128)(2,1)} %bitcast.93), calls=%async_computation.2 | async-start | bytes 4325376 | tf_op jit(solution)/shard_map/all_to_all | solution.py:185
  77.1 17.7 %shard_map.64 = bf16[256,4096]{1,0:T(8,128)(2,1)} custom-call(s32[3]{0:T(128)} %pad_add_fusion.info, bf16[256,4224]{1,0:T(8,128)(2,1)} %bitcast.90, bf16[4096,768]{1,0:T(8,128)(2,1)} %bitcast.72, bf16[4096,768]{1,0:T(8,128)(2,1)} %bitcast.77, bf16[768,4096]{1,0:T(8,128)(2,1)} %bitcast.82, bf16[4096,768]{1,0:T(8,128)(2,1)} %collective-permute-done.4.g1, ...), custom_call_target="tpu_custom_call" | custom-call | flops 9663676416 | bytes 41943040 | tf_op jit(solution)/shard_map/pallas_call | solution.py:94
  94.8 1.4 broadcast_select_fusion
  98.4 2.1 convolution_convert_fusion
  100.4 1.6 all-to-all-done.2
  102.0 1.3 copy-done.1
  103.4 4.7 %all-to-all-start.3 = ((bf16[4,64,4224]{2,1,0:T(8,128)(2,1)}), bf16[4,64,4224]{2,1,0:T(8,128)(2,1)}, u32[]{:S(2)}, u32[]{:S(2)}) async-start(bf16[4,64,4224]{2,1,0:T(8,128)(2,1)} %bitcast.95), calls=%async_computation.3 | async-start | bytes 4325376 | tf_op jit(solution)/shard_map/all_to_all | solution.py:185
  108.1 17.7 %shard_map.65 = bf16[256,4096]{1,0:T(8,128)(2,1)} custom-call(s32[3]{0:T(128)} %pad_add_fusion.info, bf16[256,4224]{1,0:T(8,128)(2,1)} %bitcast.13.x_hbm, bf16[4096,768]{1,0:T(8,128)(2,1)} %bitcast.73, bf16[4096,768]{1,0:T(8,128)(2,1)} %bitcast.78, bf16[768,4096]{1,0:T(8,128)(2,1)} %bitcast.83, bf16[4096,768]{1,0:T(8,128)(2,1)} %collective-permute-done.4.g1, ...), custom_call_target="tpu_custom_call" | custom-call | flops 9663676416 | bytes 41943040 | tf_op jit(solution)/shard_map/pallas_call | solution.py:94
  125.7 7.2 %all-to-all-done.3 = bf16[4,64,4224]{2,1,0:T(8,128)(2,1)} async-done(((bf16[4,64,4224]{2,1,0:T(8,128)(2,1)}), bf16[4,64,4224]{2,1,0:T(8,128)(2,1)}, u32[]{:S(2)}, u32[]{:S(2)}) %all-to-all-start.3) | async-done | bytes 2162720 | tf_op jit(solution)/shard_map/all_to_all | solution.py:185
  133.0 17.7 %shard_map.66 = bf16[256,4096]{1,0:T(8,128)(2,1)} custom-call(s32[3]{0:T(128)} %pad_add_fusion.info, bf16[256,4224]{1,0:T(8,128)(2,1)} %bitcast.22.x_hbm, bf16[4096,768]{1,0:T(8,128)(2,1)} %bitcast.74, bf16[4096,768]{1,0:T(8,128)(2,1)} %bitcast.79, bf16[768,4096]{1,0:T(8,128)(2,1)} %bitcast.84, bf16[4096,768]{1,0:T(8,128)(2,1)} %collective-permute-done.4.g1, ...), custom_call_target="tpu_custom_call" | custom-call | flops 9663676416 | bytes 41943040 | tf_op jit(solution)/shard_map/pallas_call | solution.py:94
  150.7 4.0 %all-to-all-start.4 = ((bf16[4,64,4096]{2,1,0:T(8,128)(2,1)}), bf16[4,64,4096]{2,1,0:T(8,128)(2,1)S(1)}, u32[]{:S(2)}, u32[]{:S(2)}) async-start(bf16[4,64,4096]{2,1,0:T(8,128)(2,1)} %bitcast.98), calls=%async_computation.4 | async-start | bytes 4194304 | tf_op jit(solution)/shard_map/all_to_all | solution.py:185
  155.4 17.7 %shard_map.67 = bf16[256,4096]{1,0:T(8,128)(2,1)} custom-call(s32[3]{0:T(128)} %pad_add_fusion.info, bf16[256,4224]{1,0:T(8,128)(2,1)} %bitcast.91, bf16[4096,768]{1,0:T(8,128)(2,1)} %bitcast.75, bf16[4096,768]{1,0:T(8,128)(2,1)} %bitcast.80, bf16[768,4096]{1,0:T(8,128)(2,1)} %bitcast.85, bf16[4096,768]{1,0:T(8,128)(2,1)} %collective-permute-done.4.g1, ...), custom_call_target="tpu_custom_call" | custom-call | flops 9663676416 | bytes 41943040 | tf_op jit(solution)/shard_map/pallas_call | solution.py:94
  173.1 5.6 %all-to-all-done.4 = bf16[4,64,4096]{2,1,0:T(8,128)(2,1)S(1)} async-done(((bf16[4,64,4096]{2,1,0:T(8,128)(2,1)}), bf16[4,64,4096]{2,1,0:T(8,128)(2,1)S(1)}, u32[]{:S(2)}, u32[]{:S(2)}) %all-to-all-start.4) | async-done | bytes 2097184 | tf_op jit(solution)/shard_map/all_to_all | solution.py:185
  178.7 4.6 %all-to-all-start.5 = ((bf16[4,64,4096]{2,1,0:T(8,128)(2,1)}), bf16[4,64,4096]{2,1,0:T(8,128)(2,1)}, u32[]{:S(2)}, u32[]{:S(2)}) async-start(bf16[4,64,4096]{2,1,0:T(8,128)(2,1)} %bitcast.99), calls=%async_computation.5 | async-start | bytes 4194304 | tf_op jit(solution)/shard_map/all_to_all | solution.py:185
  184.1 1.9 fusion.50
  186.0 8.8 %collective-permute-start.8 = (bf16[128,4096]{1,0:T(8,128)(2,1)S(1)}, bf16[128,4096]{1,0:T(8,128)(2,1)S(1)}, u32[]{:S(2)}, u32[]{:S(2)}) collective-permute-start(bf16[128,4096]{1,0:T(8,128)(2,1)S(1)} %get-tuple-element.83), channel_id=1, source_target_pairs={{0,2},{6,4},{1,3},{7,5},{8,10},{14,12},{9,11},{15,13},{16,18},{22,... | collective-permute-start | bytes 3145736 | tf_op jit(solution)/shard_map/ppermute | solution.py:156
  194.8 12.9 %all-to-all-done.5 = bf16[4,64,4096]{2,1,0:T(8,128)(2,1)} async-done(((bf16[4,64,4096]{2,1,0:T(8,128)(2,1)}), bf16[4,64,4096]{2,1,0:T(8,128)(2,1)}, u32[]{:S(2)}, u32[]{:S(2)}) %all-to-all-start.5) | async-done | bytes 2097184 | tf_op jit(solution)/shard_map/all_to_all | solution.py:185
  207.7 2.1 fusion.52
  209.7 6.5 %collective-permute-done.8 = bf16[128,4096]{1,0:T(8,128)(2,1)S(1)} collective-permute-done((bf16[128,4096]{1,0:T(8,128)(2,1)S(1)}, bf16[128,4096]{1,0:T(8,128)(2,1)S(1)}, u32[]{:S(2)}, u32[]{:S(2)}) %collective-permute-start.8) | collective-permute-done | bytes 1048608 | tf_op jit(solution)/shard_map/ppermute | solution.py:156
  216.3 3.2 %add_convert_fusion.3 = (bf16[128,4096]{1,0:T(8,128)(2,1)}, bf16[128,4096]{1,0:T(8,128)(2,1)S(1)}) fusion(bf16[128,4096]{1,0:T(8,128)(2,1)S(1)} %collective-permute-done.8, f32[128,4096]{1,0:T(8,128)S(1)} %fusion.52, bf16[128,256]{0,1:T(8,128)(2,1)S(1)} %bitcast.102, bf16[256,4096]{1,0:T(8,128)(2,1)} %bitcast.26), kind=kOutput, calls=%fused_computation.13 | convolution fusion | flops 271056896 | bytes 7405568 | tf_op jit(solution)/shard_map/dot_general | solution.py:223
  219.5 5.4 %collective-permute-start.11 = (bf16[128,4096]{1,0:T(8,128)(2,1)S(1)}, bf16[128,4096]{1,0:T(8,128)(2,1)}, u32[]{:S(2)}, u32[]{:S(2)}) collective-permute-start(bf16[128,4096]{1,0:T(8,128)(2,1)S(1)} %get-tuple-element.70), channel_id=1, source_target_pairs={{0,2},{6,4},{1,3},{7,5},{8,10},{14,12},{9,11},{15,13},{16,18},{22,... | collective-permute-start | bytes 3145736 | tf_op jit(solution)/shard_map/ppermute | solution.py:156
  224.9 3.9 %all-to-all-start.6 = ((bf16[4,64,4096]{2,1,0:T(8,128)(2,1)}), bf16[4,64,4096]{2,1,0:T(8,128)(2,1)S(1)}, u32[]{:S(2)}, u32[]{:S(2)}) async-start(bf16[4,64,4096]{2,1,0:T(8,128)(2,1)} %bitcast.97), calls=%async_computation.6 | async-start | bytes 4194304 | tf_op jit(solution)/shard_map/all_to_all | solution.py:185
  228.7 1.6 collective-permute-start.9
  230.4 14.2 %collective-permute-done.11 = bf16[128,4096]{1,0:T(8,128)(2,1)} collective-permute-done((bf16[128,4096]{1,0:T(8,128)(2,1)S(1)}, bf16[128,4096]{1,0:T(8,128)(2,1)}, u32[]{:S(2)}, u32[]{:S(2)}) %collective-permute-start.11) | collective-permute-done | bytes 1048608 | tf_op jit(solution)/shard_map/ppermute | solution.py:156
  244.5 3.0 %add_convert_fusion.1 = bf16[128,4096]{1,0:T(8,128)(2,1)} fusion(f32[128,4096]{1,0:T(8,128)} %get-tuple-element.84, bf16[128,4096]{1,0:T(8,128)(2,1)} %collective-permute-done.11), kind=kLoop, calls=%fused_computation.11 | loop fusion | flops 1572864 | bytes 4194304 | tf_op jit(solution)/shard_map/convert_element_type | solution.py:243
  248.3 3.3 %all-to-all-done.6 = bf16[4,64,4096]{2,1,0:T(8,128)(2,1)S(1)} async-done(((bf16[4,64,4096]{2,1,0:T(8,128)(2,1)}), bf16[4,64,4096]{2,1,0:T(8,128)(2,1)S(1)}, u32[]{:S(2)}, u32[]{:S(2)}) %all-to-all-start.6) | async-done | bytes 2097184 | tf_op jit(solution)/shard_map/all_to_all | solution.py:185
  251.6 4.4 %all-to-all-start.7 = ((bf16[4,64,4096]{2,1,0:T(8,128)(2,1)}), bf16[4,64,4096]{2,1,0:T(8,128)(2,1)}, u32[]{:S(2)}, u32[]{:S(2)}) async-start(bf16[4,64,4096]{2,1,0:T(8,128)(2,1)} %bitcast.96), calls=%async_computation.7 | async-start | bytes 4194304 | tf_op jit(solution)/shard_map/all_to_all | solution.py:185
  257.0 1.5 add_convert_fusion.2
  259.7 20.7 %all-to-all-done.7 = bf16[4,64,4096]{2,1,0:T(8,128)(2,1)} async-done(((bf16[4,64,4096]{2,1,0:T(8,128)(2,1)}), bf16[4,64,4096]{2,1,0:T(8,128)(2,1)}, u32[]{:S(2)}, u32[]{:S(2)}) %all-to-all-start.7) | async-done | bytes 2097184 | tf_op jit(solution)/shard_map/all_to_all | solution.py:185
  280.4 2.1 convolution_bitcast_fusion
  282.5 2.1 fusion
  284.6 1.4 add_convert_fusion
  (88 shorter events, 15.7 us)
Async XLA Ops:
  0.0 77.1 %collective-permute-start.4 = (bf16[4096,768]{1,0:T(8,128)(2,1)}, bf16[4096,768]{1,0:T(8,128)(2,1)}, u32[]{:S(2)}, u32[]{:S(2)}) collective-permute-start(bf16[4096,768]{1,0:T(8,128)(2,1)} %bitcast.71), channel_id=1, source_target_pairs={{0,8},{8,0},{1,9},{9,1},{2,10},{10,2},{3,11},{11,3},{4,12},{12,4},... | collective-permute-start | bytes 18874376 | tf_op jit(solution)/shard_map/ppermute | solution.py:168
  0.5 76.6 %collective-permute-start.5 = (bf16[4096,768]{1,0:T(8,128)(2,1)}, bf16[4096,768]{1,0:T(8,128)(2,1)}, u32[]{:S(2)}, u32[]{:S(2)}) collective-permute-start(bf16[4096,768]{1,0:T(8,128)(2,1)} %bitcast.76), channel_id=1, source_target_pairs={{0,8},{8,0},{1,9},{9,1},{2,10},{10,2},{3,11},{11,3},{4,12},{12,4},... | collective-permute-start | bytes 18874376 | tf_op jit(solution)/shard_map/ppermute | solution.py:168
  0.5 76.6 %collective-permute-start.6 = (bf16[768,4096]{1,0:T(8,128)(2,1)}, bf16[768,4096]{1,0:T(8,128)(2,1)}, u32[]{:S(2)}, u32[]{:S(2)}) collective-permute-start(bf16[768,4096]{1,0:T(8,128)(2,1)} %bitcast.81), channel_id=1, source_target_pairs={{0,8},{8,0},{1,9},{9,1},{2,10},{10,2},{3,11},{11,3},{4,12},{12,4},... | collective-permute-start | bytes 18874376 | tf_op jit(solution)/shard_map/ppermute | solution.py:168
  5.1 27.3 %collective-permute-start.2 = (bf16[128,4224]{1,0:T(8,128)(2,1)S(1)}, bf16[128,4224]{1,0:T(8,128)(2,1)}, u32[]{:S(2)}, u32[]{:S(2)}) collective-permute-start(bf16[128,4224]{1,0:T(8,128)(2,1)S(1)} %concatenate.11), channel_id=1, source_target_pairs={{0,2},{2,0},{4,6},{6,4},{1,3},{3,1},{5,7},{7,5},{8,10},{10,8},{12,... | collective-permute-start | bytes 3244040 | tf_op jit(solution)/shard_map/ppermute | solution.py:147
  7.7 24.6 %collective-permute-start = (bf16[128,4224]{1,0:T(8,128)(2,1)S(1)}, bf16[128,4224]{1,0:T(8,128)(2,1)}, u32[]{:S(2)}, u32[]{:S(2)}) collective-permute-start(bf16[128,4224]{1,0:T(8,128)(2,1)S(1)} %concatenate.11), channel_id=1, source_target_pairs={{2,4},{4,2},{3,5},{5,3},{10,12},{12,10},{11,13},{13,11},{18,20},{2... | collective-permute-start | bytes 3244040 | tf_op jit(solution)/shard_map/ppermute | solution.py:150
  10.2 88.1 %copy-start.6 = (f32[64]{0:T(128)}, f32[64]{0:T(128)S(1)}, u32[]{:S(2)}) copy-start(f32[64]{0:T(128)S(1)} %iota_convert_fusion) | copy-start | bytes 772
  12.3 29.8 %all-to-all-start = ((bf16[4,64,4224]{2,1,0:T(8,128)(2,1)}), bf16[4,64,4224]{2,1,0:T(8,128)(2,1)S(1)}, u32[]{:S(2)}, u32[]{:S(2)}) async-start(bf16[4,64,4224]{2,1,0:T(8,128)(2,1)} %bitcast.92), calls=%async_computation | async-start | bytes 4325376 | tf_op jit(solution)/shard_map/all_to_all | solution.py:185
  32.4 30.1 %collective-permute-start.1 = (bf16[128,4224]{1,0:T(8,128)(2,1)}, bf16[128,4224]{1,0:T(8,128)(2,1)}, u32[]{:S(2)}, u32[]{:S(2)}) collective-permute-start(bf16[128,4224]{1,0:T(8,128)(2,1)} %collective-permute-done), channel_id=1, source_target_pairs={{2,0},{4,6},{3,1},{5,7},{10,8},{12,14},{11,9},{13,15},{18,16},{20,... | collective-permute-start | bytes 3244040 | tf_op jit(solution)/shard_map/ppermute | solution.py:153
  33.7 14.3 %collective-permute-start.3 = (bf16[128,4224]{1,0:T(8,128)(2,1)}, bf16[128,4224]{1,0:T(8,128)(2,1)S(1)}, u32[]{:S(2)}, u32[]{:S(2)}) collective-permute-start(bf16[128,4224]{1,0:T(8,128)(2,1)} %collective-permute-done.2), channel_id=1, source_target_pairs={{2,4},{4,2},{3,5},{5,3},{10,12},{12,10},{11,13},{13,11},{18,20},{2... | collective-permute-start | bytes 3244040 | tf_op jit(solution)/shard_map/ppermute | solution.py:150
  42.2 1.4 copy-start
  43.5 29.9 %all-to-all-start.1 = ((bf16[4,64,4224]{2,1,0:T(8,128)(2,1)}), bf16[4,64,4224]{2,1,0:T(8,128)(2,1)}, u32[]{:S(2)}, u32[]{:S(2)}) async-start(bf16[4,64,4224]{2,1,0:T(8,128)(2,1)} %bitcast.94), calls=%async_computation.1 | async-start | bytes 4325376 | tf_op jit(solution)/shard_map/all_to_all | solution.py:185
  48.0 46.8 %collective-permute-start.7 = (bf16[128,4224]{1,0:T(8,128)(2,1)S(1)}, bf16[128,4224]{1,0:T(8,128)(2,1)}, u32[]{:S(2)}, u32[]{:S(2)}) collective-permute-start(bf16[128,4224]{1,0:T(8,128)(2,1)S(1)} %collective-permute-done.3), channel_id=1, source_target_pairs={{2,0},{4,6},{3,1},{5,7},{10,8},{12,14},{11,9},{13,15},{18,16},{20,... | collective-permute-start | bytes 3244040 | tf_op jit(solution)/shard_map/ppermute | solution.py:153
  73.4 28.6 %all-to-all-start.2 = ((bf16[4,64,4224]{2,1,0:T(8,128)(2,1)}), bf16[4,64,4224]{2,1,0:T(8,128)(2,1)S(1)}, u32[]{:S(2)}, u32[]{:S(2)}) async-start(bf16[4,64,4224]{2,1,0:T(8,128)(2,1)} %bitcast.93), calls=%async_computation.2 | async-start | bytes 4325376 | tf_op jit(solution)/shard_map/all_to_all | solution.py:185
  102.0 1.3 copy-start.1
  103.4 29.6 %all-to-all-start.3 = ((bf16[4,64,4224]{2,1,0:T(8,128)(2,1)}), bf16[4,64,4224]{2,1,0:T(8,128)(2,1)}, u32[]{:S(2)}, u32[]{:S(2)}) async-start(bf16[4,64,4224]{2,1,0:T(8,128)(2,1)} %bitcast.95), calls=%async_computation.3 | async-start | bytes 4325376 | tf_op jit(solution)/shard_map/all_to_all | solution.py:185
  150.7 4.3 %copy-start.3 = (f32[128,8]{1,0:T(8,128)S(1)}, f32[128,8]{1,0:T(8,128)}, u32[]{:S(2)}) copy-start(f32[128,8]{1,0:T(8,128)} %get-tuple-element.74) | copy-start | bytes 12292
  150.7 4.3 %copy-start.2 = (f32[128,8]{1,0:T(8,128)S(1)}, f32[128,8]{1,0:T(8,128)}, u32[]{:S(2)}) copy-start(f32[128,8]{1,0:T(8,128)} %get-tuple-element.75) | copy-start | bytes 12292
  150.7 4.4 %copy-start.5 = (f32[128,8]{1,0:T(8,128)S(1)}, f32[128,8]{1,0:T(8,128)}, u32[]{:S(2)}) copy-start(f32[128,8]{1,0:T(8,128)} %get-tuple-element.77) | copy-start | bytes 12292
  150.7 4.5 %copy-start.4 = (f32[128,8]{1,0:T(8,128)S(1)}, f32[128,8]{1,0:T(8,128)}, u32[]{:S(2)}) copy-start(f32[128,8]{1,0:T(8,128)} %get-tuple-element.78) | copy-start | bytes 12292
  150.7 28.0 %all-to-all-start.4 = ((bf16[4,64,4096]{2,1,0:T(8,128)(2,1)}), bf16[4,64,4096]{2,1,0:T(8,128)(2,1)S(1)}, u32[]{:S(2)}, u32[]{:S(2)}) async-start(bf16[4,64,4096]{2,1,0:T(8,128)(2,1)} %bitcast.98), calls=%async_computation.4 | async-start | bytes 4194304 | tf_op jit(solution)/shard_map/all_to_all | solution.py:185
  178.7 4.6 %copy-start.7 = (f32[64]{0:T(128)S(1)}, f32[64]{0:T(128)}, u32[]{:S(2)}) copy-start(f32[64]{0:T(128)} %copy-done.6) | copy-start | bytes 772
  178.7 29.0 %all-to-all-start.5 = ((bf16[4,64,4096]{2,1,0:T(8,128)(2,1)}), bf16[4,64,4096]{2,1,0:T(8,128)(2,1)}, u32[]{:S(2)}, u32[]{:S(2)}) async-start(bf16[4,64,4096]{2,1,0:T(8,128)(2,1)} %bitcast.99), calls=%async_computation.5 | async-start | bytes 4194304 | tf_op jit(solution)/shard_map/all_to_all | solution.py:185
  186.0 30.3 %collective-permute-start.8 = (bf16[128,4096]{1,0:T(8,128)(2,1)S(1)}, bf16[128,4096]{1,0:T(8,128)(2,1)S(1)}, u32[]{:S(2)}, u32[]{:S(2)}) collective-permute-start(bf16[128,4096]{1,0:T(8,128)(2,1)S(1)} %get-tuple-element.83), channel_id=1, source_target_pairs={{0,2},{6,4},{1,3},{7,5},{8,10},{14,12},{9,11},{15,13},{16,18},{22,... | collective-permute-start | bytes 3145736 | tf_op jit(solution)/shard_map/ppermute | solution.py:156
  219.5 25.0 %collective-permute-start.11 = (bf16[128,4096]{1,0:T(8,128)(2,1)S(1)}, bf16[128,4096]{1,0:T(8,128)(2,1)}, u32[]{:S(2)}, u32[]{:S(2)}) collective-permute-start(bf16[128,4096]{1,0:T(8,128)(2,1)S(1)} %get-tuple-element.70), channel_id=1, source_target_pairs={{0,2},{6,4},{1,3},{7,5},{8,10},{14,12},{9,11},{15,13},{16,18},{22,... | collective-permute-start | bytes 3145736 | tf_op jit(solution)/shard_map/ppermute | solution.py:156
  224.9 26.7 %all-to-all-start.6 = ((bf16[4,64,4096]{2,1,0:T(8,128)(2,1)}), bf16[4,64,4096]{2,1,0:T(8,128)(2,1)S(1)}, u32[]{:S(2)}, u32[]{:S(2)}) async-start(bf16[4,64,4096]{2,1,0:T(8,128)(2,1)} %bitcast.97), calls=%async_computation.6 | async-start | bytes 4194304 | tf_op jit(solution)/shard_map/all_to_all | solution.py:185
  228.7 28.3 %collective-permute-start.9 = (bf16[128,4096]{1,0:T(8,128)(2,1)}, bf16[128,4096]{1,0:T(8,128)(2,1)}, u32[]{:S(2)}, u32[]{:S(2)}) collective-permute-start(bf16[128,4096]{1,0:T(8,128)(2,1)} %get-tuple-element.69), channel_id=1, source_target_pairs={{2,4},{4,2},{3,5},{5,3},{10,12},{12,10},{11,13},{13,11},{18,20},{2... | collective-permute-start | bytes 3145736 | tf_op jit(solution)/shard_map/ppermute | solution.py:150
  247.6 37.0 %collective-permute-start.12 = (bf16[128,4096]{1,0:T(8,128)(2,1)}, bf16[128,4096]{1,0:T(8,128)(2,1)S(1)}, u32[]{:S(2)}, u32[]{:S(2)}) collective-permute-start(bf16[128,4096]{1,0:T(8,128)(2,1)} %add_convert_fusion.1), channel_id=1, source_target_pairs={{2,4},{4,2},{3,5},{5,3},{10,12},{12,10},{11,13},{13,11},{18,20},{2... | collective-permute-start | bytes 3145736 | tf_op jit(solution)/shard_map/ppermute | solution.py:150
  251.6 28.8 %all-to-all-start.7 = ((bf16[4,64,4096]{2,1,0:T(8,128)(2,1)}), bf16[4,64,4096]{2,1,0:T(8,128)(2,1)}, u32[]{:S(2)}, u32[]{:S(2)}) async-start(bf16[4,64,4096]{2,1,0:T(8,128)(2,1)} %bitcast.96), calls=%async_computation.7 | async-start | bytes 4194304 | tf_op jit(solution)/shard_map/all_to_all | solution.py:185
  258.5 26.0 %collective-permute-start.10 = (bf16[128,4096]{1,0:T(8,128)(2,1)S(1)}, bf16[128,4096]{1,0:T(8,128)(2,1)S(1)}, u32[]{:S(2)}, u32[]{:S(2)}) collective-permute-start(bf16[128,4096]{1,0:T(8,128)(2,1)S(1)} %add_convert_fusion.2), channel_id=1, source_target_pairs={{0,2},{2,0},{4,6},{6,4},{1,3},{3,1},{5,7},{7,5},{8,10},{10,8},{12,... | collective-permute-start | bytes 3145736 | tf_op jit(solution)/shard_map/ppermute | solution.py:147

commit v4 on v3

v4 whole, which is shorter than its diff:
```python
from functools import partial

import jax
import jax.numpy as jnp
from jax import lax
from jax.experimental import pallas as pl
from jax.experimental.pallas import tpu as pltpu
from jax.sharding import Mesh, PartitionSpec as P

F32 = jnp.float32
BF16 = jnp.bfloat16
EXTRA = 128
MIB = 2**20
ROUTE_COST = 400
MIX_COST = 4


def divisor(size, most):
    return next(d for d in range(min(size, most), 0, -1) if size % d == 0)


def experts_kernel(info, *refs, parts, rows, top, tile, span):
    x_hbm, refs = refs[:parts], refs[parts:]
    (g0, u0, d0, g1, u1, d1), refs = refs[:6], refs[6:]
    o_hbm, refs = refs[:parts], refs[parts:]
    x_ref, bg0, bu0, bd0, bg1, bu1, bd1, gate_ref, hid, o_ref, sems, out_sems = refs
    total, width = o_ref.shape
    ff = g0.shape[1]
    spans = width // span
    held = [pl.ds(p * (total // parts), total // parts) for p in range(parts)]
    x_copies = [pltpu.make_async_copy(x_hbm[p], x_ref.at[held[p]], sems.at[4 + 2 * spans + p]) for p in range(parts)]
    for c in x_copies:
        c.start()
    ins = [pltpu.make_async_copy(src, dst, sems.at[n]) for n, (src, dst) in enumerate(((g0, bg0), (u0, bu0), (g1, bg1), (u1, bu1)))]
    for c in ins:
        c.start()
    downs = []
    for n in range(spans):
        s = pl.ds(n * span, span)
        for m, (src, dst) in enumerate(((d0, bd0), (d1, bd1))):
            downs.append(pltpu.make_async_copy(src.at[:, s], dst.at[:, s], sems.at[4 + 2 * n + m]))
            downs[-1].start()
    for c in x_copies:
        c.wait()

    ids = x_ref[:, width:].astype(F32)
    is_id = lax.broadcasted_iota(jnp.int32, ids.shape, 1) < top
    low, high, flip = info[0].astype(F32), info[1].astype(F32), info[2].astype(F32)
    has_low = jnp.max(jnp.where(is_id & (ids == low), 1.0, 0.0), axis=1, keepdims=True)
    has_high = jnp.max(jnp.where(is_id & (ids == high), 1.0, 0.0), axis=1, keepdims=True)
    share = jnp.broadcast_to(has_low * (1.0 - 0.5 * has_high), (total, 128)).astype(BF16)
    r = lax.broadcasted_iota(jnp.int32, (total, total), 0)
    c = lax.broadcasted_iota(jnp.int32, (total, total), 1)
    same = jnp.where(r // rows == c // rows, 1.0, 0.0).astype(BF16)
    low_rows = jnp.dot(same, share, preferred_element_type=F32)
    at = (lax.broadcasted_iota(jnp.int32, (total, 128), 0) % rows).astype(F32)
    is_low = jnp.where(at < low_rows, 1.0, 0.0)
    first = (is_low * (1.0 - flip) + (1.0 - is_low) * flip)[:, :1]

    for which, (bg, bu) in enumerate(((bg0, bu0), (bg1, bu1))):
        keep = first if which == 0 else 1.0 - first
        ins[2 * which].wait()

        @pl.loop(0, ff // tile)
        def _(t):
            s = pl.ds(pl.multiple_of(t * tile, tile), tile)
            gate_ref[:, s] = jnp.dot(x_ref[:, :width], bg[:, s], preferred_element_type=F32)

        ins[2 * which + 1].wait()

        @pl.loop(0, ff // tile)
        def _(t):
            s = pl.ds(pl.multiple_of(t * tile, tile), tile)
            up = jnp.dot(x_ref[:, :width], bu[:, s], preferred_element_type=F32)
            gate = gate_ref[:, s]
            h = jnp.where(keep > 0.5, gate / (1.0 + jnp.exp(-gate)) * up, 0.0)
            hid[:, pl.ds(pl.multiple_of(which * ff + t * tile, tile), tile)] = h.astype(BF16)

    outs = []
    for n in range(spans):
        downs[2 * n].wait()
        downs[2 * n + 1].wait()
        s = pl.ds(n * span, span)
        o_ref[:, s] = (
            jnp.dot(hid[:, :ff], bd0[:, s], preferred_element_type=F32)
            + jnp.dot(hid[:, ff:], bd1[:, s], preferred_element_type=F32)
        ).astype(BF16)
        for p in range(parts):
            outs.append(pltpu.make_async_copy(o_ref.at[held[p], s], o_hbm[p].at[:, s], out_sems.at[n, p]))
            outs[-1].start()
    for c in outs:
        c.wait()


def experts_apply(info, xs, first, second, rows, top):
    width, ff = first[0].shape
    parts, each = len(xs), xs[0].shape[0]
    total = parts * each
    span = divisor(width // 128, 8) * 128
    spans = width // span
    anywhere = pl.BlockSpec(memory_space=pl.ANY)
    return pl.pallas_call(
        partial(experts_kernel, parts=parts, rows=rows, top=top, tile=divisor(ff // 128, 2) * 128, span=span),
        out_shape=[jax.ShapeDtypeStruct((each, width), BF16)] * parts,
        grid_spec=pltpu.PrefetchScalarGridSpec(
            num_scalar_prefetch=1,
            grid=(1,),
            in_specs=[anywhere] * (parts + 6),
            out_specs=[anywhere] * parts,
            scratch_shapes=[pltpu.VMEM((total, xs[0].shape[1]), BF16)]
            + [pltpu.VMEM(w.shape, BF16) for w in first + second]
            + [pltpu.VMEM((total, ff), F32), pltpu.VMEM((total, 2 * ff), BF16), pltpu.VMEM((total, width), BF16)]
            + [pltpu.SemaphoreType.DMA((4 + 2 * spans + parts,)), pltpu.SemaphoreType.DMA((spans, parts))],
        ),
        compiler_params=pltpu.CompilerParams(vmem_limit_bytes=54 * MIB),
        cost_estimate=pl.CostEstimate(
            flops=12 * total * width * ff, bytes_accessed=12 * width * ff + 4 * total * width, transcendentals=2 * total * ff
        ),
    )(info, *xs, *first, *second)


def pack_kernel(tokens, ids, weights, out):
    count, width = tokens.shape
    top = ids.shape[1]
    out[:, :width] = tokens[...]
    hi = weights[...].astype(BF16)
    mid = (weights[...] - hi.astype(F32)).astype(BF16)
    rest = jnp.zeros((count, EXTRA - 3 * top), F32)
    extra = [ids[...].astype(F32), hi.astype(F32), mid.astype(F32), rest]
    out[:, width:] = jnp.concatenate(extra, axis=1).astype(BF16)


def pack(tokens, ids, weights):
    count, width = tokens.shape
    return pl.pallas_call(
        pack_kernel,
        out_shape=jax.ShapeDtypeStruct((count, width + EXTRA), BF16),
        compiler_params=pltpu.CompilerParams(vmem_limit_bytes=16 * MIB),
    )(tokens, ids, weights)


def route_kernel(flag, plane, *refs, choices, parts, rows, top, width):
    blocks, outs, (mix_hi, mix_mid) = refs[:choices], refs[choices : choices + parts], refs[choices + parts :]

    def block(s):
        value = blocks[0][:, s]
        return value if choices == 1 else jnp.where(flag[0] != 0, value, blocks[1][:, s])

    extra = block(slice(width, width + EXTRA)).astype(F32)
    count = extra.shape[0]
    lanes = mix_hi.shape[1]
    ids = plane[:1, :]
    chosen = jnp.zeros((count, 128), F32)
    w_hi, w_mid = chosen, chosen
    for k in range(top):
        same = extra[:, k : k + 1] == ids
        chosen = jnp.where(same, 1.0, chosen)
        w_hi = jnp.where(same, extra[:, top + k : top + k + 1], w_hi)
        w_mid = jnp.where(same, extra[:, 2 * top + k : 2 * top + k + 1], w_mid)

    def table(shape, test):
        r = lax.broadcasted_iota(jnp.int32, shape, 0)
        c = lax.broadcasted_iota(jnp.int32, shape, 1)
        return jnp.where(test(r, c), 1.0, 0.0).astype(BF16)

    def dot(a, b):
        return jnp.dot(a.astype(BF16), b.astype(BF16), preferred_element_type=F32)

    before = table((count, count), lambda r, c: c < r)
    to_high = table((128, 128), lambda r, c: (c == r + 1) & (r % 2 == 0))
    rank = dot(before, chosen) + dot(jnp.ones((count, count), F32), dot(chosen, to_high))
    rank = jnp.where(chosen > 0.0, rank, -1.0)
    at = (lax.broadcasted_iota(jnp.int32, (count, lanes), 1) % rows).astype(F32)
    taken = jnp.zeros((count, lanes), F32)
    sum_hi, sum_mid = taken, taken
    for side in range(2):
        spread = table((128, lanes), lambda r, c: r == 2 * (c // rows) + side)
        hit = dot(rank, spread) == at
        taken = jnp.where(hit, 1.0, taken)
        sum_hi = jnp.where(hit, dot(w_hi, spread), sum_hi)
        sum_mid = jnp.where(hit, dot(w_mid, spread), sum_mid)
    mix_hi[...] = sum_hi.astype(BF16)
    mix_mid[...] = sum_mid.astype(BF16)
    taken = taken.astype(BF16)
    step = divisor((width + EXTRA) // 128, 11) * 128
    each = lanes // parts
    for n in range((width + EXTRA) // step):
        s = slice(n * step, (n + 1) * step)
        got = lax.dot_general(taken, block(s), (((0,), (0,)), ((), ())), preferred_element_type=F32).astype(BF16)
        for p in range(parts):
            outs[p][:, s] = got[p * each : (p + 1) * each]


def route(flag, plane, blocks, parts, rows, top):
    count, wide = blocks[0].shape
    lanes = parts * rows if parts > 1 else plane.shape[0] * rows
    each = lanes // parts
    chips = lanes // rows
    ids = jnp.full((8, 128), -1.0, F32).at[:, : 2 * chips].set(plane.reshape(1, -1))
    whole = pl.BlockSpec(memory_space=pltpu.VMEM)
    out = pl.pallas_call(
        partial(route_kernel, choices=len(blocks), parts=parts, rows=rows, top=top, width=wide - EXTRA),
        in_specs=[pl.BlockSpec(memory_space=pltpu.SMEM), whole] + [whole] * len(blocks),
        out_specs=[whole] * (parts + 2),
        out_shape=[jax.ShapeDtypeStruct((each, wide), BF16)] * parts + [jax.ShapeDtypeStruct((count, lanes), BF16)] * 2,
        compiler_params=pltpu.CompilerParams(vmem_limit_bytes=24 * MIB),
        cost_estimate=pl.CostEstimate(flops=ROUTE_COST * count * lanes * wide, bytes_accessed=2 * (count + lanes) * wide, transcendentals=0),
    )(flag, ids, *blocks)
    return out[:parts], out[parts:]


def mix_kernel(hi, mid, *refs, parts, terms):
    backs, refs = refs[:parts], refs[parts:]
    adds, outs = refs[: len(refs) - len(terms)], refs[len(refs) - len(terms) :]
    rows = jnp.concatenate([b[...] for b in backs], axis=0)
    total = jnp.dot(hi[...], rows, preferred_element_type=F32) + jnp.dot(mid[...], rows, preferred_element_type=F32)
    for (with_total, used), out in zip(terms, outs):
        value = total if with_total else None
        for n in used:
            add = adds[n][...].astype(F32)
            value = add if value is None else value + add
        out[...] = value.astype(out.dtype)


def mix_rows(mix, backs, adds, terms, dtypes):
    count, lanes = mix[0].shape
    width = backs[0].shape[1]
    step = divisor(width // 128, 8) * 128
    full = pl.BlockSpec((count, lanes), lambda n: (0, 0))
    tall = pl.BlockSpec((count, step), lambda n: (0, n))
    return pl.pallas_call(
        partial(mix_kernel, parts=len(backs), terms=tuple(terms)),
        grid=(width // step,),
        in_specs=[full, full] + [pl.BlockSpec((b.shape[0], step), lambda n: (0, n)) for b in backs] + [tall] * len(adds),
        out_specs=[tall] * len(terms),
        out_shape=[jax.ShapeDtypeStruct((count, width), d) for d in dtypes],
        compiler_params=pltpu.CompilerParams(vmem_limit_bytes=24 * MIB),
        cost_estimate=pl.CostEstimate(flops=MIX_COST * count * lanes * width, bytes_accessed=6 * count * width, transcendentals=0),
    )(*mix, *backs, *adds)


def after(value, *others):
    return lax.optimization_barrier((value,) + others)[0]


def local(tokens, router_weights, expert_ids, gate_weight, up_weight, down_weight):
    z_size = lax.axis_size("z")
    x_size = lax.axis_size("x")
    y_size = lax.axis_size("y")
    lane_count = z_size * x_size
    chips = y_size * x_size
    count, width = tokens.shape
    top = expert_ids.shape[1]
    rows = count * top // (y_size * lane_count)
    z_at = lax.axis_index("z")

    parts = 1
    here = lax.axis_index("y") * x_size + lax.axis_index("x")
    chip = jnp.arange(chips, dtype=jnp.int32)
    chip = chip ^ here if parts > 1 else chip
    low = 2 * (chip // x_size) * lane_count + z_at * x_size + chip % x_size
    plane = jnp.stack([low, low + lane_count], axis=-1).astype(F32)
    low_here = 2 * lax.axis_index("y") * lane_count + z_at * x_size + lax.axis_index("x")
    info = jnp.stack([low_here, low_here + lane_count, lax.axis_index("core")]).astype(jnp.int32)

    def flip(value, mask):
        return lax.ppermute(value, "z", [(i, i ^ mask) for i in range(z_size)])

    def inner(value):
        return lax.ppermute(value, "z", [(1, 2), (2, 1)])

    def outward(value):
        return lax.ppermute(value, "z", [(1, 0), (2, 3)])

    def inward(value):
        return lax.ppermute(value, "z", [(0, 1), (3, 2)])

    is_end = (z_at == 0) | (z_at == z_size - 1)

    block = pack(tokens, expert_ids, router_weights)
    flag = is_end.astype(jnp.int32).reshape(1)
    swap = [(0, 1), (1, 0)]
    own = [gate_weight[0], up_weight[0], down_weight[0]]
    other = [lax.ppermute(w, "core", swap) for w in own]

    def exchange(values):
        if parts == 1:
            value = values[0].reshape(chips, rows, values[0].shape[1])
            return [lax.all_to_all(value, ("y", "x"), 0, 0, tiled=True).reshape(values[0].shape)]
        pairs = [[(i, i ^ m) for i in range(chips)] for m in range(chips)]
        return [values[0]] + [lax.ppermute(values[m], ("y", "x"), pairs[m]) for m in range(1, chips)]

    def run(k, *others):
        outs[k] = experts_apply(info, after(arrived[k], *others), own, other, rows, top)

    line = z_size == 4
    moving = {k: flip(block, k) for k in ((1,) if line else range(1, z_size)) if k & (k - 1) == 0}
    if line:
        middle = inner(block)
    held, mixes, sent, arrived, outs = {0: [block]}, {}, {}, {}, {}
    for k in range(z_size):
        if k and line:
            if k == 1:
                held[1] = [after(moving[1], sent[0])]
                next_inner, next_outer = inner(held[1][0]), outward(after(middle, sent[0]))
            elif k == 2:
                passed = after(next_inner, sent[1])
                last_outer = outward(passed)
                held[2] = [next_outer, passed]
            else:
                held[3] = [after(last_outer, outs[0]), middle]
        elif k:
            bit = k & -k
            held[k] = [after(moving[k] if k == bit else flip(held[k ^ bit][0], bit), sent[k - 1])]
        sent[k], mixes[k] = route(flag, plane, held[k], parts, rows, top)
        if k and parts == 1:
            sent[k] = after(sent[k], arrived[k - 1])
        if k > 1:
            run(k - 2, sent[k])
        arrived[k] = exchange(sent[k])
    last = z_size - 1
    run(last, *[outs[o] for o in outs])

    back, hold, extra = None, [], []
    for k in range(last, -1, -1):
        source = outs[k] if k == last else after(outs[k], *hold, *(back if parts == 1 else []))
        if k < last:
            done = k + 1
            got = after(back, source)
            if not line:
                bit = done & -done
                adds = [r for o, r in extra if o == done]
                hold = mix_rows(mixes[done], got, adds, [(True, range(len(adds)))], [BF16])
                extra.append((done ^ bit, flip(hold[0], bit)))
            elif done == 3:
                third, total = mix_rows(mixes[3], got, [], [(True, ()), (True, ())], [F32, BF16])
                hold = [total]
                from_end = inward(total)
            elif done == 2:
                hold = mix_rows(mixes[2], got, [from_end], [(True, ()), (True, (0,))], [BF16] * 2)
                near, far = inward(hold[0]), inner(hold[1])
            else:
                hold = mix_rows(mixes[1], got, [far, third, near], [(True, (0,)), (False, (1, 2))], [BF16] * 2)
                extra += [(0, flip(hold[0], 1)), (0, inner(hold[1]))]
        if k and k - 1 not in outs:
            run(k - 1, source, *hold)
        back = exchange(source)
    adds = [r for o, r in extra if o == 0]
    return mix_rows(mixes[0], back, adds, [(True, range(len(adds)))], [BF16])[0]


def solution(mesh):
    groups, lanes = mesh.shape["dp"], mesh.shape["expert"]
    y_size = groups // 2
    x_size = y_size if lanes % y_size == 0 else 1
    fine = Mesh(mesh.devices.reshape(y_size, 2, lanes // x_size, x_size), ("y", "core", "z", "x"))
    split = ("y", "core", "z", "x")
    flat, deep = P(split, None), P(split, None, None)
    return jax.shard_map(
        local, mesh=fine, in_specs=(flat, flat, flat, deep, deep, deep), out_specs=flat, check_vma=False
    )
```

time: 288 us -> 279 us (0.969)
  Pallas kernels: 70.8 us -> 98.5 us
  matrix products: 22.8 us -> 0 us
  other arithmetic: 13.7 us -> 1.94 us
  waiting for transfers between devices: 109 us -> 106 us
    pallas_call x4 -> x13, Pallas kernels: 70.8 us -> 98.5 us  [the longest x4 70.8 us: experts_apply(): pl.pallas_call(partial(experts_kernel, parts=parts, rows=rows, top=top, t...]
    dot_general x16 -> x0, matrix products: 22.8 us -> none  [the longest x8 12.8 us: mixed(): jnp.dot(mix, arrived_back, preferred_element_type=F32)]
    ppermute x2, waiting for transfers between devices: 15.6 us -> 33.1 us  [flip(): return lax.ppermute(value, 'z', [(i, i ^ mask) for i in range(z_size)])]
    ppermute x2, waiting for transfers between devices: 20.7 us -> 8.96 us  [inward(): return lax.ppermute(value, 'z', [(0, 1), (3, 2)])]
    unnamed x16 -> x20, local copies, waits for them, and re-layouts: 2.77 us -> 11.7 us
    convert_element_type x11 -> x0, other arithmetic: 8.35 us -> none  [the longest x1 3.05 us: local(): (third + near.astype(F32)).astype(BF16)]
    all_to_all x8, waiting for transfers between devices: 59.1 us -> 52.1 us  [exchange(): lax.all_to_all(value, ('y', 'x'), 0, 0, tiled=True).reshape(values[0].shape)]
    slice x16 -> x0, local copies, waits for them, and re-layouts: 4.64 us -> none  [the longest x12 2.77 us: routed(): extra[:, n * top:(n + 1) * top, None, None]]
  transfers between devices with their start and end apart: 21 -> 21, of which waited for: 12 -> 12; matrix products, arithmetic and copies ran while one was open for 14% -> 1% of each run, Pallas kernels for 19% -> 28%
where the time goes in v4:
time: 279 us; the launch traced here: 277 us
  waiting for transfers between devices  106 us (38%)
  Pallas kernels  98.5 us (35%)
  starting transfers between devices  57.8 us (21%)
  local copies, waits for them, and re-layouts  11.8 us (4%)
    pallas_call x4, Pallas kernels, experts_apply(): pl.pallas_call(partial(experts_kernel, parts=parts, rows=rows, top=top, t...  70.8 us
    all_to_all x8, waiting for transfers between devices, exchange(): lax.all_to_all(value, ('y', 'x'), 0, 0, tiled=True).reshape(values[0].shape)  52.1 us
    all_to_all x8, starting transfers between devices, exchange(): lax.all_to_all(value, ('y', 'x'), 0, 0, tiled=True).reshape(values[0].shape)  33.5 us
    ppermute x2, waiting for transfers between devices, flip(): return lax.ppermute(value, 'z', [(i, i ^ mask) for i in range(z_size)])  33.1 us
    pallas_call x4, Pallas kernels, route(): pl.pallas_call(partial(route_kernel, choices=len(blocks), parts=parts, ro...  14.8 us
    pallas_call x4, Pallas kernels, mix_rows(): pl.pallas_call(partial(mix_kernel, parts=len(backs), terms=tuple(terms)),...  12.8 us
    ppermute x2, waiting for transfers between devices, outward(): return lax.ppermute(value, 'z', [(1, 0), (2, 3)])  12.2 us
    unnamed x20, local copies, waits for them, and re-layouts  11.7 us
  transfers between devices with their start and end apart: 21, of which 12 were waited for; matrix products, arithmetic and copies ran while one was open for 1% of the time, Pallas kernels for 28%

profile of v4, /device:TPU:0, one launch (start us, length us, event | category | flops | bytes accessed | tf_op | source)
XLA Modules:
  0.0 276.8 jit_solution(11968847990063257029)
XLA Ops:
  0.0 0.8 copy.10.weights
  0.8 0.8 copy.9.ids
  1.6 1.2 copy-done.6
  2.9 3.1 %collective-permute-start.2 = (bf16[128,4224]{1,0:T(8,128)(2,1)S(1)}, bf16[128,4224]{1,0:T(8,128)(2,1)}, u32[]{:S(2)}, u32[]{:S(2)}) collective-permute-start(bf16[128,4224]{1,0:T(8,128)(2,1)S(1)} %shard_map.64.refs_0_), channel_id=1, source_target_pairs={{0,2},{2,0},{4,6},{6,4},{1,3},{3,1},{5,7},{7,5},{8,10},{10,8},{12,... | collective-permute-start | bytes 3244040 | tf_op jit(solution)/shard_map/ppermute | solution.py:267
  8.2 2.8 shard_map.65
  11.0 4.5 %all-to-all-start = ((bf16[4,64,4224]{2,1,0:T(8,128)(2,1)}), bf16[4,64,4224]{2,1,0:T(8,128)(2,1)}, u32[]{:S(2)}, u32[]{:S(2)}) async-start(bf16[4,64,4224]{2,1,0:T(8,128)(2,1)} %bitcast.4), calls=%async_computation | async-start | bytes 4325376 | tf_op jit(solution)/shard_map/all_to_all | solution.py:289
  16.7 13.3 %collective-permute-done.2.refs_0_ = bf16[128,4224]{1,0:T(8,128)(2,1)} collective-permute-done((bf16[128,4224]{1,0:T(8,128)(2,1)S(1)}, bf16[128,4224]{1,0:T(8,128)(2,1)}, u32[]{:S(2)}, u32[]{:S(2)}) %collective-permute-start.2) | collective-permute-done | bytes 1081376 | tf_op jit(solution)/shard_map/ppermute | solution.py:267
  30.0 1.3 collective-permute-start.1
  32.0 4.1 %shard_map.66 = (bf16[256,4224]{1,0:T(8,128)(2,1)}, bf16[128,256]{1,0:T(8,128)(2,1)S(1)}, bf16[128,256]{1,0:T(8,128)(2,1)S(1)}) custom-call(s32[1]{0:T(128)} %bitcast.flag, f32[8,128]{1,0:T(8,128)S(1)} %scatter.9.plane, bf16[128,4224]{1,0:T(8,128)(2,1)} %collective-permute-done.2.refs_0_), custom_call_target="tpu_custom_call" | custom-call | flops 55364812800 | bytes 3244032 | tf_op jit(solution)/shard_map/pallas_call | solution.py:201
  36.0 5.0 %all-to-all-done = bf16[4,64,4224]{2,1,0:T(8,128)(2,1)} async-done(((bf16[4,64,4224]{2,1,0:T(8,128)(2,1)}), bf16[4,64,4224]{2,1,0:T(8,128)(2,1)}, u32[]{:S(2)}, u32[]{:S(2)}) %all-to-all-start) | async-done | bytes 2162720 | tf_op jit(solution)/shard_map/all_to_all | solution.py:289
  41.1 4.5 %all-to-all-start.1 = ((bf16[4,64,4224]{2,1,0:T(8,128)(2,1)}), bf16[4,64,4224]{2,1,0:T(8,128)(2,1)}, u32[]{:S(2)}, u32[]{:S(2)}) async-start(bf16[4,64,4224]{2,1,0:T(8,128)(2,1)} %bitcast.6), calls=%async_computation.1 | async-start | bytes 4325376 | tf_op jit(solution)/shard_map/all_to_all | solution.py:289
  45.6 1.3 collective-permute-start.7
  46.9 12.2 %collective-permute-done.1.refs_0_ = bf16[128,4224]{1,0:T(8,128)(2,1)} collective-permute-done((bf16[128,4224]{1,0:T(8,128)(2,1)S(1)}, bf16[128,4224]{1,0:T(8,128)(2,1)}, u32[]{:S(2)}, u32[]{:S(2)}) %collective-permute-start.1) | collective-permute-done | bytes 1081376 | tf_op jit(solution)/shard_map/ppermute | solution.py:273
  59.1 4.0 %shard_map.67 = (bf16[256,4224]{1,0:T(8,128)(2,1)}, bf16[128,256]{1,0:T(8,128)(2,1)S(1)}, bf16[128,256]{1,0:T(8,128)(2,1)S(1)}) custom-call(s32[1]{0:T(128)} %bitcast.flag, f32[8,128]{1,0:T(8,128)S(1)} %scatter.9.plane, bf16[128,4224]{1,0:T(8,128)(2,1)} %collective-permute-done.1.refs_0_, bf16[128,4224]{1,0:T(8,128)(2,1)S(1)} %collective-permute-done.3.refs_1_), custom_call_target="tpu_custom_call" | custom-call | flops 55364812800 | bytes 3244032 | tf_op jit(solution)/shard_map/pallas_call | solution.py:201
  63.0 7.6 %all-to-all-done.1 = bf16[4,64,4224]{2,1,0:T(8,128)(2,1)} async-done(((bf16[4,64,4224]{2,1,0:T(8,128)(2,1)}), bf16[4,64,4224]{2,1,0:T(8,128)(2,1)}, u32[]{:S(2)}, u32[]{:S(2)}) %all-to-all-start.1) | async-done | bytes 2162720 | tf_op jit(solution)/shard_map/all_to_all | solution.py:289
  70.6 4.5 %all-to-all-start.2 = ((bf16[4,64,4224]{2,1,0:T(8,128)(2,1)}), bf16[4,64,4224]{2,1,0:T(8,128)(2,1)}, u32[]{:S(2)}, u32[]{:S(2)}) async-start(bf16[4,64,4224]{2,1,0:T(8,128)(2,1)} %bitcast.11), calls=%async_computation.2 | async-start | bytes 4325376 | tf_op jit(solution)/shard_map/all_to_all | solution.py:289
  75.2 17.8 %shard_map.68 = bf16[256,4096]{1,0:T(8,128)(2,1)} custom-call(s32[3]{0:T(128)} %pad_add_fusion.info, bf16[256,4224]{1,0:T(8,128)(2,1)} %bitcast.5.refs_0_, bf16[4096,768]{1,0:T(8,128)(2,1)} %bitcast.27, bf16[4096,768]{1,0:T(8,128)(2,1)} %bitcast.32, bf16[768,4096]{1,0:T(8,128)(2,1)} %bitcast.37, bf16[4096,768]{1,0:T(8,128)(2,1)} %collective-permute-done.4.refs_4_, ...), custom_call_target="tpu_custom_call" | custom-call | flops 9663676416 | bytes 41943040 | tf_op jit(solution)/shard_map/pallas_call | solution.py:102
  93.0 4.0 %shard_map.69 = (bf16[256,4224]{1,0:T(8,128)(2,1)}, bf16[128,256]{1,0:T(8,128)(2,1)S(1)}, bf16[128,256]{1,0:T(8,128)(2,1)S(1)}) custom-call(s32[1]{0:T(128)} %bitcast.flag, f32[8,128]{1,0:T(8,128)S(1)} %scatter.9.plane, bf16[128,4224]{1,0:T(8,128)(2,1)} %collective-permute-done.7.refs_0_, bf16[128,4224]{1,0:T(8,128)(2,1)S(1)} %copy-done.8), custom_call_target="tpu_custom_call" | custom-call | flops 55364812800 | bytes 3244032 | tf_op jit(solution)/shard_map/pallas_call | solution.py:201
  96.9 3.2 %all-to-all-done.2 = bf16[4,64,4224]{2,1,0:T(8,128)(2,1)} async-done(((bf16[4,64,4224]{2,1,0:T(8,128)(2,1)}), bf16[4,64,4224]{2,1,0:T(8,128)(2,1)}, u32[]{:S(2)}, u32[]{:S(2)}) %all-to-all-start.2) | async-done | bytes 2162720 | tf_op jit(solution)/shard_map/all_to_all | solution.py:289
  100.2 4.6 %all-to-all-start.3 = ((bf16[4,64,4224]{2,1,0:T(8,128)(2,1)}), bf16[4,64,4224]{2,1,0:T(8,128)(2,1)}, u32[]{:S(2)}, u32[]{:S(2)}) async-start(bf16[4,64,4224]{2,1,0:T(8,128)(2,1)} %bitcast.13), calls=%async_computation.3 | async-start | bytes 4325376 | tf_op jit(solution)/shard_map/all_to_all | solution.py:289
  104.8 17.6 %shard_map.70 = bf16[256,4096]{1,0:T(8,128)(2,1)} custom-call(s32[3]{0:T(128)} %pad_add_fusion.info, bf16[256,4224]{1,0:T(8,128)(2,1)} %bitcast.7.refs_0_, bf16[4096,768]{1,0:T(8,128)(2,1)} %bitcast.28, bf16[4096,768]{1,0:T(8,128)(2,1)} %bitcast.33, bf16[768,4096]{1,0:T(8,128)(2,1)} %bitcast.38, bf16[4096,768]{1,0:T(8,128)(2,1)} %collective-permute-done.4.refs_4_, ...), custom_call_target="tpu_custom_call" | custom-call | flops 9663676416 | bytes 41943040 | tf_op jit(solution)/shard_map/pallas_call | solution.py:102
  122.5 7.2 %all-to-all-done.3 = bf16[4,64,4224]{2,1,0:T(8,128)(2,1)} async-done(((bf16[4,64,4224]{2,1,0:T(8,128)(2,1)}), bf16[4,64,4224]{2,1,0:T(8,128)(2,1)}, u32[]{:S(2)}, u32[]{:S(2)}) %all-to-all-start.3) | async-done | bytes 2162720 | tf_op jit(solution)/shard_map/all_to_all | solution.py:289
  129.7 17.7 %shard_map.71 = bf16[256,4096]{1,0:T(8,128)(2,1)} custom-call(s32[3]{0:T(128)} %pad_add_fusion.info, bf16[256,4224]{1,0:T(8,128)(2,1)} %bitcast.14.refs_0_, bf16[4096,768]{1,0:T(8,128)(2,1)} %bitcast.29, bf16[4096,768]{1,0:T(8,128)(2,1)} %bitcast.34, bf16[768,4096]{1,0:T(8,128)(2,1)} %bitcast.39, bf16[4096,768]{1,0:T(8,128)(2,1)} %collective-permute-done.4.refs_4_, ...), custom_call_target="tpu_custom_call" | custom-call | flops 9663676416 | bytes 41943040 | tf_op jit(solution)/shard_map/pallas_call | solution.py:102
  147.5 3.8 %all-to-all-start.4 = ((bf16[4,64,4096]{2,1,0:T(8,128)(2,1)}), bf16[4,64,4096]{2,1,0:T(8,128)(2,1)S(1)}, u32[]{:S(2)}, u32[]{:S(2)}) async-start(bf16[4,64,4096]{2,1,0:T(8,128)(2,1)} %bitcast.44), calls=%async_computation.4 | async-start | bytes 4194304 | tf_op jit(solution)/shard_map/all_to_all | solution.py:289
  151.3 17.7 %shard_map.72 = bf16[256,4096]{1,0:T(8,128)(2,1)} custom-call(s32[3]{0:T(128)} %pad_add_fusion.info, bf16[256,4224]{1,0:T(8,128)(2,1)} %bitcast.12.refs_0_, bf16[4096,768]{1,0:T(8,128)(2,1)} %bitcast.30, bf16[4096,768]{1,0:T(8,128)(2,1)} %bitcast.35, bf16[768,4096]{1,0:T(8,128)(2,1)} %bitcast.40, bf16[4096,768]{1,0:T(8,128)(2,1)} %collective-permute-done.4.refs_4_, ...), custom_call_target="tpu_custom_call" | custom-call | flops 9663676416 | bytes 41943040 | tf_op jit(solution)/shard_map/pallas_call | solution.py:102
  169.0 6.4 %all-to-all-done.4 = bf16[4,64,4096]{2,1,0:T(8,128)(2,1)S(1)} async-done(((bf16[4,64,4096]{2,1,0:T(8,128)(2,1)}), bf16[4,64,4096]{2,1,0:T(8,128)(2,1)S(1)}, u32[]{:S(2)}, u32[]{:S(2)}) %all-to-all-start.4) | async-done | bytes 2097184 | tf_op jit(solution)/shard_map/all_to_all | solution.py:289
  175.4 1.4 copy-done.2
  176.8 3.6 %all-to-all-start.5 = ((bf16[4,64,4096]{2,1,0:T(8,128)(2,1)}), bf16[4,64,4096]{2,1,0:T(8,128)(2,1)S(1)}, u32[]{:S(2)}, u32[]{:S(2)}) async-start(bf16[4,64,4096]{2,1,0:T(8,128)(2,1)} %bitcast.43), calls=%async_computation.5 | async-start | bytes 4194304 | tf_op jit(solution)/shard_map/all_to_all | solution.py:289
  180.4 1.6 copy-done.3
  182.0 2.6 shard_map.73
  184.6 1.4 copy-done.4
  185.9 6.0 %collective-permute-start.8 = (bf16[128,4096]{1,0:T(8,128)(2,1)}, bf16[128,4096]{1,0:T(8,128)(2,1)S(1)}, u32[]{:S(2)}, u32[]{:S(2)}) collective-permute-start(bf16[128,4096]{1,0:T(8,128)(2,1)} %get-tuple-element.99), channel_id=1, source_target_pairs={{0,2},{6,4},{1,3},{7,5},{8,10},{14,12},{9,11},{15,13},{16,18},{22,... | collective-permute-start | bytes 3145736 | tf_op jit(solution)/shard_map/ppermute | solution.py:276
  191.9 12.7 %all-to-all-done.5 = bf16[4,64,4096]{2,1,0:T(8,128)(2,1)S(1)} async-done(((bf16[4,64,4096]{2,1,0:T(8,128)(2,1)}), bf16[4,64,4096]{2,1,0:T(8,128)(2,1)S(1)}, u32[]{:S(2)}, u32[]{:S(2)}) %all-to-all-start.5) | async-done | bytes 2097184 | tf_op jit(solution)/shard_map/all_to_all | solution.py:289
  204.7 1.4 copy-done
  206.1 3.6 %all-to-all-start.6 = ((bf16[4,64,4096]{2,1,0:T(8,128)(2,1)}), bf16[4,64,4096]{2,1,0:T(8,128)(2,1)S(1)}, u32[]{:S(2)}, u32[]{:S(2)}) async-start(bf16[4,64,4096]{2,1,0:T(8,128)(2,1)} %bitcast.42), calls=%async_computation.6 | async-start | bytes 4194304 | tf_op jit(solution)/shard_map/all_to_all | solution.py:289
  209.7 4.1 %collective-permute-done.8.refs_1_ = bf16[128,4096]{1,0:T(8,128)(2,1)S(1)} collective-permute-done((bf16[128,4096]{1,0:T(8,128)(2,1)}, bf16[128,4096]{1,0:T(8,128)(2,1)S(1)}, u32[]{:S(2)}, u32[]{:S(2)}) %collective-permute-start.8) | collective-permute-done | bytes 1048608 | tf_op jit(solution)/shard_map/ppermute | solution.py:276
  213.8 1.6 copy-done.1
  215.4 2.7 shard_map.74
  218.1 4.3 %collective-permute-start.10 = (bf16[128,4096]{1,0:T(8,128)(2,1)}, bf16[128,4096]{1,0:T(8,128)(2,1)S(1)}, u32[]{:S(2)}, u32[]{:S(2)}) collective-permute-start(bf16[128,4096]{1,0:T(8,128)(2,1)} %get-tuple-element.102), channel_id=1, source_target_pairs={{0,2},{6,4},{1,3},{7,5},{8,10},{14,12},{9,11},{15,13},{16,18},{22,... | collective-permute-start | bytes 3145736 | tf_op jit(solution)/shard_map/ppermute | solution.py:276
  222.4 1.6 collective-permute-start.9
  224.1 9.9 %all-to-all-done.6 = bf16[4,64,4096]{2,1,0:T(8,128)(2,1)S(1)} async-done(((bf16[4,64,4096]{2,1,0:T(8,128)(2,1)}), bf16[4,64,4096]{2,1,0:T(8,128)(2,1)S(1)}, u32[]{:S(2)}, u32[]{:S(2)}) %all-to-all-start.6) | async-done | bytes 2097184 | tf_op jit(solution)/shard_map/all_to_all | solution.py:289
  234.0 4.4 %all-to-all-start.7 = ((bf16[4,64,4096]{2,1,0:T(8,128)(2,1)}), bf16[4,64,4096]{2,1,0:T(8,128)(2,1)}, u32[]{:S(2)}, u32[]{:S(2)}) async-start(bf16[4,64,4096]{2,1,0:T(8,128)(2,1)} %bitcast.41), calls=%async_computation.7 | async-start | bytes 4194304 | tf_op jit(solution)/shard_map/all_to_all | solution.py:289
  238.4 4.9 %collective-permute-done.10.refs_3_ = bf16[128,4096]{1,0:T(8,128)(2,1)S(1)} collective-permute-done((bf16[128,4096]{1,0:T(8,128)(2,1)}, bf16[128,4096]{1,0:T(8,128)(2,1)S(1)}, u32[]{:S(2)}, u32[]{:S(2)}) %collective-permute-start.10) | collective-permute-done | bytes 1048608 | tf_op jit(solution)/shard_map/ppermute | solution.py:276
  243.3 1.6 copy-done.5
  244.9 3.4 %shard_map.75 = (bf16[128,4096]{1,0:T(8,128)(2,1)S(1)}, bf16[128,4096]{1,0:T(8,128)(2,1)S(1)}) custom-call(bf16[128,256]{1,0:T(8,128)(2,1)S(1)} %get-tuple-element.105.hi, bf16[128,256]{1,0:T(8,128)(2,1)S(1)} %get-tuple-element.106.mid, bf16[256,4096]{1,0:T(8,128)(2,1)S(1)} %bitcast.23, bf16[128,4096]{1,0:T(8,128)(2,1)} %collective-permute-done.9.refs_1_, ...), custom_call_target="tpu_custom_call" | custom-call | flops 536870912 | bytes 3145728 | tf_op jit(solution)/shard_map/pallas_call | solution.py:231
  248.3 3.8 %collective-permute-start.11 = (bf16[128,4096]{1,0:T(8,128)(2,1)S(1)}, bf16[128,4096]{1,0:T(8,128)(2,1)S(1)}, u32[]{:S(2)}, u32[]{:S(2)}) collective-permute-start(bf16[128,4096]{1,0:T(8,128)(2,1)S(1)} %get-tuple-element.109), channel_id=1, source_target_pairs={{0,2},{2,0},{4,6},{6,4},{1,3},{3,1},{5,7},{7,5},{8,10},{10,8},{12,... | collective-permute-start | bytes 3145736 | tf_op jit(solution)/shard_map/ppermute | solution.py:267
  252.9 19.8 %collective-permute-done.11.refs_1_ = bf16[128,4096]{1,0:T(8,128)(2,1)S(1)} collective-permute-done((bf16[128,4096]{1,0:T(8,128)(2,1)S(1)}, bf16[128,4096]{1,0:T(8,128)(2,1)S(1)}, u32[]{:S(2)}, u32[]{:S(2)}) %collective-permute-start.11) | collective-permute-done | bytes 1048608 | tf_op jit(solution)/shard_map/ppermute | solution.py:267
  272.6 4.2 %shard_map.76 = bf16[128,4096]{1,0:T(8,128)(2,1)} custom-call(bf16[128,256]{1,0:T(8,128)(2,1)S(1)} %get-tuple-element.76.hi, bf16[128,256]{1,0:T(8,128)(2,1)S(1)} %get-tuple-element.77.mid, bf16[256,4096]{1,0:T(8,128)(2,1)} %bitcast.22.refs_0_, bf16[128,4096]{1,0:T(8,128)(2,1)S(1)} %collective-permute-done.11.refs_1_, ...), custom_call_target="tpu_custom_call" | custom-call | flops 536870912 | bytes 3145728 | tf_op jit(solution)/shard_map/pallas_call | solution.py:231
  (34 shorter events, 5.0 us)
Async XLA Ops:
  1.6 1.2 copy-start.6
  2.9 27.1 %collective-permute-start.2 = (bf16[128,4224]{1,0:T(8,128)(2,1)S(1)}, bf16[128,4224]{1,0:T(8,128)(2,1)}, u32[]{:S(2)}, u32[]{:S(2)}) collective-permute-start(bf16[128,4224]{1,0:T(8,128)(2,1)S(1)} %shard_map.64.refs_0_), channel_id=1, source_target_pairs={{0,2},{2,0},{4,6},{6,4},{1,3},{3,1},{5,7},{7,5},{8,10},{10,8},{12,... | collective-permute-start | bytes 3244040 | tf_op jit(solution)/shard_map/ppermute | solution.py:267
  6.0 24.0 %collective-permute-start = (bf16[128,4224]{1,0:T(8,128)(2,1)S(1)}, bf16[128,4224]{1,0:T(8,128)(2,1)S(1)}, u32[]{:S(2)}, u32[]{:S(2)}) collective-permute-start(bf16[128,4224]{1,0:T(8,128)(2,1)S(1)} %shard_map.64.refs_0_), channel_id=1, source_target_pairs={{2,4},{4,2},{3,5},{5,3},{10,12},{12,10},{11,13},{13,11},{18,20},{2... | collective-permute-start | bytes 3244040 | tf_op jit(solution)/shard_map/ppermute | solution.py:270
  11.0 30.1 %all-to-all-start = ((bf16[4,64,4224]{2,1,0:T(8,128)(2,1)}), bf16[4,64,4224]{2,1,0:T(8,128)(2,1)}, u32[]{:S(2)}, u32[]{:S(2)}) async-start(bf16[4,64,4224]{2,1,0:T(8,128)(2,1)} %bitcast.4), calls=%async_computation | async-start | bytes 4325376 | tf_op jit(solution)/shard_map/all_to_all | solution.py:289
  15.4 59.7 %collective-permute-start.4 = (bf16[4096,768]{1,0:T(8,128)(2,1)}, bf16[4096,768]{1,0:T(8,128)(2,1)}, u32[]{:S(2)}, u32[]{:S(2)}) collective-permute-start(bf16[4096,768]{1,0:T(8,128)(2,1)} %bitcast.26), channel_id=1, source_target_pairs={{0,8},{8,0},{1,9},{9,1},{2,10},{10,2},{3,11},{11,3},{4,12},{12,4},... | collective-permute-start | bytes 18874376 | tf_op jit(solution)/shard_map/ppermute | solution.py:284
  15.5 59.6 %collective-permute-start.5 = (bf16[4096,768]{1,0:T(8,128)(2,1)}, bf16[4096,768]{1,0:T(8,128)(2,1)}, u32[]{:S(2)}, u32[]{:S(2)}) collective-permute-start(bf16[4096,768]{1,0:T(8,128)(2,1)} %bitcast.31), channel_id=1, source_target_pairs={{0,8},{8,0},{1,9},{9,1},{2,10},{10,2},{3,11},{11,3},{4,12},{12,4},... | collective-permute-start | bytes 18874376 | tf_op jit(solution)/shard_map/ppermute | solution.py:284
  16.0 59.1 %collective-permute-start.6 = (bf16[768,4096]{1,0:T(8,128)(2,1)}, bf16[768,4096]{1,0:T(8,128)(2,1)}, u32[]{:S(2)}, u32[]{:S(2)}) collective-permute-start(bf16[768,4096]{1,0:T(8,128)(2,1)} %bitcast.36), channel_id=1, source_target_pairs={{0,8},{8,0},{1,9},{9,1},{2,10},{10,2},{3,11},{11,3},{4,12},{12,4},... | collective-permute-start | bytes 18874376 | tf_op jit(solution)/shard_map/ppermute | solution.py:284
  30.0 6.1 %copy-start.7 = (bf16[128,4224]{1,0:T(8,128)(2,1)}, bf16[128,4224]{1,0:T(8,128)(2,1)S(1)}, u32[]{:S(2)}) copy-start(bf16[128,4224]{1,0:T(8,128)(2,1)S(1)} %collective-permute-done.refs_1_) | copy-start | bytes 3244036
  30.0 29.1 %collective-permute-start.1 = (bf16[128,4224]{1,0:T(8,128)(2,1)S(1)}, bf16[128,4224]{1,0:T(8,128)(2,1)}, u32[]{:S(2)}, u32[]{:S(2)}) collective-permute-start(bf16[128,4224]{1,0:T(8,128)(2,1)S(1)} %collective-permute-done.refs_1_), channel_id=1, source_target_pairs={{2,0},{4,6},{3,1},{5,7},{10,8},{12,14},{11,9},{13,15},{18,16},{20,... | collective-permute-start | bytes 3244040 | tf_op jit(solution)/shard_map/ppermute | solution.py:273
  31.2 14.3 %collective-permute-start.3 = (bf16[128,4224]{1,0:T(8,128)(2,1)}, bf16[128,4224]{1,0:T(8,128)(2,1)S(1)}, u32[]{:S(2)}, u32[]{:S(2)}) collective-permute-start(bf16[128,4224]{1,0:T(8,128)(2,1)} %collective-permute-done.2.refs_0_), channel_id=1, source_target_pairs={{2,4},{4,2},{3,5},{5,3},{10,12},{12,10},{11,13},{13,11},{18,20},{2... | collective-permute-start | bytes 3244040 | tf_op jit(solution)/shard_map/ppermute | solution.py:270
  41.1 29.6 %all-to-all-start.1 = ((bf16[4,64,4224]{2,1,0:T(8,128)(2,1)}), bf16[4,64,4224]{2,1,0:T(8,128)(2,1)}, u32[]{:S(2)}, u32[]{:S(2)}) async-start(bf16[4,64,4224]{2,1,0:T(8,128)(2,1)} %bitcast.6), calls=%async_computation.1 | async-start | bytes 4325376 | tf_op jit(solution)/shard_map/all_to_all | solution.py:289
  45.6 47.4 %collective-permute-start.7 = (bf16[128,4224]{1,0:T(8,128)(2,1)S(1)}, bf16[128,4224]{1,0:T(8,128)(2,1)}, u32[]{:S(2)}, u32[]{:S(2)}) collective-permute-start(bf16[128,4224]{1,0:T(8,128)(2,1)S(1)} %collective-permute-done.3.refs_1_), channel_id=1, source_target_pairs={{2,0},{4,6},{3,1},{5,7},{10,8},{12,14},{11,9},{13,15},{18,16},{20,... | collective-permute-start | bytes 3244040 | tf_op jit(solution)/shard_map/ppermute | solution.py:273
  70.6 29.6 %all-to-all-start.2 = ((bf16[4,64,4224]{2,1,0:T(8,128)(2,1)}), bf16[4,64,4224]{2,1,0:T(8,128)(2,1)}, u32[]{:S(2)}, u32[]{:S(2)}) async-start(bf16[4,64,4224]{2,1,0:T(8,128)(2,1)} %bitcast.11), calls=%async_computation.2 | async-start | bytes 4325376 | tf_op jit(solution)/shard_map/all_to_all | solution.py:289
  75.1 17.8 %copy-start.8 = (bf16[128,4224]{1,0:T(8,128)(2,1)S(1)}, bf16[128,4224]{1,0:T(8,128)(2,1)}, u32[]{:S(2)}) copy-start(bf16[128,4224]{1,0:T(8,128)(2,1)} %copy-done.7) | copy-start | bytes 3244036
  100.2 29.5 %all-to-all-start.3 = ((bf16[4,64,4224]{2,1,0:T(8,128)(2,1)}), bf16[4,64,4224]{2,1,0:T(8,128)(2,1)}, u32[]{:S(2)}, u32[]{:S(2)}) async-start(bf16[4,64,4224]{2,1,0:T(8,128)(2,1)} %bitcast.13), calls=%async_computation.3 | async-start | bytes 4325376 | tf_op jit(solution)/shard_map/all_to_all | solution.py:289
  147.5 27.9 %all-to-all-start.4 = ((bf16[4,64,4096]{2,1,0:T(8,128)(2,1)}), bf16[4,64,4096]{2,1,0:T(8,128)(2,1)S(1)}, u32[]{:S(2)}, u32[]{:S(2)}) async-start(bf16[4,64,4096]{2,1,0:T(8,128)(2,1)} %bitcast.44), calls=%async_computation.4 | async-start | bytes 4194304 | tf_op jit(solution)/shard_map/all_to_all | solution.py:289
  175.4 1.4 copy-start.2
  176.8 27.9 %all-to-all-start.5 = ((bf16[4,64,4096]{2,1,0:T(8,128)(2,1)}), bf16[4,64,4096]{2,1,0:T(8,128)(2,1)S(1)}, u32[]{:S(2)}, u32[]{:S(2)}) async-start(bf16[4,64,4096]{2,1,0:T(8,128)(2,1)} %bitcast.43), calls=%async_computation.5 | async-start | bytes 4194304 | tf_op jit(solution)/shard_map/all_to_all | solution.py:289
  180.4 1.6 copy-start.3
  184.6 1.4 copy-start.4
  185.9 27.8 %collective-permute-start.8 = (bf16[128,4096]{1,0:T(8,128)(2,1)}, bf16[128,4096]{1,0:T(8,128)(2,1)S(1)}, u32[]{:S(2)}, u32[]{:S(2)}) collective-permute-start(bf16[128,4096]{1,0:T(8,128)(2,1)} %get-tuple-element.99), channel_id=1, source_target_pairs={{0,2},{6,4},{1,3},{7,5},{8,10},{14,12},{9,11},{15,13},{16,18},{22,... | collective-permute-start | bytes 3145736 | tf_op jit(solution)/shard_map/ppermute | solution.py:276
  204.7 1.4 copy-start
  206.1 27.9 %all-to-all-start.6 = ((bf16[4,64,4096]{2,1,0:T(8,128)(2,1)}), bf16[4,64,4096]{2,1,0:T(8,128)(2,1)S(1)}, u32[]{:S(2)}, u32[]{:S(2)}) async-start(bf16[4,64,4096]{2,1,0:T(8,128)(2,1)} %bitcast.42), calls=%async_computation.6 | async-start | bytes 4194304 | tf_op jit(solution)/shard_map/all_to_all | solution.py:289
  213.8 1.6 copy-start.1
  218.1 25.2 %collective-permute-start.10 = (bf16[128,4096]{1,0:T(8,128)(2,1)}, bf16[128,4096]{1,0:T(8,128)(2,1)S(1)}, u32[]{:S(2)}, u32[]{:S(2)}) collective-permute-start(bf16[128,4096]{1,0:T(8,128)(2,1)} %get-tuple-element.102), channel_id=1, source_target_pairs={{0,2},{6,4},{1,3},{7,5},{8,10},{14,12},{9,11},{15,13},{16,18},{22,... | collective-permute-start | bytes 3145736 | tf_op jit(solution)/shard_map/ppermute | solution.py:276
  222.4 20.9 %collective-permute-start.9 = (bf16[128,4096]{1,0:T(8,128)(2,1)}, bf16[128,4096]{1,0:T(8,128)(2,1)}, u32[]{:S(2)}, u32[]{:S(2)}) collective-permute-start(bf16[128,4096]{1,0:T(8,128)(2,1)} %get-tuple-element.103), channel_id=1, source_target_pairs={{2,4},{4,2},{3,5},{5,3},{10,12},{12,10},{11,13},{13,11},{18,20},{2... | collective-permute-start | bytes 3145736 | tf_op jit(solution)/shard_map/ppermute | solution.py:270
  234.0 38.6 %all-to-all-start.7 = ((bf16[4,64,4096]{2,1,0:T(8,128)(2,1)}), bf16[4,64,4096]{2,1,0:T(8,128)(2,1)}, u32[]{:S(2)}, u32[]{:S(2)}) async-start(bf16[4,64,4096]{2,1,0:T(8,128)(2,1)} %bitcast.41), calls=%async_computation.7 | async-start | bytes 4194304 | tf_op jit(solution)/shard_map/all_to_all | solution.py:289
  243.3 1.6 copy-start.5
  248.3 24.3 %collective-permute-start.11 = (bf16[128,4096]{1,0:T(8,128)(2,1)S(1)}, bf16[128,4096]{1,0:T(8,128)(2,1)S(1)}, u32[]{:S(2)}, u32[]{:S(2)}) collective-permute-start(bf16[128,4096]{1,0:T(8,128)(2,1)S(1)} %get-tuple-element.109), channel_id=1, source_target_pairs={{0,2},{2,0},{4,6},{6,4},{1,3},{3,1},{5,7},{7,5},{8,10},{10,8},{12,... | collective-permute-start | bytes 3145736 | tf_op jit(solution)/shard_map/ppermute | solution.py:267
  252.1 20.5 %collective-permute-start.12 = (bf16[128,4096]{1,0:T(8,128)(2,1)S(1)}, bf16[128,4096]{1,0:T(8,128)(2,1)S(1)}, u32[]{:S(2)}, u32[]{:S(2)}) collective-permute-start(bf16[128,4096]{1,0:T(8,128)(2,1)S(1)} %get-tuple-element.110), channel_id=1, source_target_pairs={{2,4},{4,2},{3,5},{5,3},{10,12},{12,10},{11,13},{13,11},{18,20},{2... | collective-permute-start | bytes 3145736 | tf_op jit(solution)/shard_map/ppermute | solution.py:270

commit v5 on v4

--- a/solution.py
+++ b/solution.py
@@ -11,6 +11,7 @@
 BF16 = jnp.bfloat16
 EXTRA = 128
 MIB = 2**20
+PERMUTED = (2, 3)
 ROUTE_COST = 400
 MIX_COST = 4
 
@@ -19,16 +20,20 @@
     return next(d for d in range(min(size, most), 0, -1) if size % d == 0)
 
 
-def experts_kernel(info, *refs, parts, rows, top, tile, span):
-    x_hbm, refs = refs[:parts], refs[parts:]
+def experts_kernel(info, *refs, given, parts, rows, top, tile, span):
+    x_hbm, refs = refs[:given], refs[given:]
     (g0, u0, d0, g1, u1, d1), refs = refs[:6], refs[6:]
     o_hbm, refs = refs[:parts], refs[parts:]
     x_ref, bg0, bu0, bd0, bg1, bu1, bd1, gate_ref, hid, o_ref, sems, out_sems = refs
     total, width = o_ref.shape
     ff = g0.shape[1]
     spans = width // span
-    held = [pl.ds(p * (total // parts), total // parts) for p in range(parts)]
-    x_copies = [pltpu.make_async_copy(x_hbm[p], x_ref.at[held[p]], sems.at[4 + 2 * spans + p]) for p in range(parts)]
+    each = total // parts
+    held = [pl.ds(pl.multiple_of((info[3] ^ p) * each, each), each) if parts > 1 else pl.ds(0, total) for p in range(parts)]
+    if given == 1:
+        x_copies = [pltpu.make_async_copy(x_hbm[0], x_ref, sems.at[4 + 2 * spans])]
+    else:
+        x_copies = [pltpu.make_async_copy(x_hbm[p], x_ref.at[held[p]], sems.at[4 + 2 * spans + p]) for p in range(parts)]
     for c in x_copies:
         c.start()
     ins = [pltpu.make_async_copy(src, dst, sems.at[n]) for n, (src, dst) in enumerate(((g0, bg0), (u0, bu0), (g1, bg1), (u1, bu1)))]
@@ -92,25 +97,26 @@
         c.wait()
 
 
-def experts_apply(info, xs, first, second, rows, top):
+def experts_apply(info, xs, first, second, parts, rows, top):
     width, ff = first[0].shape
-    parts, each = len(xs), xs[0].shape[0]
-    total = parts * each
+    given = len(xs)
+    total = given * xs[0].shape[0]
+    each = total // parts
     span = divisor(width // 128, 8) * 128
     spans = width // span
     anywhere = pl.BlockSpec(memory_space=pl.ANY)
     return pl.pallas_call(
-        partial(experts_kernel, parts=parts, rows=rows, top=top, tile=divisor(ff // 128, 2) * 128, span=span),
+        partial(experts_kernel, given=given, parts=parts, rows=rows, top=top, tile=divisor(ff // 128, 2) * 128, span=span),
         out_shape=[jax.ShapeDtypeStruct((each, width), BF16)] * parts,
         grid_spec=pltpu.PrefetchScalarGridSpec(
             num_scalar_prefetch=1,
             grid=(1,),
-            in_specs=[anywhere] * (parts + 6),
+            in_specs=[anywhere] * (given + 6),
             out_specs=[anywhere] * parts,
             scratch_shapes=[pltpu.VMEM((total, xs[0].shape[1]), BF16)]
             + [pltpu.VMEM(w.shape, BF16) for w in first + second]
             + [pltpu.VMEM((total, ff), F32), pltpu.VMEM((total, 2 * ff), BF16), pltpu.VMEM((total, width), BF16)]
-            + [pltpu.SemaphoreType.DMA((4 + 2 * spans + parts,)), pltpu.SemaphoreType.DMA((spans, parts))],
+            + [pltpu.SemaphoreType.DMA((4 + 2 * spans + given,)), pltpu.SemaphoreType.DMA((spans, parts))],
         ),
         compiler_params=pltpu.CompilerParams(vmem_limit_bytes=54 * MIB),
         cost_estimate=pl.CostEstimate(
@@ -139,8 +145,8 @@
     )(tokens, ids, weights)
 
 
-def route_kernel(flag, plane, *refs, choices, parts, rows, top, width):
-    blocks, outs, (mix_hi, mix_mid) = refs[:choices], refs[choices : choices + parts], refs[choices + parts :]
+def route_kernel(flag, plane, *refs, choices, sends, relative, rows, top, width):
+    blocks, outs, (mix_hi, mix_mid) = refs[:choices], refs[choices : choices + sends], refs[choices + sends :]
 
     def block(s):
         value = blocks[0][:, s]
@@ -172,41 +178,46 @@
     rank = jnp.where(chosen > 0.0, rank, -1.0)
     at = (lax.broadcasted_iota(jnp.int32, (count, lanes), 1) % rows).astype(F32)
     taken = jnp.zeros((count, lanes), F32)
-    sum_hi, sum_mid = taken, taken
+    sum_hi, sum_mid, taken_back = taken, taken, taken
     for side in range(2):
         spread = table((128, lanes), lambda r, c: r == 2 * (c // rows) + side)
         hit = dot(rank, spread) == at
         taken = jnp.where(hit, 1.0, taken)
+        if relative:
+            spread = table((128, lanes), lambda r, c: r == 2 * ((c // rows) ^ flag[1]) + side)
+            hit = dot(rank, spread) == at
+            if sends > 1:
+                taken_back = jnp.where(hit, 1.0, taken_back)
         sum_hi = jnp.where(hit, dot(w_hi, spread), sum_hi)
         sum_mid = jnp.where(hit, dot(w_mid, spread), sum_mid)
     mix_hi[...] = sum_hi.astype(BF16)
     mix_mid[...] = sum_mid.astype(BF16)
-    taken = taken.astype(BF16)
+    taken = (taken_back if sends > 1 else taken).astype(BF16)
+    each = lanes // sends
     step = divisor((width + EXTRA) // 128, 11) * 128
-    each = lanes // parts
     for n in range((width + EXTRA) // step):
         s = slice(n * step, (n + 1) * step)
         got = lax.dot_general(taken, block(s), (((0,), (0,)), ((), ())), preferred_element_type=F32).astype(BF16)
-        for p in range(parts):
+        for p in range(sends):
             outs[p][:, s] = got[p * each : (p + 1) * each]
 
 
-def route(flag, plane, blocks, parts, rows, top):
+def route(flag, plane, blocks, sends, relative, rows, top):
     count, wide = blocks[0].shape
-    lanes = parts * rows if parts > 1 else plane.shape[0] * rows
-    each = lanes // parts
-    chips = lanes // rows
+    chips = plane.shape[0]
+    lanes = chips * rows
     ids = jnp.full((8, 128), -1.0, F32).at[:, : 2 * chips].set(plane.reshape(1, -1))
     whole = pl.BlockSpec(memory_space=pltpu.VMEM)
     out = pl.pallas_call(
-        partial(route_kernel, choices=len(blocks), parts=parts, rows=rows, top=top, width=wide - EXTRA),
+        partial(route_kernel, choices=len(blocks), sends=sends, relative=relative, rows=rows, top=top, width=wide - EXTRA),
         in_specs=[pl.BlockSpec(memory_space=pltpu.SMEM), whole] + [whole] * len(blocks),
-        out_specs=[whole] * (parts + 2),
-        out_shape=[jax.ShapeDtypeStruct((each, wide), BF16)] * parts + [jax.ShapeDtypeStruct((count, lanes), BF16)] * 2,
+        out_specs=[whole] * (sends + 2),
+        out_shape=[jax.ShapeDtypeStruct((lanes // sends, wide), BF16)] * sends
+        + [jax.ShapeDtypeStruct((count, lanes), BF16)] * 2,
         compiler_params=pltpu.CompilerParams(vmem_limit_bytes=24 * MIB),
         cost_estimate=pl.CostEstimate(flops=ROUTE_COST * count * lanes * wide, bytes_accessed=2 * (count + lanes) * wide, transcendentals=0),
     )(flag, ids, *blocks)
-    return out[:parts], out[parts:]
+    return out[:sends], out[sends:]
 
 
 def mix_kernel(hi, mid, *refs, parts, terms):
@@ -254,14 +265,13 @@
     rows = count * top // (y_size * lane_count)
     z_at = lax.axis_index("z")
 
-    parts = 1
+    parts = chips if chips in (2, 4) else 1
     here = lax.axis_index("y") * x_size + lax.axis_index("x")
     chip = jnp.arange(chips, dtype=jnp.int32)
-    chip = chip ^ here if parts > 1 else chip
     low = 2 * (chip // x_size) * lane_count + z_at * x_size + chip % x_size
     plane = jnp.stack([low, low + lane_count], axis=-1).astype(F32)
     low_here = 2 * lax.axis_index("y") * lane_count + z_at * x_size + lax.axis_index("x")
-    info = jnp.stack([low_here, low_here + lane_count, lax.axis_index("core")]).astype(jnp.int32)
+    info = jnp.stack([low_here, low_here + lane_count, lax.axis_index("core"), here]).astype(jnp.int32)
 
     def flip(value, mask):
         return lax.ppermute(value, "z", [(i, i ^ mask) for i in range(z_size)])
@@ -278,20 +288,20 @@
     is_end = (z_at == 0) | (z_at == z_size - 1)
 
     block = pack(tokens, expert_ids, router_weights)
-    flag = is_end.astype(jnp.int32).reshape(1)
+    flag = jnp.stack([is_end.astype(jnp.int32), here])
     swap = [(0, 1), (1, 0)]
     own = [gate_weight[0], up_weight[0], down_weight[0]]
     other = [lax.ppermute(w, "core", swap) for w in own]
 
     def exchange(values):
-        if parts == 1:
+        if len(values) == 1:
             value = values[0].reshape(chips, rows, values[0].shape[1])
             return [lax.all_to_all(value, ("y", "x"), 0, 0, tiled=True).reshape(values[0].shape)]
         pairs = [[(i, i ^ m) for i in range(chips)] for m in range(chips)]
         return [values[0]] + [lax.ppermute(values[m], ("y", "x"), pairs[m]) for m in range(1, chips)]
 
     def run(k, *others):
-        outs[k] = experts_apply(info, after(arrived[k], *others), own, other, rows, top)
+        outs[k] = experts_apply(info, after(arrived[k], *others), own, other, parts, rows, top)
 
     line = z_size == 4
     moving = {k: flip(block, k) for k in ((1,) if line else range(1, z_size)) if k & (k - 1) == 0}
@@ -312,8 +322,9 @@
         elif k:
             bit = k & -k
             held[k] = [after(moving[k] if k == bit else flip(held[k ^ bit][0], bit), sent[k - 1])]
-        sent[k], mixes[k] = route(flag, plane, held[k], parts, rows, top)
-        if k and parts == 1:
+        sends = parts if k in PERMUTED else 1
+        sent[k], mixes[k] = route(flag, plane, held[k], sends, parts > 1, rows, top)
+        if k and sends == 1:
             sent[k] = after(sent[k], arrived[k - 1])
         if k > 1:
             run(k - 2, sent[k])

time: 279 us -> 251 us (0.90)
  starting transfers between devices: 57.8 us -> 48.7 us
  waiting for transfers between devices: 106 us -> 98.4 us
  Pallas kernels: 98.5 us -> 92.8 us
  local copies, waits for them, and re-layouts: 11.8 us -> 6.15 us
    ppermute x0 -> x18, waiting for transfers between devices: none -> 65.1 us  [exchange(): lax.ppermute(values[m], ('y', 'x'), pairs[m])]
    all_to_all x8 -> x2, waiting for transfers between devices: 52.1 us -> 5.51 us  [exchange(): lax.all_to_all(value, ('y', 'x'), 0, 0, tiled=True).reshape(values[0].shape)]
    all_to_all x8 -> x2, starting transfers between devices: 33.5 us -> 8.93 us  [exchange(): lax.all_to_all(value, ('y', 'x'), 0, 0, tiled=True).reshape(values[0].shape)]
    ppermute x0 -> x18, starting transfers between devices: none -> 23.7 us  [exchange(): lax.ppermute(values[m], ('y', 'x'), pairs[m])]
    ppermute x2, waiting for transfers between devices: 33.1 us -> 12.6 us  [flip(): return lax.ppermute(value, 'z', [(i, i ^ mask) for i in range(z_size)])]
    ppermute x2, waiting for transfers between devices: 8.96 us -> 0.01 us  [inward(): return lax.ppermute(value, 'z', [(0, 1), (3, 2)])]
    unnamed x20 -> x40, local copies, waits for them, and re-layouts: 11.7 us -> 6.05 us
    pallas_call x4, Pallas kernels: 12.8 us -> 8.23 us  [mix_rows(): pl.pallas_call(partial(mix_kernel, parts=len(backs), terms=tuple(terms)),...]
  transfers between devices with their start and end apart: 21 -> 33, of which waited for: 12 -> 12; matrix products, arithmetic and copies ran while one was open for 1% -> 1% of each run, Pallas kernels for 28% -> 34%
where the time goes in v5:
time: 251 us; the launch traced here: 249 us
  waiting for transfers between devices  98.4 us (39%)
  Pallas kernels  92.8 us (37%)
  starting transfers between devices  48.7 us (19%)
  local copies, waits for them, and re-layouts  6.15 us (2%)
    pallas_call x4, Pallas kernels, experts_apply(): pl.pallas_call(partial(experts_kernel, given=given, parts=parts, rows=row...  71.7 us
    ppermute x18, waiting for transfers between devices, exchange(): lax.ppermute(values[m], ('y', 'x'), pairs[m])  65.1 us
    ppermute x18, starting transfers between devices, exchange(): lax.ppermute(values[m], ('y', 'x'), pairs[m])  23.7 us
    ppermute x2, waiting for transfers between devices, outward(): return lax.ppermute(value, 'z', [(1, 0), (2, 3)])  15.3 us
    pallas_call x4, Pallas kernels, route(): pl.pallas_call(partial(route_kernel, choices=len(blocks), sends=sends, re...  12.8 us
    ppermute x2, waiting for transfers between devices, flip(): return lax.ppermute(value, 'z', [(i, i ^ mask) for i in range(z_size)])  12.6 us
    all_to_all x2, starting transfers between devices, exchange(): lax.all_to_all(value, ('y', 'x'), 0, 0, tiled=True).reshape(values[0].shape)  8.93 us
    pallas_call x4, Pallas kernels, mix_rows(): pl.pallas_call(partial(mix_kernel, parts=len(backs), terms=tuple(terms)),...  8.23 us
  transfers between devices with their start and end apart: 33, of which 12 were waited for; matrix products, arithmetic and copies ran while one was open for 1% of the time, Pallas kernels for 34%

profile of v5, /device:TPU:0, one launch (start us, length us, event | category | flops | bytes accessed | tf_op | source)
XLA Modules:
  0.0 248.5 jit_solution(2280342297787181592)
XLA Ops:
  1.6 1.2 copy-done
  2.9 3.1 %collective-permute-start.2 = (bf16[128,4224]{1,0:T(8,128)(2,1)S(1)}, bf16[128,4224]{1,0:T(8,128)(2,1)S(1)}, u32[]{:S(2)}, u32[]{:S(2)}) collective-permute-start(bf16[128,4224]{1,0:T(8,128)(2,1)S(1)} %shard_map.64.refs_0_), channel_id=1, source_target_pairs={{0,2},{2,0},{4,6},{6,4},{1,3},{3,1},{5,7},{7,5},{8,10},{10,8},{12,... | collective-permute-start | bytes 3244040 | tf_op jit(solution)/shard_map/ppermute | solution.py:277
  8.3 3.4 %shard_map.65 = (bf16[256,4224]{1,0:T(8,128)(2,1)}, bf16[128,256]{1,0:T(8,128)(2,1)S(1)}, bf16[128,256]{1,0:T(8,128)(2,1)S(1)}) custom-call(s32[2]{0:T(128)S(1)} %pad_add_fusion.flag, f32[8,128]{1,0:T(8,128)S(1)} %scatter.9.plane, bf16[128,4224]{1,0:T(8,128)(2,1)S(1)} %shard_map.64.refs_0_), custom_call_target="tpu_custom_call" | custom-call | flops 55364812800 | bytes 3244032 | tf_op jit(solution)/shard_map/pallas_call | solution.py:211
  11.6 4.4 %all-to-all-start = ((bf16[4,64,4224]{2,1,0:T(8,128)(2,1)}), bf16[4,64,4224]{2,1,0:T(8,128)(2,1)}, u32[]{:S(2)}, u32[]{:S(2)}) async-start(bf16[4,64,4224]{2,1,0:T(8,128)(2,1)} %bitcast.5), calls=%async_computation | async-start | bytes 4325376 | tf_op jit(solution)/shard_map/all_to_all | solution.py:299
  17.3 12.6 %collective-permute-done.2.refs_0_ = bf16[128,4224]{1,0:T(8,128)(2,1)S(1)} collective-permute-done((bf16[128,4224]{1,0:T(8,128)(2,1)S(1)}, bf16[128,4224]{1,0:T(8,128)(2,1)S(1)}, u32[]{:S(2)}, u32[]{:S(2)}) %collective-permute-start.2) | collective-permute-done | bytes 1081376 | tf_op jit(solution)/shard_map/ppermute | solution.py:277
  29.8 1.3 collective-permute-start.1
  31.1 1.6 collective-permute-start.3
  32.8 3.4 %shard_map.66 = (bf16[256,4224]{1,0:T(8,128)(2,1)}, bf16[128,256]{1,0:T(8,128)(2,1)S(1)}, bf16[128,256]{1,0:T(8,128)(2,1)S(1)}) custom-call(s32[2]{0:T(128)S(1)} %pad_add_fusion.flag, f32[8,128]{1,0:T(8,128)S(1)} %scatter.9.plane, bf16[128,4224]{1,0:T(8,128)(2,1)S(1)} %collective-permute-done.2.refs_0_), custom_call_target="tpu_custom_call" | custom-call | flops 55364812800 | bytes 3244032 | tf_op jit(solution)/shard_map/pallas_call | solution.py:211
  36.2 5.5 %all-to-all-done = bf16[4,64,4224]{2,1,0:T(8,128)(2,1)} async-done(((bf16[4,64,4224]{2,1,0:T(8,128)(2,1)}), bf16[4,64,4224]{2,1,0:T(8,128)(2,1)}, u32[]{:S(2)}, u32[]{:S(2)}) %all-to-all-start) | async-done | bytes 2162720 | tf_op jit(solution)/shard_map/all_to_all | solution.py:299
  41.7 4.5 %all-to-all-start.1 = ((bf16[4,64,4224]{2,1,0:T(8,128)(2,1)}), bf16[4,64,4224]{2,1,0:T(8,128)(2,1)}, u32[]{:S(2)}, u32[]{:S(2)}) async-start(bf16[4,64,4224]{2,1,0:T(8,128)(2,1)} %bitcast.10), calls=%async_computation.1 | async-start | bytes 4325376 | tf_op jit(solution)/shard_map/all_to_all | solution.py:299
  46.2 1.3 collective-permute-start.10
  47.5 11.6 %collective-permute-done.1.refs_0_ = bf16[128,4224]{1,0:T(8,128)(2,1)} collective-permute-done((bf16[128,4224]{1,0:T(8,128)(2,1)S(1)}, bf16[128,4224]{1,0:T(8,128)(2,1)}, u32[]{:S(2)}, u32[]{:S(2)}) %collective-permute-start.1) | collective-permute-done | bytes 1081376 | tf_op jit(solution)/shard_map/ppermute | solution.py:283
  59.1 2.9 %shard_map.67 = (bf16[64,4224]{1,0:T(8,128)(2,1)S(1)}, bf16[64,4224]{1,0:T(8,128)(2,1)S(1)}, bf16[64,4224]{1,0:T(8,128)(2,1)S(1)}, bf16[64,4224]{1,0:T(8,128)(2,...) custom-call(s32[2]{0:T(128)S(1)} %pad_add_fusion.flag, f32[8,128]{1,0:T(8,128)S(1)} %scatter.9.plane, ...), custom_call_target="tpu_custom_call" | custom-call | flops 55364812800 | bytes 3244032 | tf_op jit(solution)/shard_map/pallas_call | solution.py:211
  62.8 1.5 collective-permute-start.7
  64.3 1.5 collective-permute-start.8
  65.8 17.8 %shard_map.68 = (bf16[64,4096]{1,0:T(8,128)(2,1)}, bf16[64,4096]{1,0:T(8,128)(2,1)}, bf16[64,4096]{1,0:T(8,128)(2,1)}, bf16[64,4096]{1,0:T(8,128)(2,1)}) custom-call(s32[4]{0:T(128)} %pad_add_fusion.1.info, bf16[256,4224]{1,0:T(8,128)(2,1)} %bitcast.6.refs_0_, bf16[4096,768]{1,0:T(8,128)(2,1)} %bitcast.13, bf16[4096,768]{1,0:T(8,128)(2,1)} %bitcast.18, ...), custom_call_target="tpu_custom_call" | custom-call | flops 9663676416 | bytes 41943040 | tf_op jit(solution)/shard_map/pallas_call | solution.py:108
  83.7 3.7 %collective-permute-done.10.refs_0_ = bf16[128,4224]{1,0:T(8,128)(2,1)S(1)} collective-permute-done((bf16[128,4224]{1,0:T(8,128)(2,1)}, bf16[128,4224]{1,0:T(8,128)(2,1)S(1)}, u32[]{:S(2)}, u32[]{:S(2)}) %collective-permute-start.10) | collective-permute-done | bytes 1081376 | tf_op jit(solution)/shard_map/ppermute | solution.py:283
  87.4 3.1 %shard_map.69 = (bf16[64,4224]{1,0:T(8,128)(2,1)S(1)}, bf16[64,4224]{1,0:T(8,128)(2,1)}, bf16[64,4224]{1,0:T(8,128)(2,1)}, bf16[64,4224]{1,0:T(8,128)(2,1)}, bf1...) custom-call(s32[2]{0:T(128)S(1)} %pad_add_fusion.flag, f32[8,128]{1,0:T(8,128)S(1)} %scatter.9.plane, ...), custom_call_target="tpu_custom_call" | custom-call | flops 55364812800 | bytes 3244032 | tf_op jit(solution)/shard_map/pallas_call | solution.py:211
  90.4 0.8 copy-done.2
  91.2 1.5 collective-permute-start.11
  92.7 1.5 collective-permute-start.12
  94.7 17.8 %shard_map.70 = (bf16[64,4096]{1,0:T(8,128)(2,1)}, bf16[64,4096]{1,0:T(8,128)(2,1)}, bf16[64,4096]{1,0:T(8,128)(2,1)}, bf16[64,4096]{1,0:T(8,128)(2,1)}) custom-call(s32[4]{0:T(128)} %pad_add_fusion.1.info, bf16[256,4224]{1,0:T(8,128)(2,1)} %bitcast.11.refs_0_, bf16[4096,768]{1,0:T(8,128)(2,1)} %bitcast.14, bf16[4096,768]{1,0:T(8,128)(2,1)} %bitcast.19, ...), custom_call_target="tpu_custom_call" | custom-call | flops 9663676416 | bytes 41943040 | tf_op jit(solution)/shard_map/pallas_call | solution.py:108
  112.6 2.5 %collective-permute-start.9 = (bf16[64,4224]{1,0:T(8,128)(2,1)S(1)}, bf16[64,4224]{1,0:T(8,128)(2,1)S(1)}, u32[]{:S(2)}, u32[]{:S(2)}) collective-permute-start(bf16[64,4224]{1,0:T(8,128)(2,1)S(1)} %get-tuple-element.127), channel_id=1, source_target_pairs={{0,17},{1,16},{16,1},{17,0},{2,19},{3,18},{18,3},{19,2},{4,21},{5,... | collective-permute-start | bytes 1622024 | tf_op jit(solution)/shard_map/ppermute | solution.py:301
  115.1 12.4 %collective-permute-done.12.refs_2_ = bf16[64,4224]{1,0:T(8,128)(2,1)S(1)} collective-permute-done((bf16[64,4224]{1,0:T(8,128)(2,1)}, bf16[64,4224]{1,0:T(8,128)(2,1)S(1)}, u32[]{:S(2)}, u32[]{:S(2)}) %collective-permute-start.12) | collective-permute-done | bytes 540704 | tf_op jit(solution)/shard_map/ppermute | solution.py:301
  127.5 0.8 copy-done.9
  128.3 18.1 %shard_map.71 = (bf16[64,4096]{1,0:T(8,128)(2,1)}, bf16[64,4096]{1,0:T(8,128)(2,1)}, bf16[64,4096]{1,0:T(8,128)(2,1)}, bf16[64,4096]{1,0:T(8,128)(2,1)}) custom-call(s32[4]{0:T(128)} %pad_add_fusion.1.info, bf16[64,4224]{1,0:T(8,128)(2,1)} %copy-done.2, bf16[64,4224]{1,0:T(8,128)(2,1)} %copy-done.8, bf16[64,4224]{1,0:T(8,128)(2,1)} %copy-done.9, ...), custom_call_target="tpu_custom_call" | custom-call | flops 9663676416 | bytes 41943040 | tf_op jit(solution)/shard_map/pallas_call | solution.py:108
  146.5 2.0 collective-permute-start.18
  148.5 1.4 collective-permute-start.19
  150.8 18.0 %shard_map.72 = (bf16[64,4096]{1,0:T(8,128)(2,1)}, bf16[64,4096]{1,0:T(8,128)(2,1)}, bf16[64,4096]{1,0:T(8,128)(2,1)}, bf16[64,4096]{1,0:T(8,128)(2,1)}) custom-call(s32[4]{0:T(128)} %pad_add_fusion.1.info, bf16[64,4224]{1,0:T(8,128)(2,1)} %copy-done.1, bf16[64,4224]{1,0:T(8,128)(2,1)} %collective-permute-done.7.refs_1_, ...), custom_call_target="tpu_custom_call" | custom-call | flops 9663676416 | bytes 41943040 | tf_op jit(solution)/shard_map/pallas_call | solution.py:108
  168.8 1.7 shard_map.73
  170.6 3.6 %collective-permute-start.20 = (bf16[128,4096]{1,0:T(8,128)(2,1)S(1)}, bf16[128,4096]{1,0:T(8,128)(2,1)S(1)}, u32[]{:S(2)}, u32[]{:S(2)}) collective-permute-start(bf16[128,4096]{1,0:T(8,128)(2,1)S(1)} %get-tuple-element.167), channel_id=1, source_target_pairs={{0,2},{6,4},{1,3},{7,5},{8,10},{14,12},{9,11},{15,13},{16,18},{22,... | collective-permute-start | bytes 3145736 | tf_op jit(solution)/shard_map/ppermute | solution.py:286
  174.2 1.6 collective-permute-start.14
  176.2 1.5 collective-permute-start.16
  177.7 6.7 %collective-permute-done.14.refs_1_ = bf16[64,4096]{1,0:T(8,128)(2,1)S(1)} collective-permute-done((bf16[64,4096]{1,0:T(8,128)(2,1)S(1)}, bf16[64,4096]{1,0:T(8,128)(2,1)S(1)}, u32[]{:S(2)}, u32[]{:S(2)}) %collective-permute-start.14) | collective-permute-done | bytes 524320 | tf_op jit(solution)/shard_map/ppermute | solution.py:301
  184.4 6.4 %collective-permute-done.15.refs_2_ = bf16[64,4096]{1,0:T(8,128)(2,1)S(1)} collective-permute-done((bf16[64,4096]{1,0:T(8,128)(2,1)S(1)}, bf16[64,4096]{1,0:T(8,128)(2,1)S(1)}, u32[]{:S(2)}, u32[]{:S(2)}) %collective-permute-start.15) | collective-permute-done | bytes 524320 | tf_op jit(solution)/shard_map/ppermute | solution.py:301
  190.9 4.8 %collective-permute-done.16.refs_3_ = bf16[64,4096]{1,0:T(8,128)(2,1)S(1)} collective-permute-done((bf16[64,4096]{1,0:T(8,128)(2,1)S(1)}, bf16[64,4096]{1,0:T(8,128)(2,1)S(1)}, u32[]{:S(2)}, u32[]{:S(2)}) %collective-permute-start.16) | collective-permute-done | bytes 524320 | tf_op jit(solution)/shard_map/ppermute | solution.py:301
  195.6 1.7 shard_map.74
  197.3 2.3 collective-permute-start.28
  200.4 2.5 %collective-permute-start.24 = (bf16[64,4096]{1,0:T(8,128)(2,1)S(1)}, bf16[64,4096]{1,0:T(8,128)(2,1)S(1)}, u32[]{:S(2)}, u32[]{:S(2)}) collective-permute-start(bf16[64,4096]{1,0:T(8,128)(2,1)S(1)} %copy-done.15), channel_id=1, source_target_pairs={{0,1},{1,0},{16,17},{17,16},{2,3},{3,2},{18,19},{19,18},{4,5},{5,4... | collective-permute-start | bytes 1572872 | tf_op jit(solution)/shard_map/ppermute | solution.py:301
  203.5 1.0 collective-permute-start.26
  204.4 9.3 %collective-permute-done.24.refs_1_ = bf16[64,4096]{1,0:T(8,128)(2,1)S(1)} collective-permute-done((bf16[64,4096]{1,0:T(8,128)(2,1)S(1)}, bf16[64,4096]{1,0:T(8,128)(2,1)S(1)}, u32[]{:S(2)}, u32[]{:S(2)}) %collective-permute-start.24) | collective-permute-done | bytes 524320 | tf_op jit(solution)/shard_map/ppermute | solution.py:301
  213.7 14.0 %collective-permute-done.25.refs_2_ = bf16[64,4096]{1,0:T(8,128)(2,1)S(1)} collective-permute-done((bf16[64,4096]{1,0:T(8,128)(2,1)S(1)}, bf16[64,4096]{1,0:T(8,128)(2,1)S(1)}, u32[]{:S(2)}, u32[]{:S(2)}) %collective-permute-start.25) | collective-permute-done | bytes 524320 | tf_op jit(solution)/shard_map/ppermute | solution.py:301
  227.8 2.2 shard_map.75
  231.0 1.1 collective-permute-start.22
  232.1 2.4 collective-permute-start.23
  234.4 5.7 %collective-permute-done.21.refs_1_ = bf16[64,4096]{1,0:T(8,128)(2,1)S(1)} collective-permute-done((bf16[64,4096]{1,0:T(8,128)(2,1)S(1)}, bf16[64,4096]{1,0:T(8,128)(2,1)S(1)}, u32[]{:S(2)}, u32[]{:S(2)}) %collective-permute-start.21) | collective-permute-done | bytes 524320 | tf_op jit(solution)/shard_map/ppermute | solution.py:301
  240.1 5.7 %collective-permute-done.22.refs_2_ = bf16[64,4096]{1,0:T(8,128)(2,1)S(1)} collective-permute-done((bf16[64,4096]{1,0:T(8,128)(2,1)S(1)}, bf16[64,4096]{1,0:T(8,128)(2,1)S(1)}, u32[]{:S(2)}, u32[]{:S(2)}) %collective-permute-start.22) | collective-permute-done | bytes 524320 | tf_op jit(solution)/shard_map/ppermute | solution.py:301
  245.9 2.6 %shard_map.76 = bf16[128,4096]{1,0:T(8,128)(2,1)} custom-call(bf16[128,256]{1,0:T(8,128)(2,1)S(1)} %get-tuple-element.116.hi, bf16[128,256]{1,0:T(8,128)(2,1)S(1)} %get-tuple-element.117.mid, bf16[64,4096]{1,0:T(8,128)(2,1)S(1)} %copy-done.6, bf16[64,4096]{1,0:T(8,128)(2,1)S(1)} %collective-permute-done.21.refs_1_, ...), custom_call_target="tpu_custom_call" | custom-call | flops 536870912 | bytes 3145728 | tf_op jit(solution)/shard_map/pallas_call | solution.py:242
  (79 shorter events, 10.1 us)
Async XLA Ops:
  1.6 1.2 copy-start
  2.9 26.9 %collective-permute-start.2 = (bf16[128,4224]{1,0:T(8,128)(2,1)S(1)}, bf16[128,4224]{1,0:T(8,128)(2,1)S(1)}, u32[]{:S(2)}, u32[]{:S(2)}) collective-permute-start(bf16[128,4224]{1,0:T(8,128)(2,1)S(1)} %shard_map.64.refs_0_), channel_id=1, source_target_pairs={{0,2},{2,0},{4,6},{6,4},{1,3},{3,1},{5,7},{7,5},{8,10},{10,8},{12,... | collective-permute-start | bytes 3244040 | tf_op jit(solution)/shard_map/ppermute | solution.py:277
  6.0 23.9 %collective-permute-start = (bf16[128,4224]{1,0:T(8,128)(2,1)S(1)}, bf16[128,4224]{1,0:T(8,128)(2,1)S(1)}, u32[]{:S(2)}, u32[]{:S(2)}) collective-permute-start(bf16[128,4224]{1,0:T(8,128)(2,1)S(1)} %shard_map.64.refs_0_), channel_id=1, source_target_pairs={{2,4},{4,2},{3,5},{5,3},{10,12},{12,10},{11,13},{13,11},{18,20},{2... | collective-permute-start | bytes 3244040 | tf_op jit(solution)/shard_map/ppermute | solution.py:280
  11.6 30.1 %all-to-all-start = ((bf16[4,64,4224]{2,1,0:T(8,128)(2,1)}), bf16[4,64,4224]{2,1,0:T(8,128)(2,1)}, u32[]{:S(2)}, u32[]{:S(2)}) async-start(bf16[4,64,4224]{2,1,0:T(8,128)(2,1)} %bitcast.5), calls=%async_computation | async-start | bytes 4325376 | tf_op jit(solution)/shard_map/all_to_all | solution.py:299
  16.1 48.2 %collective-permute-start.4 = (bf16[4096,768]{1,0:T(8,128)(2,1)}, bf16[4096,768]{1,0:T(8,128)(2,1)}, u32[]{:S(2)}, u32[]{:S(2)}) collective-permute-start(bf16[4096,768]{1,0:T(8,128)(2,1)} %bitcast.12), channel_id=1, source_target_pairs={{0,8},{8,0},{1,9},{9,1},{2,10},{10,2},{3,11},{11,3},{4,12},{12,4},... | collective-permute-start | bytes 18874376 | tf_op jit(solution)/shard_map/ppermute | solution.py:294
  16.2 49.7 %collective-permute-start.5 = (bf16[4096,768]{1,0:T(8,128)(2,1)}, bf16[4096,768]{1,0:T(8,128)(2,1)}, u32[]{:S(2)}, u32[]{:S(2)}) collective-permute-start(bf16[4096,768]{1,0:T(8,128)(2,1)} %bitcast.17), channel_id=1, source_target_pairs={{0,8},{8,0},{1,9},{9,1},{2,10},{10,2},{3,11},{11,3},{4,12},{12,4},... | collective-permute-start | bytes 18874376 | tf_op jit(solution)/shard_map/ppermute | solution.py:294
  16.6 49.2 %collective-permute-start.6 = (bf16[768,4096]{1,0:T(8,128)(2,1)}, bf16[768,4096]{1,0:T(8,128)(2,1)}, u32[]{:S(2)}, u32[]{:S(2)}) collective-permute-start(bf16[768,4096]{1,0:T(8,128)(2,1)} %bitcast.22), channel_id=1, source_target_pairs={{0,8},{8,0},{1,9},{9,1},{2,10},{10,2},{3,11},{11,3},{4,12},{12,4},... | collective-permute-start | bytes 18874376 | tf_op jit(solution)/shard_map/ppermute | solution.py:294
  29.8 29.2 %collective-permute-start.1 = (bf16[128,4224]{1,0:T(8,128)(2,1)S(1)}, bf16[128,4224]{1,0:T(8,128)(2,1)}, u32[]{:S(2)}, u32[]{:S(2)}) collective-permute-start(bf16[128,4224]{1,0:T(8,128)(2,1)S(1)} %collective-permute-done.refs_1_), channel_id=1, source_target_pairs={{2,0},{4,6},{3,1},{5,7},{10,8},{12,14},{11,9},{13,15},{18,16},{20,... | collective-permute-start | bytes 3244040 | tf_op jit(solution)/shard_map/ppermute | solution.py:283
  31.1 15.0 %collective-permute-start.3 = (bf16[128,4224]{1,0:T(8,128)(2,1)S(1)}, bf16[128,4224]{1,0:T(8,128)(2,1)}, u32[]{:S(2)}, u32[]{:S(2)}) collective-permute-start(bf16[128,4224]{1,0:T(8,128)(2,1)S(1)} %collective-permute-done.2.refs_0_), channel_id=1, source_target_pairs={{2,4},{4,2},{3,5},{5,3},{10,12},{12,10},{11,13},{13,11},{18,20},{2... | collective-permute-start | bytes 3244040 | tf_op jit(solution)/shard_map/ppermute | solution.py:280
  41.7 53.0 %all-to-all-start.1 = ((bf16[4,64,4224]{2,1,0:T(8,128)(2,1)}), bf16[4,64,4224]{2,1,0:T(8,128)(2,1)}, u32[]{:S(2)}, u32[]{:S(2)}) async-start(bf16[4,64,4224]{2,1,0:T(8,128)(2,1)} %bitcast.10), calls=%async_computation.1 | async-start | bytes 4325376 | tf_op jit(solution)/shard_map/all_to_all | solution.py:299
  46.2 41.2 %collective-permute-start.10 = (bf16[128,4224]{1,0:T(8,128)(2,1)}, bf16[128,4224]{1,0:T(8,128)(2,1)S(1)}, u32[]{:S(2)}, u32[]{:S(2)}) collective-permute-start(bf16[128,4224]{1,0:T(8,128)(2,1)} %collective-permute-done.3.refs_1_), channel_id=1, source_target_pairs={{2,0},{4,6},{3,1},{5,7},{10,8},{12,14},{11,9},{13,15},{18,16},{20,... | collective-permute-start | bytes 3244040 | tf_op jit(solution)/shard_map/ppermute | solution.py:283
  62.8 85.7 %collective-permute-start.7 = (bf16[64,4224]{1,0:T(8,128)(2,1)S(1)}, bf16[64,4224]{1,0:T(8,128)(2,1)}, u32[]{:S(2)}, u32[]{:S(2)}) collective-permute-start(bf16[64,4224]{1,0:T(8,128)(2,1)S(1)} %get-tuple-element.125), channel_id=1, source_target_pairs={{0,1},{1,0},{16,17},{17,16},{2,3},{3,2},{18,19},{19,18},{4,5},{5,4... | collective-permute-start | bytes 1622024 | tf_op jit(solution)/shard_map/ppermute | solution.py:301
  64.3 85.7 %collective-permute-start.8 = (bf16[64,4224]{1,0:T(8,128)(2,1)S(1)}, bf16[64,4224]{1,0:T(8,128)(2,1)}, u32[]{:S(2)}, u32[]{:S(2)}) collective-permute-start(bf16[64,4224]{1,0:T(8,128)(2,1)S(1)} %get-tuple-element.126), channel_id=1, source_target_pairs={{0,16},{1,17},{16,0},{17,1},{2,18},{3,19},{18,2},{19,3},{4,20},{5,... | collective-permute-start | bytes 1622024 | tf_op jit(solution)/shard_map/ppermute | solution.py:301
  91.2 21.4 %collective-permute-start.11 = (bf16[64,4224]{1,0:T(8,128)(2,1)}, bf16[64,4224]{1,0:T(8,128)(2,1)S(1)}, u32[]{:S(2)}, u32[]{:S(2)}) collective-permute-start(bf16[64,4224]{1,0:T(8,128)(2,1)} %get-tuple-element.137), channel_id=1, source_target_pairs={{0,1},{1,0},{16,17},{17,16},{2,3},{3,2},{18,19},{19,18},{4,5},{5,4... | collective-permute-start | bytes 1622024 | tf_op jit(solution)/shard_map/ppermute | solution.py:301
  92.7 34.8 %collective-permute-start.12 = (bf16[64,4224]{1,0:T(8,128)(2,1)}, bf16[64,4224]{1,0:T(8,128)(2,1)S(1)}, u32[]{:S(2)}, u32[]{:S(2)}) collective-permute-start(bf16[64,4224]{1,0:T(8,128)(2,1)} %get-tuple-element.138), channel_id=1, source_target_pairs={{0,16},{1,17},{16,0},{17,1},{2,18},{3,19},{18,2},{19,3},{4,20},{5,... | collective-permute-start | bytes 1622024 | tf_op jit(solution)/shard_map/ppermute | solution.py:301
  94.3 33.3 %collective-permute-start.13 = (bf16[64,4224]{1,0:T(8,128)(2,1)}, bf16[64,4224]{1,0:T(8,128)(2,1)}, u32[]{:S(2)}, u32[]{:S(2)}) collective-permute-start(bf16[64,4224]{1,0:T(8,128)(2,1)} %get-tuple-element.139), channel_id=1, source_target_pairs={{0,17},{1,16},{16,1},{17,0},{2,19},{3,18},{18,3},{19,2},{4,21},{5,... | collective-permute-start | bytes 1622024 | tf_op jit(solution)/shard_map/ppermute | solution.py:301
  112.6 14.9 %copy-start.8 = (bf16[64,4224]{1,0:T(8,128)(2,1)}, bf16[64,4224]{1,0:T(8,128)(2,1)S(1)}, u32[]{:S(2)}) copy-start(bf16[64,4224]{1,0:T(8,128)(2,1)S(1)} %collective-permute-done.11.refs_1_) | copy-start | bytes 1622020
  112.6 37.4 %collective-permute-start.9 = (bf16[64,4224]{1,0:T(8,128)(2,1)S(1)}, bf16[64,4224]{1,0:T(8,128)(2,1)S(1)}, u32[]{:S(2)}, u32[]{:S(2)}) collective-permute-start(bf16[64,4224]{1,0:T(8,128)(2,1)S(1)} %get-tuple-element.127), channel_id=1, source_target_pairs={{0,17},{1,16},{16,1},{17,0},{2,19},{3,18},{18,3},{19,2},{4,21},{5,... | collective-permute-start | bytes 1622024 | tf_op jit(solution)/shard_map/ppermute | solution.py:301
  146.4 22.4 %collective-permute-start.17 = (bf16[64,4096]{1,0:T(8,128)(2,1)}, bf16[64,4096]{1,0:T(8,128)(2,1)S(1)}, u32[]{:S(2)}, u32[]{:S(2)}) collective-permute-start(bf16[64,4096]{1,0:T(8,128)(2,1)} %get-tuple-element.150), channel_id=1, source_target_pairs={{0,1},{1,0},{16,17},{17,16},{2,3},{3,2},{18,19},{19,18},{4,5},{5,4... | collective-permute-start | bytes 1572872 | tf_op jit(solution)/shard_map/ppermute | solution.py:301
  146.5 22.3 %collective-permute-start.18 = (bf16[64,4096]{1,0:T(8,128)(2,1)}, bf16[64,4096]{1,0:T(8,128)(2,1)S(1)}, u32[]{:S(2)}, u32[]{:S(2)}) collective-permute-start(bf16[64,4096]{1,0:T(8,128)(2,1)} %get-tuple-element.151), channel_id=1, source_target_pairs={{0,16},{1,17},{16,0},{17,1},{2,18},{3,19},{18,2},{19,3},{4,20},{5,... | collective-permute-start | bytes 1572872 | tf_op jit(solution)/shard_map/ppermute | solution.py:301
  148.5 20.3 %collective-permute-start.19 = (bf16[64,4096]{1,0:T(8,128)(2,1)}, bf16[64,4096]{1,0:T(8,128)(2,1)S(1)}, u32[]{:S(2)}, u32[]{:S(2)}) collective-permute-start(bf16[64,4096]{1,0:T(8,128)(2,1)} %get-tuple-element.152), channel_id=1, source_target_pairs={{0,17},{1,16},{16,1},{17,0},{2,19},{3,18},{18,3},{19,2},{4,21},{5,... | collective-permute-start | bytes 1572872 | tf_op jit(solution)/shard_map/ppermute | solution.py:301
  150.8 18.1 %copy-start.5 = (bf16[64,4096]{1,0:T(8,128)(2,1)S(1)}, bf16[64,4096]{1,0:T(8,128)(2,1)}, u32[]{:S(2)}) copy-start(bf16[64,4096]{1,0:T(8,128)(2,1)} %get-tuple-element.163.refs_0_) | copy-start | bytes 1572868
  168.8 5.4 %copy-start.18 = (bf16[64,4096]{1,0:T(8,128)(2,1)S(1)}, bf16[64,4096]{1,0:T(8,128)(2,1)}, u32[]{:S(2)}) copy-start(bf16[64,4096]{1,0:T(8,128)(2,1)} %get-tuple-element.158) | copy-start | bytes 1572868
  168.8 6.9 %copy-start.17 = (bf16[64,4096]{1,0:T(8,128)(2,1)S(1)}, bf16[64,4096]{1,0:T(8,128)(2,1)}, u32[]{:S(2)}) copy-start(bf16[64,4096]{1,0:T(8,128)(2,1)} %get-tuple-element.159) | copy-start | bytes 1572868
  168.8 7.4 %copy-start.16 = (bf16[64,4096]{1,0:T(8,128)(2,1)S(1)}, bf16[64,4096]{1,0:T(8,128)(2,1)}, u32[]{:S(2)}) copy-start(bf16[64,4096]{1,0:T(8,128)(2,1)} %get-tuple-element.160) | copy-start | bytes 1572868
  168.8 26.8 %copy-start.4 = (bf16[64,4096]{1,0:T(8,128)(2,1)S(1)}, bf16[64,4096]{1,0:T(8,128)(2,1)}, u32[]{:S(2)}) copy-start(bf16[64,4096]{1,0:T(8,128)(2,1)} %get-tuple-element.172.refs_0_) | copy-start | bytes 1572868
  170.5 29.8 %copy-start.15 = (bf16[64,4096]{1,0:T(8,128)(2,1)S(1)}, bf16[64,4096]{1,0:T(8,128)(2,1)}, u32[]{:S(2)}) copy-start(bf16[64,4096]{1,0:T(8,128)(2,1)} %get-tuple-element.169) | copy-start | bytes 1572868
  170.6 32.3 %copy-start.14 = (bf16[64,4096]{1,0:T(8,128)(2,1)S(1)}, bf16[64,4096]{1,0:T(8,128)(2,1)}, u32[]{:S(2)}) copy-start(bf16[64,4096]{1,0:T(8,128)(2,1)} %get-tuple-element.170) | copy-start | bytes 1572868
  170.6 32.9 %copy-start.13 = (bf16[64,4096]{1,0:T(8,128)(2,1)S(1)}, bf16[64,4096]{1,0:T(8,128)(2,1)}, u32[]{:S(2)}) copy-start(bf16[64,4096]{1,0:T(8,128)(2,1)} %get-tuple-element.171) | copy-start | bytes 1572868
  170.6 57.2 %copy-start.3 = (bf16[64,4096]{1,0:T(8,128)(2,1)S(1)}, bf16[64,4096]{1,0:T(8,128)(2,1)}, u32[]{:S(2)}) copy-start(bf16[64,4096]{1,0:T(8,128)(2,1)} %get-tuple-element.184.refs_0_) | copy-start | bytes 1572868
  170.6 25.1 %collective-permute-start.20 = (bf16[128,4096]{1,0:T(8,128)(2,1)S(1)}, bf16[128,4096]{1,0:T(8,128)(2,1)S(1)}, u32[]{:S(2)}, u32[]{:S(2)}) collective-permute-start(bf16[128,4096]{1,0:T(8,128)(2,1)S(1)} %get-tuple-element.167), channel_id=1, source_target_pairs={{0,2},{6,4},{1,3},{7,5},{8,10},{14,12},{9,11},{15,13},{16,18},{22,... | collective-permute-start | bytes 3145736 | tf_op jit(solution)/shard_map/ppermute | solution.py:286
  174.2 10.3 %collective-permute-start.14 = (bf16[64,4096]{1,0:T(8,128)(2,1)S(1)}, bf16[64,4096]{1,0:T(8,128)(2,1)S(1)}, u32[]{:S(2)}, u32[]{:S(2)}) collective-permute-start(bf16[64,4096]{1,0:T(8,128)(2,1)S(1)} %copy-done.18), channel_id=1, source_target_pairs={{0,1},{1,0},{16,17},{17,16},{2,3},{3,2},{18,19},{19,18},{4,5},{5,4... | collective-permute-start | bytes 1572872 | tf_op jit(solution)/shard_map/ppermute | solution.py:301
  175.7 15.1 %collective-permute-start.15 = (bf16[64,4096]{1,0:T(8,128)(2,1)S(1)}, bf16[64,4096]{1,0:T(8,128)(2,1)S(1)}, u32[]{:S(2)}, u32[]{:S(2)}) collective-permute-start(bf16[64,4096]{1,0:T(8,128)(2,1)S(1)} %copy-done.17), channel_id=1, source_target_pairs={{0,16},{1,17},{16,0},{17,1},{2,18},{3,19},{18,2},{19,3},{4,20},{5,... | collective-permute-start | bytes 1572872 | tf_op jit(solution)/shard_map/ppermute | solution.py:301
  176.2 19.4 %collective-permute-start.16 = (bf16[64,4096]{1,0:T(8,128)(2,1)S(1)}, bf16[64,4096]{1,0:T(8,128)(2,1)S(1)}, u32[]{:S(2)}, u32[]{:S(2)}) collective-permute-start(bf16[64,4096]{1,0:T(8,128)(2,1)S(1)} %copy-done.16), channel_id=1, source_target_pairs={{0,17},{1,16},{16,1},{17,0},{2,19},{3,18},{18,3},{19,2},{4,21},{5,... | collective-permute-start | bytes 1572872 | tf_op jit(solution)/shard_map/ppermute | solution.py:301
  197.3 30.4 %collective-permute-start.28 = (bf16[128,4096]{1,0:T(8,128)(2,1)S(1)}, bf16[128,4096]{1,0:T(8,128)(2,1)S(1)}, u32[]{:S(2)}, u32[]{:S(2)}) collective-permute-start(bf16[128,4096]{1,0:T(8,128)(2,1)S(1)} %get-tuple-element.176), channel_id=1, source_target_pairs={{0,2},{6,4},{1,3},{7,5},{8,10},{14,12},{9,11},{15,13},{16,18},{22,... | collective-permute-start | bytes 3145736 | tf_op jit(solution)/shard_map/ppermute | solution.py:286
  199.6 28.2 %collective-permute-start.27 = (bf16[128,4096]{1,0:T(8,128)(2,1)S(1)}, bf16[128,4096]{1,0:T(8,128)(2,1)S(1)}, u32[]{:S(2)}, u32[]{:S(2)}) collective-permute-start(bf16[128,4096]{1,0:T(8,128)(2,1)S(1)} %get-tuple-element.177), channel_id=1, source_target_pairs={{2,4},{4,2},{3,5},{5,3},{10,12},{12,10},{11,13},{13,11},{18,20},{2... | collective-permute-start | bytes 3145736 | tf_op jit(solution)/shard_map/ppermute | solution.py:280
  200.4 13.4 %collective-permute-start.24 = (bf16[64,4096]{1,0:T(8,128)(2,1)S(1)}, bf16[64,4096]{1,0:T(8,128)(2,1)S(1)}, u32[]{:S(2)}, u32[]{:S(2)}) collective-permute-start(bf16[64,4096]{1,0:T(8,128)(2,1)S(1)} %copy-done.15), channel_id=1, source_target_pairs={{0,1},{1,0},{16,17},{17,16},{2,3},{3,2},{18,19},{19,18},{4,5},{5,4... | collective-permute-start | bytes 1572872 | tf_op jit(solution)/shard_map/ppermute | solution.py:301
  202.9 24.9 %collective-permute-start.25 = (bf16[64,4096]{1,0:T(8,128)(2,1)S(1)}, bf16[64,4096]{1,0:T(8,128)(2,1)S(1)}, u32[]{:S(2)}, u32[]{:S(2)}) collective-permute-start(bf16[64,4096]{1,0:T(8,128)(2,1)S(1)} %copy-done.14), channel_id=1, source_target_pairs={{0,16},{1,17},{16,0},{17,1},{2,18},{3,19},{18,2},{19,3},{4,20},{5,... | collective-permute-start | bytes 1572872 | tf_op jit(solution)/shard_map/ppermute | solution.py:301
  203.5 24.3 %collective-permute-start.26 = (bf16[64,4096]{1,0:T(8,128)(2,1)S(1)}, bf16[64,4096]{1,0:T(8,128)(2,1)S(1)}, u32[]{:S(2)}, u32[]{:S(2)}) collective-permute-start(bf16[64,4096]{1,0:T(8,128)(2,1)S(1)} %copy-done.13), channel_id=1, source_target_pairs={{0,17},{1,16},{16,1},{17,0},{2,19},{3,18},{18,3},{19,2},{4,21},{5,... | collective-permute-start | bytes 1572872 | tf_op jit(solution)/shard_map/ppermute | solution.py:301
  227.8 3.1 %copy-start.12 = (bf16[64,4096]{1,0:T(8,128)(2,1)S(1)}, bf16[64,4096]{1,0:T(8,128)(2,1)}, u32[]{:S(2)}) copy-start(bf16[64,4096]{1,0:T(8,128)(2,1)} %get-tuple-element.179) | copy-start | bytes 1572868
  227.8 3.2 %copy-start.11 = (bf16[64,4096]{1,0:T(8,128)(2,1)S(1)}, bf16[64,4096]{1,0:T(8,128)(2,1)}, u32[]{:S(2)}) copy-start(bf16[64,4096]{1,0:T(8,128)(2,1)} %get-tuple-element.180) | copy-start | bytes 1572868
  227.8 4.3 %copy-start.10 = (bf16[64,4096]{1,0:T(8,128)(2,1)S(1)}, bf16[64,4096]{1,0:T(8,128)(2,1)}, u32[]{:S(2)}) copy-start(bf16[64,4096]{1,0:T(8,128)(2,1)} %get-tuple-element.181) | copy-start | bytes 1572868
  227.8 18.0 %copy-start.6 = (bf16[64,4096]{1,0:T(8,128)(2,1)S(1)}, bf16[64,4096]{1,0:T(8,128)(2,1)}, u32[]{:S(2)}) copy-start(bf16[64,4096]{1,0:T(8,128)(2,1)} %get-tuple-element.178.refs_0_) | copy-start | bytes 1572868
  230.1 15.8 %collective-permute-start.29 = (bf16[128,4096]{1,0:T(8,128)(2,1)S(1)}, bf16[128,4096]{1,0:T(8,128)(2,1)S(1)}, u32[]{:S(2)}, u32[]{:S(2)}) collective-permute-start(bf16[128,4096]{1,0:T(8,128)(2,1)S(1)} %get-tuple-element.189), channel_id=1, source_target_pairs={{0,2},{2,0},{4,6},{6,4},{1,3},{3,1},{5,7},{7,5},{8,10},{10,8},{12,... | collective-permute-start | bytes 3145736 | tf_op jit(solution)/shard_map/ppermute | solution.py:277
  230.1 15.7 %collective-permute-start.30 = (bf16[128,4096]{1,0:T(8,128)(2,1)S(1)}, bf16[128,4096]{1,0:T(8,128)(2,1)S(1)}, u32[]{:S(2)}, u32[]{:S(2)}) collective-permute-start(bf16[128,4096]{1,0:T(8,128)(2,1)S(1)} %get-tuple-element.190), channel_id=1, source_target_pairs={{2,4},{4,2},{3,5},{5,3},{10,12},{12,10},{11,13},{13,11},{18,20},{2... | collective-permute-start | bytes 3145736 | tf_op jit(solution)/shard_map/ppermute | solution.py:280
  230.9 9.2 %collective-permute-start.21 = (bf16[64,4096]{1,0:T(8,128)(2,1)S(1)}, bf16[64,4096]{1,0:T(8,128)(2,1)S(1)}, u32[]{:S(2)}, u32[]{:S(2)}) collective-permute-start(bf16[64,4096]{1,0:T(8,128)(2,1)S(1)} %copy-done.12), channel_id=1, source_target_pairs={{0,1},{1,0},{16,17},{17,16},{2,3},{3,2},{18,19},{19,18},{4,5},{5,4... | collective-permute-start | bytes 1572872 | tf_op jit(solution)/shard_map/ppermute | solution.py:301
  231.0 14.9 %collective-permute-start.22 = (bf16[64,4096]{1,0:T(8,128)(2,1)S(1)}, bf16[64,4096]{1,0:T(8,128)(2,1)S(1)}, u32[]{:S(2)}, u32[]{:S(2)}) collective-permute-start(bf16[64,4096]{1,0:T(8,128)(2,1)S(1)} %copy-done.11), channel_id=1, source_target_pairs={{0,16},{1,17},{16,0},{17,1},{2,18},{3,19},{18,2},{19,3},{4,20},{5,... | collective-permute-start | bytes 1572872 | tf_op jit(solution)/shard_map/ppermute | solution.py:301
  232.1 13.8 %collective-permute-start.23 = (bf16[64,4096]{1,0:T(8,128)(2,1)S(1)}, bf16[64,4096]{1,0:T(8,128)(2,1)S(1)}, u32[]{:S(2)}, u32[]{:S(2)}) collective-permute-start(bf16[64,4096]{1,0:T(8,128)(2,1)S(1)} %copy-done.10), channel_id=1, source_target_pairs={{0,17},{1,16},{16,1},{17,0},{2,19},{3,18},{18,3},{19,2},{4,21},{5,... | collective-permute-start | bytes 1572872 | tf_op jit(solution)/shard_map/ppermute | solution.py:301
  (4 other events, 3.2 us)

commit v6 on v5

--- a/solution.py
+++ b/solution.py
@@ -324,7 +324,7 @@
             held[k] = [after(moving[k] if k == bit else flip(held[k ^ bit][0], bit), sent[k - 1])]
         sends = parts if k in PERMUTED else 1
         sent[k], mixes[k] = route(flag, plane, held[k], sends, parts > 1, rows, top)
-        if k and sends == 1:
+        if k:
             sent[k] = after(sent[k], arrived[k - 1])
         if k > 1:
             run(k - 2, sent[k])

time: 251 us -> 243 us (0.968)
  waiting for transfers between devices: 98.4 us -> 93.1 us
    ppermute x18, waiting for transfers between devices: 65.1 us -> 56.6 us  [exchange(): lax.ppermute(values[m], ('y', 'x'), pairs[m])]
    all_to_all x2, waiting for transfers between devices: 5.51 us -> 12.4 us  [exchange(): lax.all_to_all(value, ('y', 'x'), 0, 0, tiled=True).reshape(values[0].shape)]
    ppermute x2, waiting for transfers between devices: 15.3 us -> 11.6 us  [outward(): return lax.ppermute(value, 'z', [(1, 0), (2, 3)])]
    unnamed x40 -> x50, local copies, waits for them, and re-layouts: 6.05 us -> 6.85 us
  transfers between devices with their start and end apart: 33 -> 33, of which waited for: 12 -> 15; matrix products, arithmetic and copies ran while one was open for 1% -> 1% of each run, Pallas kernels for 34% -> 27%
where the time goes in v6:
time: 243 us
  waiting for transfers between devices  93.1 us (38%)
  Pallas kernels  91.6 us (38%)
  starting transfers between devices  48.7 us (20%)
  local copies, waits for them, and re-layouts  6.94 us (3%)
    pallas_call x4, Pallas kernels, experts_apply(): pl.pallas_call(partial(experts_kernel, given=given, parts=parts, rows=row...  71.6 us
    ppermute x18, waiting for transfers between devices, exchange(): lax.ppermute(values[m], ('y', 'x'), pairs[m])  56.6 us
    ppermute x18, starting transfers between devices, exchange(): lax.ppermute(values[m], ('y', 'x'), pairs[m])  21.3 us
    ppermute x2, waiting for transfers between devices, flip(): return lax.ppermute(value, 'z', [(i, i ^ mask) for i in range(z_size)])  12.5 us
    all_to_all x2, waiting for transfers between devices, exchange(): lax.all_to_all(value, ('y', 'x'), 0, 0, tiled=True).reshape(values[0].shape)  12.4 us
    pallas_call x4, Pallas kernels, route(): pl.pallas_call(partial(route_kernel, choices=len(blocks), sends=sends, re...  11.7 us
    ppermute x2, waiting for transfers between devices, outward(): return lax.ppermute(value, 'z', [(1, 0), (2, 3)])  11.6 us
    all_to_all x2, starting transfers between devices, exchange(): lax.all_to_all(value, ('y', 'x'), 0, 0, tiled=True).reshape(values[0].shape)  8.94 us
  transfers between devices with their start and end apart: 33, of which 15 were waited for; matrix products, arithmetic and copies ran while one was open for 1% of the time, Pallas kernels for 27%

profile of v6, /device:TPU:0, one launch (start us, length us, event | category | flops | bytes accessed | tf_op | source)
XLA Modules:
  0.0 242.8 jit_solution(13240384558975821125)
XLA Ops:
  1.6 1.2 copy-done
  2.9 3.1 %collective-permute-start.2 = (bf16[128,4224]{1,0:T(8,128)(2,1)S(1)}, bf16[128,4224]{1,0:T(8,128)(2,1)S(1)}, u32[]{:S(2)}, u32[]{:S(2)}) collective-permute-start(bf16[128,4224]{1,0:T(8,128)(2,1)S(1)} %shard_map.64.refs_0_), channel_id=1, source_target_pairs={{0,2},{2,0},{4,6},{6,4},{1,3},{3,1},{5,7},{7,5},{8,10},{10,8},{12,... | collective-permute-start | bytes 3244040 | tf_op jit(solution)/shard_map/ppermute | solution.py:277
  8.3 3.4 %shard_map.65 = (bf16[256,4224]{1,0:T(8,128)(2,1)}, bf16[128,256]{1,0:T(8,128)(2,1)S(1)}, bf16[128,256]{1,0:T(8,128)(2,1)S(1)}) custom-call(s32[2]{0:T(128)S(1)} %pad_add_fusion.flag, f32[8,128]{1,0:T(8,128)S(1)} %scatter.9.plane, bf16[128,4224]{1,0:T(8,128)(2,1)S(1)} %shard_map.64.refs_0_), custom_call_target="tpu_custom_call" | custom-call | flops 55364812800 | bytes 3244032 | tf_op jit(solution)/shard_map/pallas_call | solution.py:211
  11.6 4.5 %all-to-all-start = ((bf16[4,64,4224]{2,1,0:T(8,128)(2,1)}), bf16[4,64,4224]{2,1,0:T(8,128)(2,1)}, u32[]{:S(2)}, u32[]{:S(2)}) async-start(bf16[4,64,4224]{2,1,0:T(8,128)(2,1)} %bitcast.5), calls=%async_computation | async-start | bytes 4325376 | tf_op jit(solution)/shard_map/all_to_all | solution.py:299
  17.3 12.5 %collective-permute-done.2.refs_0_ = bf16[128,4224]{1,0:T(8,128)(2,1)S(1)} collective-permute-done((bf16[128,4224]{1,0:T(8,128)(2,1)S(1)}, bf16[128,4224]{1,0:T(8,128)(2,1)S(1)}, u32[]{:S(2)}, u32[]{:S(2)}) %collective-permute-start.2) | collective-permute-done | bytes 1081376 | tf_op jit(solution)/shard_map/ppermute | solution.py:277
  29.8 1.3 collective-permute-start.1
  31.1 1.7 collective-permute-start.3
  32.8 3.4 %shard_map.66 = (bf16[256,4224]{1,0:T(8,128)(2,1)}, bf16[128,256]{1,0:T(8,128)(2,1)S(1)}, bf16[128,256]{1,0:T(8,128)(2,1)S(1)}) custom-call(s32[2]{0:T(128)S(1)} %pad_add_fusion.flag, f32[8,128]{1,0:T(8,128)S(1)} %scatter.9.plane, bf16[128,4224]{1,0:T(8,128)(2,1)S(1)} %collective-permute-done.2.refs_0_), custom_call_target="tpu_custom_call" | custom-call | flops 55364812800 | bytes 3244032 | tf_op jit(solution)/shard_map/pallas_call | solution.py:211
  36.2 5.5 %all-to-all-done = bf16[4,64,4224]{2,1,0:T(8,128)(2,1)} async-done(((bf16[4,64,4224]{2,1,0:T(8,128)(2,1)}), bf16[4,64,4224]{2,1,0:T(8,128)(2,1)}, u32[]{:S(2)}, u32[]{:S(2)}) %all-to-all-start) | async-done | bytes 2162720 | tf_op jit(solution)/shard_map/all_to_all | solution.py:299
  41.7 4.5 %all-to-all-start.1 = ((bf16[4,64,4224]{2,1,0:T(8,128)(2,1)}), bf16[4,64,4224]{2,1,0:T(8,128)(2,1)}, u32[]{:S(2)}, u32[]{:S(2)}) async-start(bf16[4,64,4224]{2,1,0:T(8,128)(2,1)} %bitcast.7), calls=%async_computation.1 | async-start | bytes 4325376 | tf_op jit(solution)/shard_map/all_to_all | solution.py:299
  46.2 1.3 collective-permute-start.10
  47.5 11.6 %collective-permute-done.1.refs_0_ = bf16[128,4224]{1,0:T(8,128)(2,1)} collective-permute-done((bf16[128,4224]{1,0:T(8,128)(2,1)S(1)}, bf16[128,4224]{1,0:T(8,128)(2,1)}, u32[]{:S(2)}, u32[]{:S(2)}) %collective-permute-start.1) | collective-permute-done | bytes 1081376 | tf_op jit(solution)/shard_map/ppermute | solution.py:283
  59.1 2.9 %shard_map.67 = (bf16[64,4224]{1,0:T(8,128)(2,1)S(1)}, bf16[64,4224]{1,0:T(8,128)(2,1)S(1)}, bf16[64,4224]{1,0:T(8,128)(2,1)S(1)}, bf16[64,4224]{1,0:T(8,128)(2,...) custom-call(s32[2]{0:T(128)S(1)} %pad_add_fusion.flag, f32[8,128]{1,0:T(8,128)S(1)} %scatter.9.plane, ...), custom_call_target="tpu_custom_call" | custom-call | flops 55364812800 | bytes 3244032 | tf_op jit(solution)/shard_map/pallas_call | solution.py:211
  64.4 6.9 %all-to-all-done.1 = bf16[4,64,4224]{2,1,0:T(8,128)(2,1)} async-done(((bf16[4,64,4224]{2,1,0:T(8,128)(2,1)}), bf16[4,64,4224]{2,1,0:T(8,128)(2,1)}, u32[]{:S(2)}, u32[]{:S(2)}) %all-to-all-start.1) | async-done | bytes 2162720 | tf_op jit(solution)/shard_map/all_to_all | solution.py:299
  71.3 1.4 collective-permute-start.7
  73.3 1.5 collective-permute-start.9
  74.8 17.8 %shard_map.68 = (bf16[64,4096]{1,0:T(8,128)(2,1)}, bf16[64,4096]{1,0:T(8,128)(2,1)}, bf16[64,4096]{1,0:T(8,128)(2,1)}, bf16[64,4096]{1,0:T(8,128)(2,1)}) custom-call(s32[4]{0:T(128)} %pad_add_fusion.1.info, bf16[256,4224]{1,0:T(8,128)(2,1)} %bitcast.6.refs_0_, bf16[4096,768]{1,0:T(8,128)(2,1)} %bitcast.13, bf16[4096,768]{1,0:T(8,128)(2,1)} %bitcast.18, ...), custom_call_target="tpu_custom_call" | custom-call | flops 9663676416 | bytes 41943040 | tf_op jit(solution)/shard_map/pallas_call | solution.py:108
  92.6 1.9 shard_map.69
  95.4 1.1 collective-permute-done.8.refs_2_
  96.5 1.6 collective-permute-start.11
  98.7 1.4 collective-permute-start.13
  100.1 17.8 %shard_map.70 = (bf16[64,4096]{1,0:T(8,128)(2,1)}, bf16[64,4096]{1,0:T(8,128)(2,1)}, bf16[64,4096]{1,0:T(8,128)(2,1)}, bf16[64,4096]{1,0:T(8,128)(2,1)}) custom-call(s32[4]{0:T(128)} %pad_add_fusion.1.info, bf16[256,4224]{1,0:T(8,128)(2,1)} %bitcast.8.refs_0_, bf16[4096,768]{1,0:T(8,128)(2,1)} %bitcast.14, bf16[4096,768]{1,0:T(8,128)(2,1)} %bitcast.19, ...), custom_call_target="tpu_custom_call" | custom-call | flops 9663676416 | bytes 41943040 | tf_op jit(solution)/shard_map/pallas_call | solution.py:108
  117.9 1.2 collective-permute-done.12.refs_2_
  119.1 1.9 collective-permute-done.13.refs_3_
  121.8 18.0 %shard_map.71 = (bf16[64,4096]{1,0:T(8,128)(2,1)}, bf16[64,4096]{1,0:T(8,128)(2,1)}, bf16[64,4096]{1,0:T(8,128)(2,1)}, bf16[64,4096]{1,0:T(8,128)(2,1)}) custom-call(s32[4]{0:T(128)} %pad_add_fusion.1.info, bf16[64,4224]{1,0:T(8,128)(2,1)} %copy-done.2, bf16[64,4224]{1,0:T(8,128)(2,1)} %copy-done.12, bf16[64,4224]{1,0:T(8,128)(2,1)} %copy-done.13, ...), custom_call_target="tpu_custom_call" | custom-call | flops 9663676416 | bytes 41943040 | tf_op jit(solution)/shard_map/pallas_call | solution.py:108
  140.7 1.8 collective-permute-start.18
  143.5 18.0 %shard_map.72 = (bf16[64,4096]{1,0:T(8,128)(2,1)}, bf16[64,4096]{1,0:T(8,128)(2,1)}, bf16[64,4096]{1,0:T(8,128)(2,1)}, bf16[64,4096]{1,0:T(8,128)(2,1)}) custom-call(s32[4]{0:T(128)} %pad_add_fusion.1.info, bf16[64,4224]{1,0:T(8,128)(2,1)} %copy-done.1, bf16[64,4224]{1,0:T(8,128)(2,1)} %copy-done.9, bf16[64,4224]{1,0:T(8,128)(2,1)} %copy-done.10, ...), custom_call_target="tpu_custom_call" | custom-call | flops 9663676416 | bytes 41943040 | tf_op jit(solution)/shard_map/pallas_call | solution.py:108
  161.5 1.0 collective-permute-done.18.refs_2_
  162.5 1.7 shard_map.73
  164.2 6.1 %collective-permute-start.20 = (bf16[128,4096]{1,0:T(8,128)(2,1)S(1)}, bf16[128,4096]{1,0:T(8,128)(2,1)S(1)}, u32[]{:S(2)}, u32[]{:S(2)}) collective-permute-start(bf16[128,4096]{1,0:T(8,128)(2,1)S(1)} %get-tuple-element.183), channel_id=1, source_target_pairs={{0,2},{6,4},{1,3},{7,5},{8,10},{14,12},{9,11},{15,13},{16,18},{22,... | collective-permute-start | bytes 3145736 | tf_op jit(solution)/shard_map/ppermute | solution.py:286
  170.4 1.7 collective-permute-start.14
  172.4 1.5 collective-permute-start.16
  173.9 11.0 %collective-permute-done.14.refs_1_ = bf16[64,4096]{1,0:T(8,128)(2,1)S(1)} collective-permute-done((bf16[64,4096]{1,0:T(8,128)(2,1)S(1)}, bf16[64,4096]{1,0:T(8,128)(2,1)S(1)}, u32[]{:S(2)}, u32[]{:S(2)}) %collective-permute-start.14) | collective-permute-done | bytes 524320 | tf_op jit(solution)/shard_map/ppermute | solution.py:301
  184.9 7.6 %collective-permute-done.15.refs_2_ = bf16[64,4096]{1,0:T(8,128)(2,1)S(1)} collective-permute-done((bf16[64,4096]{1,0:T(8,128)(2,1)S(1)}, bf16[64,4096]{1,0:T(8,128)(2,1)S(1)}, u32[]{:S(2)}, u32[]{:S(2)}) %collective-permute-start.15) | collective-permute-done | bytes 524320 | tf_op jit(solution)/shard_map/ppermute | solution.py:301
  192.5 1.7 shard_map.74
  194.2 1.4 collective-permute-start.28
  196.9 1.7 collective-permute-start.25
  198.7 1.2 collective-permute-start.26
  199.9 10.9 %collective-permute-done.24.refs_1_ = bf16[64,4096]{1,0:T(8,128)(2,1)S(1)} collective-permute-done((bf16[64,4096]{1,0:T(8,128)(2,1)S(1)}, bf16[64,4096]{1,0:T(8,128)(2,1)S(1)}, u32[]{:S(2)}, u32[]{:S(2)}) %collective-permute-start.24) | collective-permute-done | bytes 524320 | tf_op jit(solution)/shard_map/ppermute | solution.py:301
  210.8 5.0 %collective-permute-done.25.refs_2_ = bf16[64,4096]{1,0:T(8,128)(2,1)S(1)} collective-permute-done((bf16[64,4096]{1,0:T(8,128)(2,1)S(1)}, bf16[64,4096]{1,0:T(8,128)(2,1)S(1)}, u32[]{:S(2)}, u32[]{:S(2)}) %collective-permute-start.25) | collective-permute-done | bytes 524320 | tf_op jit(solution)/shard_map/ppermute | solution.py:301
  215.8 1.1 collective-permute-done.26.refs_3_
  217.0 2.2 shard_map.75
  220.9 1.3 collective-permute-start.21
  222.2 1.1 collective-permute-start.22
  223.2 1.2 collective-permute-start.23
  224.4 9.5 %collective-permute-done.21.refs_1_ = bf16[64,4096]{1,0:T(8,128)(2,1)S(1)} collective-permute-done((bf16[64,4096]{1,0:T(8,128)(2,1)S(1)}, bf16[64,4096]{1,0:T(8,128)(2,1)S(1)}, u32[]{:S(2)}, u32[]{:S(2)}) %collective-permute-start.21) | collective-permute-done | bytes 524320 | tf_op jit(solution)/shard_map/ppermute | solution.py:301
  233.9 6.2 %collective-permute-done.22.refs_2_ = bf16[64,4096]{1,0:T(8,128)(2,1)S(1)} collective-permute-done((bf16[64,4096]{1,0:T(8,128)(2,1)S(1)}, bf16[64,4096]{1,0:T(8,128)(2,1)S(1)}, u32[]{:S(2)}, u32[]{:S(2)}) %collective-permute-start.22) | collective-permute-done | bytes 524320 | tf_op jit(solution)/shard_map/ppermute | solution.py:301
  240.2 2.6 %shard_map.76 = bf16[128,4096]{1,0:T(8,128)(2,1)} custom-call(bf16[128,256]{1,0:T(8,128)(2,1)S(1)} %get-tuple-element.124.hi, bf16[128,256]{1,0:T(8,128)(2,1)S(1)} %get-tuple-element.125.mid, bf16[64,4096]{1,0:T(8,128)(2,1)S(1)} %copy-done.6, bf16[64,4096]{1,0:T(8,128)(2,1)S(1)} %collective-permute-done.21.refs_1_, ...), custom_call_target="tpu_custom_call" | custom-call | flops 536870912 | bytes 3145728 | tf_op jit(solution)/shard_map/pallas_call | solution.py:242
  (89 shorter events, 15.4 us)
Async XLA Ops:
  2.9 26.9 %collective-permute-start.2 = (bf16[128,4224]{1,0:T(8,128)(2,1)S(1)}, bf16[128,4224]{1,0:T(8,128)(2,1)S(1)}, u32[]{:S(2)}, u32[]{:S(2)}) collective-permute-start(bf16[128,4224]{1,0:T(8,128)(2,1)S(1)} %shard_map.64.refs_0_), channel_id=1, source_target_pairs={{0,2},{2,0},{4,6},{6,4},{1,3},{3,1},{5,7},{7,5},{8,10},{10,8},{12,... | collective-permute-start | bytes 3244040 | tf_op jit(solution)/shard_map/ppermute | solution.py:277
  6.0 23.9 %collective-permute-start = (bf16[128,4224]{1,0:T(8,128)(2,1)S(1)}, bf16[128,4224]{1,0:T(8,128)(2,1)S(1)}, u32[]{:S(2)}, u32[]{:S(2)}) collective-permute-start(bf16[128,4224]{1,0:T(8,128)(2,1)S(1)} %shard_map.64.refs_0_), channel_id=1, source_target_pairs={{2,4},{4,2},{3,5},{5,3},{10,12},{12,10},{11,13},{13,11},{18,20},{2... | collective-permute-start | bytes 3244040 | tf_op jit(solution)/shard_map/ppermute | solution.py:280
  11.6 30.1 %all-to-all-start = ((bf16[4,64,4224]{2,1,0:T(8,128)(2,1)}), bf16[4,64,4224]{2,1,0:T(8,128)(2,1)}, u32[]{:S(2)}, u32[]{:S(2)}) async-start(bf16[4,64,4224]{2,1,0:T(8,128)(2,1)} %bitcast.5), calls=%async_computation | async-start | bytes 4325376 | tf_op jit(solution)/shard_map/all_to_all | solution.py:299
  16.1 56.6 %collective-permute-start.4 = (bf16[4096,768]{1,0:T(8,128)(2,1)}, bf16[4096,768]{1,0:T(8,128)(2,1)}, u32[]{:S(2)}, u32[]{:S(2)}) collective-permute-start(bf16[4096,768]{1,0:T(8,128)(2,1)} %bitcast.12), channel_id=1, source_target_pairs={{0,8},{8,0},{1,9},{9,1},{2,10},{10,2},{3,11},{11,3},{4,12},{12,4},... | collective-permute-start | bytes 18874376 | tf_op jit(solution)/shard_map/ppermute | solution.py:294
  16.2 57.1 %collective-permute-start.5 = (bf16[4096,768]{1,0:T(8,128)(2,1)}, bf16[4096,768]{1,0:T(8,128)(2,1)}, u32[]{:S(2)}, u32[]{:S(2)}) collective-permute-start(bf16[4096,768]{1,0:T(8,128)(2,1)} %bitcast.17), channel_id=1, source_target_pairs={{0,8},{8,0},{1,9},{9,1},{2,10},{10,2},{3,11},{11,3},{4,12},{12,4},... | collective-permute-start | bytes 18874376 | tf_op jit(solution)/shard_map/ppermute | solution.py:294
  16.7 58.1 %collective-permute-start.6 = (bf16[768,4096]{1,0:T(8,128)(2,1)}, bf16[768,4096]{1,0:T(8,128)(2,1)}, u32[]{:S(2)}, u32[]{:S(2)}) collective-permute-start(bf16[768,4096]{1,0:T(8,128)(2,1)} %bitcast.22), channel_id=1, source_target_pairs={{0,8},{8,0},{1,9},{9,1},{2,10},{10,2},{3,11},{11,3},{4,12},{12,4},... | collective-permute-start | bytes 18874376 | tf_op jit(solution)/shard_map/ppermute | solution.py:294
  29.8 29.2 %collective-permute-start.1 = (bf16[128,4224]{1,0:T(8,128)(2,1)S(1)}, bf16[128,4224]{1,0:T(8,128)(2,1)}, u32[]{:S(2)}, u32[]{:S(2)}) collective-permute-start(bf16[128,4224]{1,0:T(8,128)(2,1)S(1)} %collective-permute-done.refs_1_), channel_id=1, source_target_pairs={{2,0},{4,6},{3,1},{5,7},{10,8},{12,14},{11,9},{13,15},{18,16},{20,... | collective-permute-start | bytes 3244040 | tf_op jit(solution)/shard_map/ppermute | solution.py:283
  31.1 15.1 %collective-permute-start.3 = (bf16[128,4224]{1,0:T(8,128)(2,1)S(1)}, bf16[128,4224]{1,0:T(8,128)(2,1)}, u32[]{:S(2)}, u32[]{:S(2)}) collective-permute-start(bf16[128,4224]{1,0:T(8,128)(2,1)S(1)} %collective-permute-done.2.refs_0_), channel_id=1, source_target_pairs={{2,4},{4,2},{3,5},{5,3},{10,12},{12,10},{11,13},{13,11},{18,20},{2... | collective-permute-start | bytes 3244040 | tf_op jit(solution)/shard_map/ppermute | solution.py:280
  41.7 29.6 %all-to-all-start.1 = ((bf16[4,64,4224]{2,1,0:T(8,128)(2,1)}), bf16[4,64,4224]{2,1,0:T(8,128)(2,1)}, u32[]{:S(2)}, u32[]{:S(2)}) async-start(bf16[4,64,4224]{2,1,0:T(8,128)(2,1)} %bitcast.7), calls=%async_computation.1 | async-start | bytes 4325376 | tf_op jit(solution)/shard_map/all_to_all | solution.py:299
  46.2 46.4 %collective-permute-start.10 = (bf16[128,4224]{1,0:T(8,128)(2,1)}, bf16[128,4224]{1,0:T(8,128)(2,1)S(1)}, u32[]{:S(2)}, u32[]{:S(2)}) collective-permute-start(bf16[128,4224]{1,0:T(8,128)(2,1)} %collective-permute-done.3.refs_1_), channel_id=1, source_target_pairs={{2,0},{4,6},{3,1},{5,7},{10,8},{12,14},{11,9},{13,15},{18,16},{20,... | collective-permute-start | bytes 3244040 | tf_op jit(solution)/shard_map/ppermute | solution.py:283
  71.3 24.1 %collective-permute-start.7 = (bf16[64,4224]{1,0:T(8,128)(2,1)}, bf16[64,4224]{1,0:T(8,128)(2,1)S(1)}, u32[]{:S(2)}, u32[]{:S(2)}) collective-permute-start(bf16[64,4224]{1,0:T(8,128)(2,1)} %copy-done.8), channel_id=1, source_target_pairs={{0,1},{1,0},{16,17},{17,16},{2,3},{3,2},{18,19},{19,18},{4,5},{5,4... | collective-permute-start | bytes 1622024 | tf_op jit(solution)/shard_map/ppermute | solution.py:301
  72.7 23.8 %collective-permute-start.8 = (bf16[64,4224]{1,0:T(8,128)(2,1)}, bf16[64,4224]{1,0:T(8,128)(2,1)S(1)}, u32[]{:S(2)}, u32[]{:S(2)}) collective-permute-start(bf16[64,4224]{1,0:T(8,128)(2,1)} %copy-done.7), channel_id=1, source_target_pairs={{0,16},{1,17},{16,0},{17,1},{2,18},{3,19},{18,2},{19,3},{4,20},{5,... | collective-permute-start | bytes 1622024 | tf_op jit(solution)/shard_map/ppermute | solution.py:301
  73.3 23.2 %collective-permute-start.9 = (bf16[64,4224]{1,0:T(8,128)(2,1)S(1)}, bf16[64,4224]{1,0:T(8,128)(2,1)S(1)}, u32[]{:S(2)}, u32[]{:S(2)}) collective-permute-start(bf16[64,4224]{1,0:T(8,128)(2,1)S(1)} %get-tuple-element.139), channel_id=1, source_target_pairs={{0,17},{1,16},{16,1},{17,0},{2,19},{3,18},{18,3},{19,2},{4,21},{5,... | collective-permute-start | bytes 1622024 | tf_op jit(solution)/shard_map/ppermute | solution.py:301
  95.4 22.5 %copy-start.9 = (bf16[64,4224]{1,0:T(8,128)(2,1)}, bf16[64,4224]{1,0:T(8,128)(2,1)S(1)}, u32[]{:S(2)}) copy-start(bf16[64,4224]{1,0:T(8,128)(2,1)S(1)} %collective-permute-done.7.refs_1_) | copy-start | bytes 1622020
  96.5 21.4 %copy-start.10 = (bf16[64,4224]{1,0:T(8,128)(2,1)}, bf16[64,4224]{1,0:T(8,128)(2,1)S(1)}, u32[]{:S(2)}) copy-start(bf16[64,4224]{1,0:T(8,128)(2,1)S(1)} %collective-permute-done.8.refs_2_) | copy-start | bytes 1622020
  96.5 21.4 %copy-start.11 = (bf16[64,4224]{1,0:T(8,128)(2,1)}, bf16[64,4224]{1,0:T(8,128)(2,1)S(1)}, u32[]{:S(2)}) copy-start(bf16[64,4224]{1,0:T(8,128)(2,1)S(1)} %collective-permute-done.9.refs_3_) | copy-start | bytes 1622020
  96.5 21.4 %collective-permute-start.11 = (bf16[64,4224]{1,0:T(8,128)(2,1)S(1)}, bf16[64,4224]{1,0:T(8,128)(2,1)S(1)}, u32[]{:S(2)}, u32[]{:S(2)}) collective-permute-start(bf16[64,4224]{1,0:T(8,128)(2,1)S(1)} %get-tuple-element.153), channel_id=1, source_target_pairs={{0,1},{1,0},{16,17},{17,16},{2,3},{3,2},{18,19},{19,18},{4,5},{5,4... | collective-permute-start | bytes 1622024 | tf_op jit(solution)/shard_map/ppermute | solution.py:301
  98.1 21.0 %collective-permute-start.12 = (bf16[64,4224]{1,0:T(8,128)(2,1)S(1)}, bf16[64,4224]{1,0:T(8,128)(2,1)S(1)}, u32[]{:S(2)}, u32[]{:S(2)}) collective-permute-start(bf16[64,4224]{1,0:T(8,128)(2,1)S(1)} %get-tuple-element.154), channel_id=1, source_target_pairs={{0,16},{1,17},{16,0},{17,1},{2,18},{3,19},{18,2},{19,3},{4,20},{5,... | collective-permute-start | bytes 1622024 | tf_op jit(solution)/shard_map/ppermute | solution.py:301
  98.7 22.3 %collective-permute-start.13 = (bf16[64,4224]{1,0:T(8,128)(2,1)S(1)}, bf16[64,4224]{1,0:T(8,128)(2,1)S(1)}, u32[]{:S(2)}, u32[]{:S(2)}) collective-permute-start(bf16[64,4224]{1,0:T(8,128)(2,1)S(1)} %get-tuple-element.155), channel_id=1, source_target_pairs={{0,17},{1,16},{16,1},{17,0},{2,19},{3,18},{18,3},{19,2},{4,21},{5,... | collective-permute-start | bytes 1622024 | tf_op jit(solution)/shard_map/ppermute | solution.py:301
  139.9 21.6 %collective-permute-start.17 = (bf16[64,4096]{1,0:T(8,128)(2,1)}, bf16[64,4096]{1,0:T(8,128)(2,1)S(1)}, u32[]{:S(2)}, u32[]{:S(2)}) collective-permute-start(bf16[64,4096]{1,0:T(8,128)(2,1)} %get-tuple-element.166), channel_id=1, source_target_pairs={{0,1},{1,0},{16,17},{17,16},{2,3},{3,2},{18,19},{19,18},{4,5},{5,4... | collective-permute-start | bytes 1572872 | tf_op jit(solution)/shard_map/ppermute | solution.py:301
  140.7 21.7 %collective-permute-start.18 = (bf16[64,4096]{1,0:T(8,128)(2,1)}, bf16[64,4096]{1,0:T(8,128)(2,1)S(1)}, u32[]{:S(2)}, u32[]{:S(2)}) collective-permute-start(bf16[64,4096]{1,0:T(8,128)(2,1)} %get-tuple-element.167), channel_id=1, source_target_pairs={{0,16},{1,17},{16,0},{17,1},{2,18},{3,19},{18,2},{19,3},{4,20},{5,... | collective-permute-start | bytes 1572872 | tf_op jit(solution)/shard_map/ppermute | solution.py:301
  142.5 20.0 %collective-permute-start.19 = (bf16[64,4096]{1,0:T(8,128)(2,1)}, bf16[64,4096]{1,0:T(8,128)(2,1)S(1)}, u32[]{:S(2)}, u32[]{:S(2)}) collective-permute-start(bf16[64,4096]{1,0:T(8,128)(2,1)} %get-tuple-element.168), channel_id=1, source_target_pairs={{0,17},{1,16},{16,1},{17,0},{2,19},{3,18},{18,3},{19,2},{4,21},{5,... | collective-permute-start | bytes 1572872 | tf_op jit(solution)/shard_map/ppermute | solution.py:301
  143.5 19.0 %copy-start.5 = (bf16[64,4096]{1,0:T(8,128)(2,1)S(1)}, bf16[64,4096]{1,0:T(8,128)(2,1)}, u32[]{:S(2)}) copy-start(bf16[64,4096]{1,0:T(8,128)(2,1)} %get-tuple-element.179.refs_0_) | copy-start | bytes 1572868
  161.4 8.9 %copy-start.23 = (bf16[64,4096]{1,0:T(8,128)(2,1)S(1)}, bf16[64,4096]{1,0:T(8,128)(2,1)}, u32[]{:S(2)}) copy-start(bf16[64,4096]{1,0:T(8,128)(2,1)} %get-tuple-element.174) | copy-start | bytes 1572868
  161.4 10.7 %copy-start.22 = (bf16[64,4096]{1,0:T(8,128)(2,1)S(1)}, bf16[64,4096]{1,0:T(8,128)(2,1)}, u32[]{:S(2)}) copy-start(bf16[64,4096]{1,0:T(8,128)(2,1)} %get-tuple-element.175) | copy-start | bytes 1572868
  161.4 10.9 %copy-start.21 = (bf16[64,4096]{1,0:T(8,128)(2,1)S(1)}, bf16[64,4096]{1,0:T(8,128)(2,1)}, u32[]{:S(2)}) copy-start(bf16[64,4096]{1,0:T(8,128)(2,1)} %get-tuple-element.176) | copy-start | bytes 1572868
  161.5 31.1 %copy-start.4 = (bf16[64,4096]{1,0:T(8,128)(2,1)S(1)}, bf16[64,4096]{1,0:T(8,128)(2,1)}, u32[]{:S(2)}) copy-start(bf16[64,4096]{1,0:T(8,128)(2,1)} %get-tuple-element.188.refs_0_) | copy-start | bytes 1572868
  164.2 32.2 %copy-start.20 = (bf16[64,4096]{1,0:T(8,128)(2,1)S(1)}, bf16[64,4096]{1,0:T(8,128)(2,1)}, u32[]{:S(2)}) copy-start(bf16[64,4096]{1,0:T(8,128)(2,1)} %get-tuple-element.185) | copy-start | bytes 1572868
  164.2 32.8 %copy-start.19 = (bf16[64,4096]{1,0:T(8,128)(2,1)S(1)}, bf16[64,4096]{1,0:T(8,128)(2,1)}, u32[]{:S(2)}) copy-start(bf16[64,4096]{1,0:T(8,128)(2,1)} %get-tuple-element.186) | copy-start | bytes 1572868
  164.2 34.5 %copy-start.18 = (bf16[64,4096]{1,0:T(8,128)(2,1)S(1)}, bf16[64,4096]{1,0:T(8,128)(2,1)}, u32[]{:S(2)}) copy-start(bf16[64,4096]{1,0:T(8,128)(2,1)} %get-tuple-element.187) | copy-start | bytes 1572868
  164.2 52.8 %copy-start.3 = (bf16[64,4096]{1,0:T(8,128)(2,1)S(1)}, bf16[64,4096]{1,0:T(8,128)(2,1)}, u32[]{:S(2)}) copy-start(bf16[64,4096]{1,0:T(8,128)(2,1)} %get-tuple-element.200.refs_0_) | copy-start | bytes 1572868
  164.2 28.3 %collective-permute-start.20 = (bf16[128,4096]{1,0:T(8,128)(2,1)S(1)}, bf16[128,4096]{1,0:T(8,128)(2,1)S(1)}, u32[]{:S(2)}, u32[]{:S(2)}) collective-permute-start(bf16[128,4096]{1,0:T(8,128)(2,1)S(1)} %get-tuple-element.183), channel_id=1, source_target_pairs={{0,2},{6,4},{1,3},{7,5},{8,10},{14,12},{9,11},{15,13},{16,18},{22,... | collective-permute-start | bytes 3145736 | tf_op jit(solution)/shard_map/ppermute | solution.py:286
  170.4 14.6 %collective-permute-start.14 = (bf16[64,4096]{1,0:T(8,128)(2,1)S(1)}, bf16[64,4096]{1,0:T(8,128)(2,1)S(1)}, u32[]{:S(2)}, u32[]{:S(2)}) collective-permute-start(bf16[64,4096]{1,0:T(8,128)(2,1)S(1)} %copy-done.23), channel_id=1, source_target_pairs={{0,1},{1,0},{16,17},{17,16},{2,3},{3,2},{18,19},{19,18},{4,5},{5,4... | collective-permute-start | bytes 1572872 | tf_op jit(solution)/shard_map/ppermute | solution.py:301
  172.1 20.4 %collective-permute-start.15 = (bf16[64,4096]{1,0:T(8,128)(2,1)S(1)}, bf16[64,4096]{1,0:T(8,128)(2,1)S(1)}, u32[]{:S(2)}, u32[]{:S(2)}) collective-permute-start(bf16[64,4096]{1,0:T(8,128)(2,1)S(1)} %copy-done.22), channel_id=1, source_target_pairs={{0,16},{1,17},{16,0},{17,1},{2,18},{3,19},{18,2},{19,3},{4,20},{5,... | collective-permute-start | bytes 1572872 | tf_op jit(solution)/shard_map/ppermute | solution.py:301
  172.4 20.1 %collective-permute-start.16 = (bf16[64,4096]{1,0:T(8,128)(2,1)S(1)}, bf16[64,4096]{1,0:T(8,128)(2,1)S(1)}, u32[]{:S(2)}, u32[]{:S(2)}) collective-permute-start(bf16[64,4096]{1,0:T(8,128)(2,1)S(1)} %copy-done.21), channel_id=1, source_target_pairs={{0,17},{1,16},{16,1},{17,0},{2,19},{3,18},{18,3},{19,2},{4,21},{5,... | collective-permute-start | bytes 1572872 | tf_op jit(solution)/shard_map/ppermute | solution.py:301
  194.2 22.7 %collective-permute-start.28 = (bf16[128,4096]{1,0:T(8,128)(2,1)S(1)}, bf16[128,4096]{1,0:T(8,128)(2,1)S(1)}, u32[]{:S(2)}, u32[]{:S(2)}) collective-permute-start(bf16[128,4096]{1,0:T(8,128)(2,1)S(1)} %get-tuple-element.192), channel_id=1, source_target_pairs={{0,2},{6,4},{1,3},{7,5},{8,10},{14,12},{9,11},{15,13},{16,18},{22,... | collective-permute-start | bytes 3145736 | tf_op jit(solution)/shard_map/ppermute | solution.py:286
  195.6 21.4 %collective-permute-start.27 = (bf16[128,4096]{1,0:T(8,128)(2,1)S(1)}, bf16[128,4096]{1,0:T(8,128)(2,1)S(1)}, u32[]{:S(2)}, u32[]{:S(2)}) collective-permute-start(bf16[128,4096]{1,0:T(8,128)(2,1)S(1)} %get-tuple-element.193), channel_id=1, source_target_pairs={{2,4},{4,2},{3,5},{5,3},{10,12},{12,10},{11,13},{13,11},{18,20},{2... | collective-permute-start | bytes 3145736 | tf_op jit(solution)/shard_map/ppermute | solution.py:280
  196.4 14.5 %collective-permute-start.24 = (bf16[64,4096]{1,0:T(8,128)(2,1)S(1)}, bf16[64,4096]{1,0:T(8,128)(2,1)S(1)}, u32[]{:S(2)}, u32[]{:S(2)}) collective-permute-start(bf16[64,4096]{1,0:T(8,128)(2,1)S(1)} %copy-done.20), channel_id=1, source_target_pairs={{0,1},{1,0},{16,17},{17,16},{2,3},{3,2},{18,19},{19,18},{4,5},{5,4... | collective-permute-start | bytes 1572872 | tf_op jit(solution)/shard_map/ppermute | solution.py:301
  196.9 18.9 %collective-permute-start.25 = (bf16[64,4096]{1,0:T(8,128)(2,1)S(1)}, bf16[64,4096]{1,0:T(8,128)(2,1)S(1)}, u32[]{:S(2)}, u32[]{:S(2)}) collective-permute-start(bf16[64,4096]{1,0:T(8,128)(2,1)S(1)} %copy-done.19), channel_id=1, source_target_pairs={{0,16},{1,17},{16,0},{17,1},{2,18},{3,19},{18,2},{19,3},{4,20},{5,... | collective-permute-start | bytes 1572872 | tf_op jit(solution)/shard_map/ppermute | solution.py:301
  198.7 18.3 %collective-permute-start.26 = (bf16[64,4096]{1,0:T(8,128)(2,1)S(1)}, bf16[64,4096]{1,0:T(8,128)(2,1)S(1)}, u32[]{:S(2)}, u32[]{:S(2)}) collective-permute-start(bf16[64,4096]{1,0:T(8,128)(2,1)S(1)} %copy-done.18), channel_id=1, source_target_pairs={{0,17},{1,16},{16,1},{17,0},{2,19},{3,18},{18,3},{19,2},{4,21},{5,... | collective-permute-start | bytes 1572872 | tf_op jit(solution)/shard_map/ppermute | solution.py:301
  217.0 5.2 %copy-start.16 = (bf16[64,4096]{1,0:T(8,128)(2,1)S(1)}, bf16[64,4096]{1,0:T(8,128)(2,1)}, u32[]{:S(2)}) copy-start(bf16[64,4096]{1,0:T(8,128)(2,1)} %get-tuple-element.196) | copy-start | bytes 1572868
  217.0 6.2 %copy-start.15 = (bf16[64,4096]{1,0:T(8,128)(2,1)S(1)}, bf16[64,4096]{1,0:T(8,128)(2,1)}, u32[]{:S(2)}) copy-start(bf16[64,4096]{1,0:T(8,128)(2,1)} %get-tuple-element.197) | copy-start | bytes 1572868
  217.0 23.1 %copy-start.6 = (bf16[64,4096]{1,0:T(8,128)(2,1)S(1)}, bf16[64,4096]{1,0:T(8,128)(2,1)}, u32[]{:S(2)}) copy-start(bf16[64,4096]{1,0:T(8,128)(2,1)} %get-tuple-element.194.refs_0_) | copy-start | bytes 1572868
  219.3 20.9 %collective-permute-start.29 = (bf16[128,4096]{1,0:T(8,128)(2,1)S(1)}, bf16[128,4096]{1,0:T(8,128)(2,1)S(1)}, u32[]{:S(2)}, u32[]{:S(2)}) collective-permute-start(bf16[128,4096]{1,0:T(8,128)(2,1)S(1)} %get-tuple-element.205), channel_id=1, source_target_pairs={{0,2},{2,0},{4,6},{6,4},{1,3},{3,1},{5,7},{7,5},{8,10},{10,8},{12,... | collective-permute-start | bytes 3145736 | tf_op jit(solution)/shard_map/ppermute | solution.py:277
  220.1 20.0 %collective-permute-start.30 = (bf16[128,4096]{1,0:T(8,128)(2,1)S(1)}, bf16[128,4096]{1,0:T(8,128)(2,1)S(1)}, u32[]{:S(2)}, u32[]{:S(2)}) collective-permute-start(bf16[128,4096]{1,0:T(8,128)(2,1)S(1)} %get-tuple-element.206), channel_id=1, source_target_pairs={{2,4},{4,2},{3,5},{5,3},{10,12},{12,10},{11,13},{13,11},{18,20},{2... | collective-permute-start | bytes 3145736 | tf_op jit(solution)/shard_map/ppermute | solution.py:280
  220.9 13.0 %collective-permute-start.21 = (bf16[64,4096]{1,0:T(8,128)(2,1)S(1)}, bf16[64,4096]{1,0:T(8,128)(2,1)S(1)}, u32[]{:S(2)}, u32[]{:S(2)}) collective-permute-start(bf16[64,4096]{1,0:T(8,128)(2,1)S(1)} %copy-done.17), channel_id=1, source_target_pairs={{0,1},{1,0},{16,17},{17,16},{2,3},{3,2},{18,19},{19,18},{4,5},{5,4... | collective-permute-start | bytes 1572872 | tf_op jit(solution)/shard_map/ppermute | solution.py:301
  222.2 18.0 %collective-permute-start.22 = (bf16[64,4096]{1,0:T(8,128)(2,1)S(1)}, bf16[64,4096]{1,0:T(8,128)(2,1)S(1)}, u32[]{:S(2)}, u32[]{:S(2)}) collective-permute-start(bf16[64,4096]{1,0:T(8,128)(2,1)S(1)} %copy-done.16), channel_id=1, source_target_pairs={{0,16},{1,17},{16,0},{17,1},{2,18},{3,19},{18,2},{19,3},{4,20},{5,... | collective-permute-start | bytes 1572872 | tf_op jit(solution)/shard_map/ppermute | solution.py:301
  223.2 16.9 %collective-permute-start.23 = (bf16[64,4096]{1,0:T(8,128)(2,1)S(1)}, bf16[64,4096]{1,0:T(8,128)(2,1)S(1)}, u32[]{:S(2)}, u32[]{:S(2)}) collective-permute-start(bf16[64,4096]{1,0:T(8,128)(2,1)S(1)} %copy-done.15), channel_id=1, source_target_pairs={{0,17},{1,16},{16,1},{17,0},{2,19},{3,18},{18,3},{19,2},{4,21},{5,... | collective-permute-start | bytes 1572872 | tf_op jit(solution)/shard_map/ppermute | solution.py:301
  (9 other events, 14.1 us)

commit v7 on v6

--- a/solution.py
+++ b/solution.py
@@ -145,7 +145,7 @@
     )(tokens, ids, weights)
 
 
-def route_kernel(flag, plane, *refs, choices, sends, relative, rows, top, width):
+def route_kernel(flag, *refs, choices, sends, relative, rows, top, width, sizes):
     blocks, outs, (mix_hi, mix_mid) = refs[:choices], refs[choices : choices + sends], refs[choices + sends :]
 
     def block(s):
@@ -155,7 +155,11 @@
     extra = block(slice(width, width + EXTRA)).astype(F32)
     count = extra.shape[0]
     lanes = mix_hi.shape[1]
-    ids = plane[:1, :]
+    chips, x_size, lane_count = sizes
+    lane = lax.broadcasted_iota(jnp.int32, (1, 128), 1)
+    chip = lane // 2
+    ids = 2 * (chip // x_size) * lane_count + flag[2] * x_size + chip % x_size + lane % 2 * lane_count
+    ids = jnp.where(lane < 2 * chips, ids, -1).astype(F32)
     chosen = jnp.zeros((count, 128), F32)
     w_hi, w_mid = chosen, chosen
     for k in range(top):
@@ -202,21 +206,19 @@
             outs[p][:, s] = got[p * each : (p + 1) * each]
 
 
-def route(flag, plane, blocks, sends, relative, rows, top):
+def route(flag, sizes, blocks, sends, relative, rows, top):
     count, wide = blocks[0].shape
-    chips = plane.shape[0]
-    lanes = chips * rows
-    ids = jnp.full((8, 128), -1.0, F32).at[:, : 2 * chips].set(plane.reshape(1, -1))
+    lanes = sizes[0] * rows
     whole = pl.BlockSpec(memory_space=pltpu.VMEM)
     out = pl.pallas_call(
-        partial(route_kernel, choices=len(blocks), sends=sends, relative=relative, rows=rows, top=top, width=wide - EXTRA),
-        in_specs=[pl.BlockSpec(memory_space=pltpu.SMEM), whole] + [whole] * len(blocks),
+        partial(route_kernel, choices=len(blocks), sends=sends, relative=relative, rows=rows, top=top, width=wide - EXTRA, sizes=sizes),
+        in_specs=[pl.BlockSpec(memory_space=pltpu.SMEM)] + [whole] * len(blocks),
         out_specs=[whole] * (sends + 2),
         out_shape=[jax.ShapeDtypeStruct((lanes // sends, wide), BF16)] * sends
         + [jax.ShapeDtypeStruct((count, lanes), BF16)] * 2,
         compiler_params=pltpu.CompilerParams(vmem_limit_bytes=24 * MIB),
         cost_estimate=pl.CostEstimate(flops=ROUTE_COST * count * lanes * wide, bytes_accessed=2 * (count + lanes) * wide, transcendentals=0),
-    )(flag, ids, *blocks)
+    )(flag, *blocks)
     return out[:sends], out[sends:]
 
 
@@ -267,9 +269,6 @@
 
     parts = chips if chips in (2, 4) else 1
     here = lax.axis_index("y") * x_size + lax.axis_index("x")
-    chip = jnp.arange(chips, dtype=jnp.int32)
-    low = 2 * (chip // x_size) * lane_count + z_at * x_size + chip % x_size
-    plane = jnp.stack([low, low + lane_count], axis=-1).astype(F32)
     low_here = 2 * lax.axis_index("y") * lane_count + z_at * x_size + lax.axis_index("x")
     info = jnp.stack([low_here, low_here + lane_count, lax.axis_index("core"), here]).astype(jnp.int32)
 
@@ -288,7 +287,7 @@
     is_end = (z_at == 0) | (z_at == z_size - 1)
 
     block = pack(tokens, expert_ids, router_weights)
-    flag = jnp.stack([is_end.astype(jnp.int32), here])
+    flag = jnp.stack([is_end.astype(jnp.int32), here, z_at])
     swap = [(0, 1), (1, 0)]
     own = [gate_weight[0], up_weight[0], down_weight[0]]
     other = [lax.ppermute(w, "core", swap) for w in own]
@@ -323,7 +322,7 @@
             bit = k & -k
             held[k] = [after(moving[k] if k == bit else flip(held[k ^ bit][0], bit), sent[k - 1])]
         sends = parts if k in PERMUTED else 1
-        sent[k], mixes[k] = route(flag, plane, held[k], sends, parts > 1, rows, top)
+        sent[k], mixes[k] = route(flag, (chips, x_size, lane_count), held[k], sends, parts > 1, rows, top)
         if k:
             sent[k] = after(sent[k], arrived[k - 1])
         if k > 1:

time: 243 us -> 242 us (level)
    all_to_all x2, waiting for transfers between devices: 12.4 us -> 9.48 us  [exchange(): lax.all_to_all(value, ('y', 'x'), 0, 0, tiled=True).reshape(values[0].shape)]
  transfers between devices with their start and end apart: 33 -> 33, of which waited for: 15 -> 15; matrix products, arithmetic and copies ran while one was open for 1% -> 0% of each run, Pallas kernels for 27% -> 27%
where the time goes in v7:
time: 242 us; the launch traced here: 241 us
  waiting for transfers between devices  93.1 us (38%)
  Pallas kernels  91.5 us (38%)
  starting transfers between devices  48.7 us (20%)
  local copies, waits for them, and re-layouts  6.87 us (3%)
    pallas_call x4, Pallas kernels, experts_apply(): pl.pallas_call(partial(experts_kernel, given=given, parts=parts, rows=row...  71.6 us
    ppermute x18, waiting for transfers between devices, exchange(): lax.ppermute(values[m], ('y', 'x'), pairs[m])  56.6 us
    ppermute x18, starting transfers between devices, exchange(): lax.ppermute(values[m], ('y', 'x'), pairs[m])  21.2 us
    ppermute x2, waiting for transfers between devices, flip(): return lax.ppermute(value, 'z', [(i, i ^ mask) for i in range(z_size)])  13.9 us
    ppermute x2, waiting for transfers between devices, outward(): return lax.ppermute(value, 'z', [(1, 0), (2, 3)])  13 us
    pallas_call x4, Pallas kernels, route(): pl.pallas_call(partial(route_kernel, choices=len(blocks), sends=sends, re...  11.6 us
    all_to_all x2, waiting for transfers between devices, exchange(): lax.all_to_all(value, ('y', 'x'), 0, 0, tiled=True).reshape(values[0].shape)  9.48 us
    all_to_all x2, starting transfers between devices, exchange(): lax.all_to_all(value, ('y', 'x'), 0, 0, tiled=True).reshape(values[0].shape)  8.94 us
  transfers between devices with their start and end apart: 33, of which 15 were waited for; matrix products, arithmetic and copies ran while one was open for 0% of the time, Pallas kernels for 27%

profile of v7, /device:TPU:0, one launch (start us, length us, event | category | flops | bytes accessed | tf_op | source)
XLA Modules:
  0.0 241.3 jit_solution(12174139367382126469)
XLA Ops:
  1.6 1.2 copy-done
  2.9 3.1 %collective-permute-start.2 = (bf16[128,4224]{1,0:T(8,128)(2,1)S(1)}, bf16[128,4224]{1,0:T(8,128)(2,1)S(1)}, u32[]{:S(2)}, u32[]{:S(2)}) collective-permute-start(bf16[128,4224]{1,0:T(8,128)(2,1)S(1)} %shard_map.64.refs_0_), channel_id=1, source_target_pairs={{0,2},{2,0},{4,6},{6,4},{1,3},{3,1},{5,7},{7,5},{8,10},{10,8},{12,... | collective-permute-start | bytes 3244040 | tf_op jit(solution)/shard_map/ppermute | solution.py:276
  6.8 3.4 %shard_map.65 = (bf16[256,4224]{1,0:T(8,128)(2,1)}, bf16[128,256]{1,0:T(8,128)(2,1)S(1)}, bf16[128,256]{1,0:T(8,128)(2,1)S(1)}) custom-call(s32[3]{0:T(128)S(1)} %pad_add_fusion.flag, bf16[128,4224]{1,0:T(8,128)(2,1)S(1)} %shard_map.64.refs_0_), custom_call_target="tpu_custom_call" | custom-call | flops 55364812800 | bytes 3244032 | tf_op jit(solution)/shard_map/pallas_call | solution.py:213
  10.2 4.4 %all-to-all-start = ((bf16[4,64,4224]{2,1,0:T(8,128)(2,1)}), bf16[4,64,4224]{2,1,0:T(8,128)(2,1)}, u32[]{:S(2)}, u32[]{:S(2)}) async-start(bf16[4,64,4224]{2,1,0:T(8,128)(2,1)} %bitcast.6), calls=%async_computation | async-start | bytes 4325376 | tf_op jit(solution)/shard_map/all_to_all | solution.py:298
  15.9 13.9 %collective-permute-done.2.refs_0_ = bf16[128,4224]{1,0:T(8,128)(2,1)S(1)} collective-permute-done((bf16[128,4224]{1,0:T(8,128)(2,1)S(1)}, bf16[128,4224]{1,0:T(8,128)(2,1)S(1)}, u32[]{:S(2)}, u32[]{:S(2)}) %collective-permute-start.2) | collective-permute-done | bytes 1081376 | tf_op jit(solution)/shard_map/ppermute | solution.py:276
  29.8 1.3 collective-permute-start.1
  31.1 1.7 collective-permute-start.3
  32.8 3.4 %shard_map.66 = (bf16[256,4224]{1,0:T(8,128)(2,1)}, bf16[128,256]{1,0:T(8,128)(2,1)S(1)}, bf16[128,256]{1,0:T(8,128)(2,1)S(1)}) custom-call(s32[3]{0:T(128)S(1)} %pad_add_fusion.flag, bf16[128,4224]{1,0:T(8,128)(2,1)S(1)} %collective-permute-done.2.refs_0_), custom_call_target="tpu_custom_call" | custom-call | flops 55364812800 | bytes 3244032 | tf_op jit(solution)/shard_map/pallas_call | solution.py:213
  36.2 4.1 %all-to-all-done = bf16[4,64,4224]{2,1,0:T(8,128)(2,1)} async-done(((bf16[4,64,4224]{2,1,0:T(8,128)(2,1)}), bf16[4,64,4224]{2,1,0:T(8,128)(2,1)}, u32[]{:S(2)}, u32[]{:S(2)}) %all-to-all-start) | async-done | bytes 2162720 | tf_op jit(solution)/shard_map/all_to_all | solution.py:298
  40.2 4.5 %all-to-all-start.1 = ((bf16[4,64,4224]{2,1,0:T(8,128)(2,1)}), bf16[4,64,4224]{2,1,0:T(8,128)(2,1)}, u32[]{:S(2)}, u32[]{:S(2)}) async-start(bf16[4,64,4224]{2,1,0:T(8,128)(2,1)} %bitcast.8), calls=%async_computation.1 | async-start | bytes 4325376 | tf_op jit(solution)/shard_map/all_to_all | solution.py:298
  44.8 1.3 collective-permute-start.10
  46.1 13.0 %collective-permute-done.1.refs_0_ = bf16[128,4224]{1,0:T(8,128)(2,1)} collective-permute-done((bf16[128,4224]{1,0:T(8,128)(2,1)S(1)}, bf16[128,4224]{1,0:T(8,128)(2,1)}, u32[]{:S(2)}, u32[]{:S(2)}) %collective-permute-start.1) | collective-permute-done | bytes 1081376 | tf_op jit(solution)/shard_map/ppermute | solution.py:282
  59.1 2.9 %shard_map.67 = (bf16[64,4224]{1,0:T(8,128)(2,1)S(1)}, bf16[64,4224]{1,0:T(8,128)(2,1)S(1)}, bf16[64,4224]{1,0:T(8,128)(2,1)S(1)}, bf16[64,4224]{1,0:T(8,128)(2,...) custom-call(s32[3]{0:T(128)S(1)} %pad_add_fusion.flag, ...), custom_call_target="tpu_custom_call" | custom-call | flops 55364812800 | bytes 3244032 | tf_op jit(solution)/shard_map/pallas_call | solution.py:213
  64.4 5.4 %all-to-all-done.1 = bf16[4,64,4224]{2,1,0:T(8,128)(2,1)} async-done(((bf16[4,64,4224]{2,1,0:T(8,128)(2,1)}), bf16[4,64,4224]{2,1,0:T(8,128)(2,1)}, u32[]{:S(2)}, u32[]{:S(2)}) %all-to-all-start.1) | async-done | bytes 2162720 | tf_op jit(solution)/shard_map/all_to_all | solution.py:298
  69.8 1.4 collective-permute-start.7
  71.8 1.5 collective-permute-start.9
  73.3 17.8 %shard_map.68 = (bf16[64,4096]{1,0:T(8,128)(2,1)}, bf16[64,4096]{1,0:T(8,128)(2,1)}, bf16[64,4096]{1,0:T(8,128)(2,1)}, bf16[64,4096]{1,0:T(8,128)(2,1)}) custom-call(s32[4]{0:T(128)} %pad_add_fusion.1.info, bf16[256,4224]{1,0:T(8,128)(2,1)} %bitcast.7.refs_0_, bf16[4096,768]{1,0:T(8,128)(2,1)} %bitcast.14, bf16[4096,768]{1,0:T(8,128)(2,1)} %bitcast.19, ...), custom_call_target="tpu_custom_call" | custom-call | flops 9663676416 | bytes 41943040 | tf_op jit(solution)/shard_map/pallas_call | solution.py:108
  91.1 1.9 shard_map.69
  93.9 1.2 collective-permute-done.8.refs_2_
  95.1 1.6 collective-permute-start.11
  97.2 1.4 collective-permute-start.13
  98.6 17.8 %shard_map.70 = (bf16[64,4096]{1,0:T(8,128)(2,1)}, bf16[64,4096]{1,0:T(8,128)(2,1)}, bf16[64,4096]{1,0:T(8,128)(2,1)}, bf16[64,4096]{1,0:T(8,128)(2,1)}) custom-call(s32[4]{0:T(128)} %pad_add_fusion.1.info, bf16[256,4224]{1,0:T(8,128)(2,1)} %bitcast.9.refs_0_, bf16[4096,768]{1,0:T(8,128)(2,1)} %bitcast.15, bf16[4096,768]{1,0:T(8,128)(2,1)} %bitcast.20, ...), custom_call_target="tpu_custom_call" | custom-call | flops 9663676416 | bytes 41943040 | tf_op jit(solution)/shard_map/pallas_call | solution.py:108
  116.5 1.2 collective-permute-done.12.refs_2_
  117.7 1.9 collective-permute-done.13.refs_3_
  120.4 18.0 %shard_map.71 = (bf16[64,4096]{1,0:T(8,128)(2,1)}, bf16[64,4096]{1,0:T(8,128)(2,1)}, bf16[64,4096]{1,0:T(8,128)(2,1)}, bf16[64,4096]{1,0:T(8,128)(2,1)}) custom-call(s32[4]{0:T(128)} %pad_add_fusion.1.info, bf16[64,4224]{1,0:T(8,128)(2,1)} %copy-done.2, bf16[64,4224]{1,0:T(8,128)(2,1)} %copy-done.12, bf16[64,4224]{1,0:T(8,128)(2,1)} %copy-done.13, ...), custom_call_target="tpu_custom_call" | custom-call | flops 9663676416 | bytes 41943040 | tf_op jit(solution)/shard_map/pallas_call | solution.py:108
  139.3 1.7 collective-permute-start.18
  142.0 18.0 %shard_map.72 = (bf16[64,4096]{1,0:T(8,128)(2,1)}, bf16[64,4096]{1,0:T(8,128)(2,1)}, bf16[64,4096]{1,0:T(8,128)(2,1)}, bf16[64,4096]{1,0:T(8,128)(2,1)}) custom-call(s32[4]{0:T(128)} %pad_add_fusion.1.info, bf16[64,4224]{1,0:T(8,128)(2,1)} %copy-done.1, bf16[64,4224]{1,0:T(8,128)(2,1)} %copy-done.9, bf16[64,4224]{1,0:T(8,128)(2,1)} %copy-done.10, ...), custom_call_target="tpu_custom_call" | custom-call | flops 9663676416 | bytes 41943040 | tf_op jit(solution)/shard_map/pallas_call | solution.py:108
  160.0 1.0 collective-permute-done.18.refs_2_
  161.0 1.7 shard_map.73
  162.7 6.1 %collective-permute-start.20 = (bf16[128,4096]{1,0:T(8,128)(2,1)S(1)}, bf16[128,4096]{1,0:T(8,128)(2,1)S(1)}, u32[]{:S(2)}, u32[]{:S(2)}) collective-permute-start(bf16[128,4096]{1,0:T(8,128)(2,1)S(1)} %get-tuple-element.147), channel_id=1, source_target_pairs={{0,2},{6,4},{1,3},{7,5},{8,10},{14,12},{9,11},{15,13},{16,18},{22,... | collective-permute-start | bytes 3145736 | tf_op jit(solution)/shard_map/ppermute | solution.py:285
  168.9 1.7 collective-permute-start.14
  170.9 1.5 collective-permute-start.16
  172.4 11.0 %collective-permute-done.14.refs_1_ = bf16[64,4096]{1,0:T(8,128)(2,1)S(1)} collective-permute-done((bf16[64,4096]{1,0:T(8,128)(2,1)S(1)}, bf16[64,4096]{1,0:T(8,128)(2,1)S(1)}, u32[]{:S(2)}, u32[]{:S(2)}) %collective-permute-start.14) | collective-permute-done | bytes 524320 | tf_op jit(solution)/shard_map/ppermute | solution.py:300
  183.5 7.6 %collective-permute-done.15.refs_2_ = bf16[64,4096]{1,0:T(8,128)(2,1)S(1)} collective-permute-done((bf16[64,4096]{1,0:T(8,128)(2,1)S(1)}, bf16[64,4096]{1,0:T(8,128)(2,1)S(1)}, u32[]{:S(2)}, u32[]{:S(2)}) %collective-permute-start.15) | collective-permute-done | bytes 524320 | tf_op jit(solution)/shard_map/ppermute | solution.py:300
  191.1 1.7 shard_map.74
  192.8 1.4 collective-permute-start.28
  195.5 1.7 collective-permute-start.25
  197.2 1.2 collective-permute-start.26
  198.4 10.9 %collective-permute-done.24.refs_1_ = bf16[64,4096]{1,0:T(8,128)(2,1)S(1)} collective-permute-done((bf16[64,4096]{1,0:T(8,128)(2,1)S(1)}, bf16[64,4096]{1,0:T(8,128)(2,1)S(1)}, u32[]{:S(2)}, u32[]{:S(2)}) %collective-permute-start.24) | collective-permute-done | bytes 524320 | tf_op jit(solution)/shard_map/ppermute | solution.py:300
  209.4 5.0 %collective-permute-done.25.refs_2_ = bf16[64,4096]{1,0:T(8,128)(2,1)S(1)} collective-permute-done((bf16[64,4096]{1,0:T(8,128)(2,1)S(1)}, bf16[64,4096]{1,0:T(8,128)(2,1)S(1)}, u32[]{:S(2)}, u32[]{:S(2)}) %collective-permute-start.25) | collective-permute-done | bytes 524320 | tf_op jit(solution)/shard_map/ppermute | solution.py:300
  214.4 1.1 collective-permute-done.26.refs_3_
  215.6 2.2 shard_map.75
  219.4 1.3 collective-permute-start.21
  220.7 1.1 collective-permute-start.22
  221.8 1.2 collective-permute-start.23
  222.9 9.5 %collective-permute-done.21.refs_1_ = bf16[64,4096]{1,0:T(8,128)(2,1)S(1)} collective-permute-done((bf16[64,4096]{1,0:T(8,128)(2,1)S(1)}, bf16[64,4096]{1,0:T(8,128)(2,1)S(1)}, u32[]{:S(2)}, u32[]{:S(2)}) %collective-permute-start.21) | collective-permute-done | bytes 524320 | tf_op jit(solution)/shard_map/ppermute | solution.py:300
  232.4 6.2 %collective-permute-done.22.refs_2_ = bf16[64,4096]{1,0:T(8,128)(2,1)S(1)} collective-permute-done((bf16[64,4096]{1,0:T(8,128)(2,1)S(1)}, bf16[64,4096]{1,0:T(8,128)(2,1)S(1)}, u32[]{:S(2)}, u32[]{:S(2)}) %collective-permute-start.22) | collective-permute-done | bytes 524320 | tf_op jit(solution)/shard_map/ppermute | solution.py:300
  238.7 2.6 %shard_map.76 = bf16[128,4096]{1,0:T(8,128)(2,1)} custom-call(bf16[128,256]{1,0:T(8,128)(2,1)S(1)} %get-tuple-element.88.hi, bf16[128,256]{1,0:T(8,128)(2,1)S(1)} %get-tuple-element.89.mid, bf16[64,4096]{1,0:T(8,128)(2,1)S(1)} %copy-done.6, bf16[64,4096]{1,0:T(8,128)(2,1)S(1)} %collective-permute-done.21.refs_1_, ...), custom_call_target="tpu_custom_call" | custom-call | flops 536870912 | bytes 3145728 | tf_op jit(solution)/shard_map/pallas_call | solution.py:244
  (83 shorter events, 14.1 us)
Async XLA Ops:
  2.9 26.9 %collective-permute-start.2 = (bf16[128,4224]{1,0:T(8,128)(2,1)S(1)}, bf16[128,4224]{1,0:T(8,128)(2,1)S(1)}, u32[]{:S(2)}, u32[]{:S(2)}) collective-permute-start(bf16[128,4224]{1,0:T(8,128)(2,1)S(1)} %shard_map.64.refs_0_), channel_id=1, source_target_pairs={{0,2},{2,0},{4,6},{6,4},{1,3},{3,1},{5,7},{7,5},{8,10},{10,8},{12,... | collective-permute-start | bytes 3244040 | tf_op jit(solution)/shard_map/ppermute | solution.py:276
  6.0 23.9 %collective-permute-start = (bf16[128,4224]{1,0:T(8,128)(2,1)S(1)}, bf16[128,4224]{1,0:T(8,128)(2,1)S(1)}, u32[]{:S(2)}, u32[]{:S(2)}) collective-permute-start(bf16[128,4224]{1,0:T(8,128)(2,1)S(1)} %shard_map.64.refs_0_), channel_id=1, source_target_pairs={{2,4},{4,2},{3,5},{5,3},{10,12},{12,10},{11,13},{13,11},{18,20},{2... | collective-permute-start | bytes 3244040 | tf_op jit(solution)/shard_map/ppermute | solution.py:279
  10.2 30.1 %all-to-all-start = ((bf16[4,64,4224]{2,1,0:T(8,128)(2,1)}), bf16[4,64,4224]{2,1,0:T(8,128)(2,1)}, u32[]{:S(2)}, u32[]{:S(2)}) async-start(bf16[4,64,4224]{2,1,0:T(8,128)(2,1)} %bitcast.6), calls=%async_computation | async-start | bytes 4325376 | tf_op jit(solution)/shard_map/all_to_all | solution.py:298
  14.6 56.6 %collective-permute-start.4 = (bf16[4096,768]{1,0:T(8,128)(2,1)}, bf16[4096,768]{1,0:T(8,128)(2,1)}, u32[]{:S(2)}, u32[]{:S(2)}) collective-permute-start(bf16[4096,768]{1,0:T(8,128)(2,1)} %bitcast.13), channel_id=1, source_target_pairs={{0,8},{8,0},{1,9},{9,1},{2,10},{10,2},{3,11},{11,3},{4,12},{12,4},... | collective-permute-start | bytes 18874376 | tf_op jit(solution)/shard_map/ppermute | solution.py:293
  14.7 57.1 %collective-permute-start.5 = (bf16[4096,768]{1,0:T(8,128)(2,1)}, bf16[4096,768]{1,0:T(8,128)(2,1)}, u32[]{:S(2)}, u32[]{:S(2)}) collective-permute-start(bf16[4096,768]{1,0:T(8,128)(2,1)} %bitcast.18), channel_id=1, source_target_pairs={{0,8},{8,0},{1,9},{9,1},{2,10},{10,2},{3,11},{11,3},{4,12},{12,4},... | collective-permute-start | bytes 18874376 | tf_op jit(solution)/shard_map/ppermute | solution.py:293
  15.2 58.1 %collective-permute-start.6 = (bf16[768,4096]{1,0:T(8,128)(2,1)}, bf16[768,4096]{1,0:T(8,128)(2,1)}, u32[]{:S(2)}, u32[]{:S(2)}) collective-permute-start(bf16[768,4096]{1,0:T(8,128)(2,1)} %bitcast.23), channel_id=1, source_target_pairs={{0,8},{8,0},{1,9},{9,1},{2,10},{10,2},{3,11},{11,3},{4,12},{12,4},... | collective-permute-start | bytes 18874376 | tf_op jit(solution)/shard_map/ppermute | solution.py:293
  29.8 29.2 %collective-permute-start.1 = (bf16[128,4224]{1,0:T(8,128)(2,1)S(1)}, bf16[128,4224]{1,0:T(8,128)(2,1)}, u32[]{:S(2)}, u32[]{:S(2)}) collective-permute-start(bf16[128,4224]{1,0:T(8,128)(2,1)S(1)} %collective-permute-done.refs_1_), channel_id=1, source_target_pairs={{2,0},{4,6},{3,1},{5,7},{10,8},{12,14},{11,9},{13,15},{18,16},{20,... | collective-permute-start | bytes 3244040 | tf_op jit(solution)/shard_map/ppermute | solution.py:282
  31.1 13.6 %collective-permute-start.3 = (bf16[128,4224]{1,0:T(8,128)(2,1)S(1)}, bf16[128,4224]{1,0:T(8,128)(2,1)}, u32[]{:S(2)}, u32[]{:S(2)}) collective-permute-start(bf16[128,4224]{1,0:T(8,128)(2,1)S(1)} %collective-permute-done.2.refs_0_), channel_id=1, source_target_pairs={{2,4},{4,2},{3,5},{5,3},{10,12},{12,10},{11,13},{13,11},{18,20},{2... | collective-permute-start | bytes 3244040 | tf_op jit(solution)/shard_map/ppermute | solution.py:279
  40.2 29.6 %all-to-all-start.1 = ((bf16[4,64,4224]{2,1,0:T(8,128)(2,1)}), bf16[4,64,4224]{2,1,0:T(8,128)(2,1)}, u32[]{:S(2)}, u32[]{:S(2)}) async-start(bf16[4,64,4224]{2,1,0:T(8,128)(2,1)} %bitcast.8), calls=%async_computation.1 | async-start | bytes 4325376 | tf_op jit(solution)/shard_map/all_to_all | solution.py:298
  44.8 46.4 %collective-permute-start.10 = (bf16[128,4224]{1,0:T(8,128)(2,1)}, bf16[128,4224]{1,0:T(8,128)(2,1)S(1)}, u32[]{:S(2)}, u32[]{:S(2)}) collective-permute-start(bf16[128,4224]{1,0:T(8,128)(2,1)} %collective-permute-done.3.refs_1_), channel_id=1, source_target_pairs={{2,0},{4,6},{3,1},{5,7},{10,8},{12,14},{11,9},{13,15},{18,16},{20,... | collective-permute-start | bytes 3244040 | tf_op jit(solution)/shard_map/ppermute | solution.py:282
  69.8 24.1 %collective-permute-start.7 = (bf16[64,4224]{1,0:T(8,128)(2,1)}, bf16[64,4224]{1,0:T(8,128)(2,1)S(1)}, u32[]{:S(2)}, u32[]{:S(2)}) collective-permute-start(bf16[64,4224]{1,0:T(8,128)(2,1)} %copy-done.8), channel_id=1, source_target_pairs={{0,1},{1,0},{16,17},{17,16},{2,3},{3,2},{18,19},{19,18},{4,5},{5,4... | collective-permute-start | bytes 1622024 | tf_op jit(solution)/shard_map/ppermute | solution.py:300
  71.3 23.8 %collective-permute-start.8 = (bf16[64,4224]{1,0:T(8,128)(2,1)}, bf16[64,4224]{1,0:T(8,128)(2,1)S(1)}, u32[]{:S(2)}, u32[]{:S(2)}) collective-permute-start(bf16[64,4224]{1,0:T(8,128)(2,1)} %copy-done.7), channel_id=1, source_target_pairs={{0,16},{1,17},{16,0},{17,1},{2,18},{3,19},{18,2},{19,3},{4,20},{5,... | collective-permute-start | bytes 1622024 | tf_op jit(solution)/shard_map/ppermute | solution.py:300
  71.8 23.2 %collective-permute-start.9 = (bf16[64,4224]{1,0:T(8,128)(2,1)S(1)}, bf16[64,4224]{1,0:T(8,128)(2,1)S(1)}, u32[]{:S(2)}, u32[]{:S(2)}) collective-permute-start(bf16[64,4224]{1,0:T(8,128)(2,1)S(1)} %get-tuple-element.103), channel_id=1, source_target_pairs={{0,17},{1,16},{16,1},{17,0},{2,19},{3,18},{18,3},{19,2},{4,21},{5,... | collective-permute-start | bytes 1622024 | tf_op jit(solution)/shard_map/ppermute | solution.py:300
  93.9 22.5 %copy-start.9 = (bf16[64,4224]{1,0:T(8,128)(2,1)}, bf16[64,4224]{1,0:T(8,128)(2,1)S(1)}, u32[]{:S(2)}) copy-start(bf16[64,4224]{1,0:T(8,128)(2,1)S(1)} %collective-permute-done.7.refs_1_) | copy-start | bytes 1622020
  95.1 21.4 %copy-start.10 = (bf16[64,4224]{1,0:T(8,128)(2,1)}, bf16[64,4224]{1,0:T(8,128)(2,1)S(1)}, u32[]{:S(2)}) copy-start(bf16[64,4224]{1,0:T(8,128)(2,1)S(1)} %collective-permute-done.8.refs_2_) | copy-start | bytes 1622020
  95.1 21.4 %copy-start.11 = (bf16[64,4224]{1,0:T(8,128)(2,1)}, bf16[64,4224]{1,0:T(8,128)(2,1)S(1)}, u32[]{:S(2)}) copy-start(bf16[64,4224]{1,0:T(8,128)(2,1)S(1)} %collective-permute-done.9.refs_3_) | copy-start | bytes 1622020
  95.1 21.4 %collective-permute-start.11 = (bf16[64,4224]{1,0:T(8,128)(2,1)S(1)}, bf16[64,4224]{1,0:T(8,128)(2,1)S(1)}, u32[]{:S(2)}, u32[]{:S(2)}) collective-permute-start(bf16[64,4224]{1,0:T(8,128)(2,1)S(1)} %get-tuple-element.117), channel_id=1, source_target_pairs={{0,1},{1,0},{16,17},{17,16},{2,3},{3,2},{18,19},{19,18},{4,5},{5,4... | collective-permute-start | bytes 1622024 | tf_op jit(solution)/shard_map/ppermute | solution.py:300
  96.6 21.0 %collective-permute-start.12 = (bf16[64,4224]{1,0:T(8,128)(2,1)S(1)}, bf16[64,4224]{1,0:T(8,128)(2,1)S(1)}, u32[]{:S(2)}, u32[]{:S(2)}) collective-permute-start(bf16[64,4224]{1,0:T(8,128)(2,1)S(1)} %get-tuple-element.118), channel_id=1, source_target_pairs={{0,16},{1,17},{16,0},{17,1},{2,18},{3,19},{18,2},{19,3},{4,20},{5,... | collective-permute-start | bytes 1622024 | tf_op jit(solution)/shard_map/ppermute | solution.py:300
  97.2 22.3 %collective-permute-start.13 = (bf16[64,4224]{1,0:T(8,128)(2,1)S(1)}, bf16[64,4224]{1,0:T(8,128)(2,1)S(1)}, u32[]{:S(2)}, u32[]{:S(2)}) collective-permute-start(bf16[64,4224]{1,0:T(8,128)(2,1)S(1)} %get-tuple-element.119), channel_id=1, source_target_pairs={{0,17},{1,16},{16,1},{17,0},{2,19},{3,18},{18,3},{19,2},{4,21},{5,... | collective-permute-start | bytes 1622024 | tf_op jit(solution)/shard_map/ppermute | solution.py:300
  138.4 21.6 %collective-permute-start.17 = (bf16[64,4096]{1,0:T(8,128)(2,1)}, bf16[64,4096]{1,0:T(8,128)(2,1)S(1)}, u32[]{:S(2)}, u32[]{:S(2)}) collective-permute-start(bf16[64,4096]{1,0:T(8,128)(2,1)} %get-tuple-element.130), channel_id=1, source_target_pairs={{0,1},{1,0},{16,17},{17,16},{2,3},{3,2},{18,19},{19,18},{4,5},{5,4... | collective-permute-start | bytes 1572872 | tf_op jit(solution)/shard_map/ppermute | solution.py:300
  139.3 21.7 %collective-permute-start.18 = (bf16[64,4096]{1,0:T(8,128)(2,1)}, bf16[64,4096]{1,0:T(8,128)(2,1)S(1)}, u32[]{:S(2)}, u32[]{:S(2)}) collective-permute-start(bf16[64,4096]{1,0:T(8,128)(2,1)} %get-tuple-element.131), channel_id=1, source_target_pairs={{0,16},{1,17},{16,0},{17,1},{2,18},{3,19},{18,2},{19,3},{4,20},{5,... | collective-permute-start | bytes 1572872 | tf_op jit(solution)/shard_map/ppermute | solution.py:300
  141.0 20.0 %collective-permute-start.19 = (bf16[64,4096]{1,0:T(8,128)(2,1)}, bf16[64,4096]{1,0:T(8,128)(2,1)S(1)}, u32[]{:S(2)}, u32[]{:S(2)}) collective-permute-start(bf16[64,4096]{1,0:T(8,128)(2,1)} %get-tuple-element.132), channel_id=1, source_target_pairs={{0,17},{1,16},{16,1},{17,0},{2,19},{3,18},{18,3},{19,2},{4,21},{5,... | collective-permute-start | bytes 1572872 | tf_op jit(solution)/shard_map/ppermute | solution.py:300
  142.0 19.0 %copy-start.5 = (bf16[64,4096]{1,0:T(8,128)(2,1)S(1)}, bf16[64,4096]{1,0:T(8,128)(2,1)}, u32[]{:S(2)}) copy-start(bf16[64,4096]{1,0:T(8,128)(2,1)} %get-tuple-element.143.refs_0_) | copy-start | bytes 1572868
  160.0 8.9 %copy-start.23 = (bf16[64,4096]{1,0:T(8,128)(2,1)S(1)}, bf16[64,4096]{1,0:T(8,128)(2,1)}, u32[]{:S(2)}) copy-start(bf16[64,4096]{1,0:T(8,128)(2,1)} %get-tuple-element.138) | copy-start | bytes 1572868
  160.0 10.7 %copy-start.22 = (bf16[64,4096]{1,0:T(8,128)(2,1)S(1)}, bf16[64,4096]{1,0:T(8,128)(2,1)}, u32[]{:S(2)}) copy-start(bf16[64,4096]{1,0:T(8,128)(2,1)} %get-tuple-element.139) | copy-start | bytes 1572868
  160.0 10.9 %copy-start.21 = (bf16[64,4096]{1,0:T(8,128)(2,1)S(1)}, bf16[64,4096]{1,0:T(8,128)(2,1)}, u32[]{:S(2)}) copy-start(bf16[64,4096]{1,0:T(8,128)(2,1)} %get-tuple-element.140) | copy-start | bytes 1572868
  160.0 31.1 %copy-start.4 = (bf16[64,4096]{1,0:T(8,128)(2,1)S(1)}, bf16[64,4096]{1,0:T(8,128)(2,1)}, u32[]{:S(2)}) copy-start(bf16[64,4096]{1,0:T(8,128)(2,1)} %get-tuple-element.152.refs_0_) | copy-start | bytes 1572868
  162.7 32.2 %copy-start.20 = (bf16[64,4096]{1,0:T(8,128)(2,1)S(1)}, bf16[64,4096]{1,0:T(8,128)(2,1)}, u32[]{:S(2)}) copy-start(bf16[64,4096]{1,0:T(8,128)(2,1)} %get-tuple-element.149) | copy-start | bytes 1572868
  162.7 32.8 %copy-start.19 = (bf16[64,4096]{1,0:T(8,128)(2,1)S(1)}, bf16[64,4096]{1,0:T(8,128)(2,1)}, u32[]{:S(2)}) copy-start(bf16[64,4096]{1,0:T(8,128)(2,1)} %get-tuple-element.150) | copy-start | bytes 1572868
  162.7 34.5 %copy-start.18 = (bf16[64,4096]{1,0:T(8,128)(2,1)S(1)}, bf16[64,4096]{1,0:T(8,128)(2,1)}, u32[]{:S(2)}) copy-start(bf16[64,4096]{1,0:T(8,128)(2,1)} %get-tuple-element.151) | copy-start | bytes 1572868
  162.7 52.8 %copy-start.3 = (bf16[64,4096]{1,0:T(8,128)(2,1)S(1)}, bf16[64,4096]{1,0:T(8,128)(2,1)}, u32[]{:S(2)}) copy-start(bf16[64,4096]{1,0:T(8,128)(2,1)} %get-tuple-element.164.refs_0_) | copy-start | bytes 1572868
  162.7 28.3 %collective-permute-start.20 = (bf16[128,4096]{1,0:T(8,128)(2,1)S(1)}, bf16[128,4096]{1,0:T(8,128)(2,1)S(1)}, u32[]{:S(2)}, u32[]{:S(2)}) collective-permute-start(bf16[128,4096]{1,0:T(8,128)(2,1)S(1)} %get-tuple-element.147), channel_id=1, source_target_pairs={{0,2},{6,4},{1,3},{7,5},{8,10},{14,12},{9,11},{15,13},{16,18},{22,... | collective-permute-start | bytes 3145736 | tf_op jit(solution)/shard_map/ppermute | solution.py:285
  168.9 14.6 %collective-permute-start.14 = (bf16[64,4096]{1,0:T(8,128)(2,1)S(1)}, bf16[64,4096]{1,0:T(8,128)(2,1)S(1)}, u32[]{:S(2)}, u32[]{:S(2)}) collective-permute-start(bf16[64,4096]{1,0:T(8,128)(2,1)S(1)} %copy-done.23), channel_id=1, source_target_pairs={{0,1},{1,0},{16,17},{17,16},{2,3},{3,2},{18,19},{19,18},{4,5},{5,4... | collective-permute-start | bytes 1572872 | tf_op jit(solution)/shard_map/ppermute | solution.py:300
  170.6 20.4 %collective-permute-start.15 = (bf16[64,4096]{1,0:T(8,128)(2,1)S(1)}, bf16[64,4096]{1,0:T(8,128)(2,1)S(1)}, u32[]{:S(2)}, u32[]{:S(2)}) collective-permute-start(bf16[64,4096]{1,0:T(8,128)(2,1)S(1)} %copy-done.22), channel_id=1, source_target_pairs={{0,16},{1,17},{16,0},{17,1},{2,18},{3,19},{18,2},{19,3},{4,20},{5,... | collective-permute-start | bytes 1572872 | tf_op jit(solution)/shard_map/ppermute | solution.py:300
  170.9 20.1 %collective-permute-start.16 = (bf16[64,4096]{1,0:T(8,128)(2,1)S(1)}, bf16[64,4096]{1,0:T(8,128)(2,1)S(1)}, u32[]{:S(2)}, u32[]{:S(2)}) collective-permute-start(bf16[64,4096]{1,0:T(8,128)(2,1)S(1)} %copy-done.21), channel_id=1, source_target_pairs={{0,17},{1,16},{16,1},{17,0},{2,19},{3,18},{18,3},{19,2},{4,21},{5,... | collective-permute-start | bytes 1572872 | tf_op jit(solution)/shard_map/ppermute | solution.py:300
  192.8 22.7 %collective-permute-start.28 = (bf16[128,4096]{1,0:T(8,128)(2,1)S(1)}, bf16[128,4096]{1,0:T(8,128)(2,1)S(1)}, u32[]{:S(2)}, u32[]{:S(2)}) collective-permute-start(bf16[128,4096]{1,0:T(8,128)(2,1)S(1)} %get-tuple-element.156), channel_id=1, source_target_pairs={{0,2},{6,4},{1,3},{7,5},{8,10},{14,12},{9,11},{15,13},{16,18},{22,... | collective-permute-start | bytes 3145736 | tf_op jit(solution)/shard_map/ppermute | solution.py:285
  194.1 21.4 %collective-permute-start.27 = (bf16[128,4096]{1,0:T(8,128)(2,1)S(1)}, bf16[128,4096]{1,0:T(8,128)(2,1)S(1)}, u32[]{:S(2)}, u32[]{:S(2)}) collective-permute-start(bf16[128,4096]{1,0:T(8,128)(2,1)S(1)} %get-tuple-element.157), channel_id=1, source_target_pairs={{2,4},{4,2},{3,5},{5,3},{10,12},{12,10},{11,13},{13,11},{18,20},{2... | collective-permute-start | bytes 3145736 | tf_op jit(solution)/shard_map/ppermute | solution.py:279
  194.9 14.5 %collective-permute-start.24 = (bf16[64,4096]{1,0:T(8,128)(2,1)S(1)}, bf16[64,4096]{1,0:T(8,128)(2,1)S(1)}, u32[]{:S(2)}, u32[]{:S(2)}) collective-permute-start(bf16[64,4096]{1,0:T(8,128)(2,1)S(1)} %copy-done.20), channel_id=1, source_target_pairs={{0,1},{1,0},{16,17},{17,16},{2,3},{3,2},{18,19},{19,18},{4,5},{5,4... | collective-permute-start | bytes 1572872 | tf_op jit(solution)/shard_map/ppermute | solution.py:300
  195.5 18.9 %collective-permute-start.25 = (bf16[64,4096]{1,0:T(8,128)(2,1)S(1)}, bf16[64,4096]{1,0:T(8,128)(2,1)S(1)}, u32[]{:S(2)}, u32[]{:S(2)}) collective-permute-start(bf16[64,4096]{1,0:T(8,128)(2,1)S(1)} %copy-done.19), channel_id=1, source_target_pairs={{0,16},{1,17},{16,0},{17,1},{2,18},{3,19},{18,2},{19,3},{4,20},{5,... | collective-permute-start | bytes 1572872 | tf_op jit(solution)/shard_map/ppermute | solution.py:300
  197.2 18.3 %collective-permute-start.26 = (bf16[64,4096]{1,0:T(8,128)(2,1)S(1)}, bf16[64,4096]{1,0:T(8,128)(2,1)S(1)}, u32[]{:S(2)}, u32[]{:S(2)}) collective-permute-start(bf16[64,4096]{1,0:T(8,128)(2,1)S(1)} %copy-done.18), channel_id=1, source_target_pairs={{0,17},{1,16},{16,1},{17,0},{2,19},{3,18},{18,3},{19,2},{4,21},{5,... | collective-permute-start | bytes 1572872 | tf_op jit(solution)/shard_map/ppermute | solution.py:300
  215.5 5.2 %copy-start.16 = (bf16[64,4096]{1,0:T(8,128)(2,1)S(1)}, bf16[64,4096]{1,0:T(8,128)(2,1)}, u32[]{:S(2)}) copy-start(bf16[64,4096]{1,0:T(8,128)(2,1)} %get-tuple-element.160) | copy-start | bytes 1572868
  215.5 6.2 %copy-start.15 = (bf16[64,4096]{1,0:T(8,128)(2,1)S(1)}, bf16[64,4096]{1,0:T(8,128)(2,1)}, u32[]{:S(2)}) copy-start(bf16[64,4096]{1,0:T(8,128)(2,1)} %get-tuple-element.161) | copy-start | bytes 1572868
  215.5 23.1 %copy-start.6 = (bf16[64,4096]{1,0:T(8,128)(2,1)S(1)}, bf16[64,4096]{1,0:T(8,128)(2,1)}, u32[]{:S(2)}) copy-start(bf16[64,4096]{1,0:T(8,128)(2,1)} %get-tuple-element.158.refs_0_) | copy-start | bytes 1572868
  217.8 20.9 %collective-permute-start.29 = (bf16[128,4096]{1,0:T(8,128)(2,1)S(1)}, bf16[128,4096]{1,0:T(8,128)(2,1)S(1)}, u32[]{:S(2)}, u32[]{:S(2)}) collective-permute-start(bf16[128,4096]{1,0:T(8,128)(2,1)S(1)} %get-tuple-element.169), channel_id=1, source_target_pairs={{0,2},{2,0},{4,6},{6,4},{1,3},{3,1},{5,7},{7,5},{8,10},{10,8},{12,... | collective-permute-start | bytes 3145736 | tf_op jit(solution)/shard_map/ppermute | solution.py:276
  218.7 20.0 %collective-permute-start.30 = (bf16[128,4096]{1,0:T(8,128)(2,1)S(1)}, bf16[128,4096]{1,0:T(8,128)(2,1)S(1)}, u32[]{:S(2)}, u32[]{:S(2)}) collective-permute-start(bf16[128,4096]{1,0:T(8,128)(2,1)S(1)} %get-tuple-element.170), channel_id=1, source_target_pairs={{2,4},{4,2},{3,5},{5,3},{10,12},{12,10},{11,13},{13,11},{18,20},{2... | collective-permute-start | bytes 3145736 | tf_op jit(solution)/shard_map/ppermute | solution.py:279
  219.4 13.0 %collective-permute-start.21 = (bf16[64,4096]{1,0:T(8,128)(2,1)S(1)}, bf16[64,4096]{1,0:T(8,128)(2,1)S(1)}, u32[]{:S(2)}, u32[]{:S(2)}) collective-permute-start(bf16[64,4096]{1,0:T(8,128)(2,1)S(1)} %copy-done.17), channel_id=1, source_target_pairs={{0,1},{1,0},{16,17},{17,16},{2,3},{3,2},{18,19},{19,18},{4,5},{5,4... | collective-permute-start | bytes 1572872 | tf_op jit(solution)/shard_map/ppermute | solution.py:300
  220.7 18.0 %collective-permute-start.22 = (bf16[64,4096]{1,0:T(8,128)(2,1)S(1)}, bf16[64,4096]{1,0:T(8,128)(2,1)S(1)}, u32[]{:S(2)}, u32[]{:S(2)}) collective-permute-start(bf16[64,4096]{1,0:T(8,128)(2,1)S(1)} %copy-done.16), channel_id=1, source_target_pairs={{0,16},{1,17},{16,0},{17,1},{2,18},{3,19},{18,2},{19,3},{4,20},{5,... | collective-permute-start | bytes 1572872 | tf_op jit(solution)/shard_map/ppermute | solution.py:300
  221.8 16.9 %collective-permute-start.23 = (bf16[64,4096]{1,0:T(8,128)(2,1)S(1)}, bf16[64,4096]{1,0:T(8,128)(2,1)S(1)}, u32[]{:S(2)}, u32[]{:S(2)}) collective-permute-start(bf16[64,4096]{1,0:T(8,128)(2,1)S(1)} %copy-done.15), channel_id=1, source_target_pairs={{0,17},{1,16},{16,1},{17,0},{2,19},{3,18},{18,3},{19,2},{4,21},{5,... | collective-permute-start | bytes 1572872 | tf_op jit(solution)/shard_map/ppermute | solution.py:300
  (9 other events, 14.1 us)
